TPU v7x, 512 devices: a whole 4x8x8 slice. The times are simulated.
512 devices in a mesh: row: 16 (over z, core), col: 32 (over x, y).
Axes of the slice: x: 4, y: 8, z: 8, core: 2. Of those that a mesh axis runs over, the one named last changes fastest.
Arguments:
- trail_adj: float32 [16384, 16384], P('row', 'col'), may hold values from -34 to 34
- factor_panels: float32 [16384, 384], P('row', 'col'), may hold values from -4 to 4, as said below
- factor_adj: float32 [16384, 384], P('row', 'col'), may hold values from -6 to 6
Outputs:
- panel_adj: float32 [16384, 384], P('row', 'col')
Inputs may be any that keep to these rules, and one draw needn't show every extreme that they name: `factor_panels`: in column block k of 128 columns, rows above k * 128 are zero and rows k * 128 to k * 128 + 127 form a lower-triangular block with diagonal entries 1.5 to 4.
All inputs are finite; a program needn't handle non-finite values.
Results may differ from a plain program's by a relative error of at most 0.00011.
Values sent between devices are 32-bit elements; how exact they have to be, the bound alone decides.
No kernel may reach another device: no remote copies, remote signals or barrier semaphores. Data moves between devices by JAX's collectives and lax.ppermute only.
A program may use at most 64 MiB of HBM per device.

v0:
```python
import jax
import jax.numpy as jnp
from jax import lax
from jax.sharding import PartitionSpec as P

B = 128
STEPS = 3


def broadcast(value, axis, root):
    mine = lax.axis_index(axis) == root
    return lax.psum(jnp.where(mine, value, jnp.zeros_like(value)), axis)


def mdot(operand, other):
    return jnp.dot(
        operand, other, precision=lax.Precision.HIGHEST, preferred_element_type=jnp.float32
    )


def place_rows(block_rows, global_rows, first_row, block_height):
    offsets = global_rows - first_row
    inside = (offsets >= 0) & (offsets < block_height)
    taken = jnp.take(block_rows, jnp.clip(offsets, 0, block_height - 1), axis=0)
    return jnp.where(inside[:, None], taken, jnp.zeros_like(taken))


def diag_adjoint(lower_block, lower_inverse, block_total):
    product = mdot(lower_block.T, block_total)
    halved = jnp.tril(product) - 0.5 * jnp.diag(jnp.diag(product))
    sandwich = mdot(mdot(lower_inverse.T, halved), lower_inverse)
    return 0.5 * (sandwich + sandwich.T)


def on_device(trail_adj, factor_panels, factor_adj):
    row_count = factor_panels.shape[0]
    col_width = trail_adj.shape[1]
    row_devices = lax.axis_size("row")
    col_devices = lax.axis_size("col")
    row_index = lax.axis_index("row")
    col_index = lax.axis_index("col")
    panel_width = STEPS * B
    global_rows = row_index * row_count + jnp.arange(row_count, dtype=jnp.int32)
    col_rows = col_index * col_width + jnp.arange(col_width, dtype=jnp.int32)
    corner_ids = jnp.arange(panel_width, dtype=jnp.int32)
    full_factor, full_adj = (
        lax.all_gather(factor_panels, "col", axis=1, tiled=True),
        lax.all_gather(factor_adj, "col", axis=1, tiled=True),
    )
    corner_factor, corner_adj = (
        broadcast(full_factor[:panel_width], "row", 0),
        broadcast(full_adj[:panel_width], "row", 0),
    )
    per_row = col_devices // row_devices
    offset = col_index % per_row * col_width
    root_row = col_index // per_row
    identity = jnp.eye(B, dtype=jnp.float32)
    accum = jnp.zeros((row_count, panel_width), jnp.float32)
    for panel_step in reversed(range(STEPS)):
        col_start = panel_step * B
        remote = broadcast(
            lax.dynamic_slice_in_dim(
                full_factor[:, col_start : col_start + B], offset, col_width, 0
            ),
            "row",
            root_row,
        )
        remote = jnp.where((col_rows >= col_start + B)[:, None], remote, 0.0)
        top_part = jnp.where(
            (corner_ids >= col_start + B)[:, None], corner_factor[:, col_start : col_start + B], 0.0
        )
        lower_block = jnp.tril(corner_factor[col_start : col_start + B, col_start : col_start + B])
        block_adj = corner_adj[col_start : col_start + B, col_start : col_start + B]
        lower_inverse = jax.scipy.linalg.solve_triangular(lower_block, identity, lower=True)
        lower_mask = (global_rows >= col_start + B)[:, None]
        partial_value = mdot(trail_adj, remote)
        column = jnp.where(lower_mask, full_factor[:, col_start : col_start + B], 0.0)
        local_adj = full_adj[:, col_start : col_start + B]
        summed = lax.psum(partial_value, "col")
        cross_term = lax.psum(mdot(accum.T, column), "row")
        image_term = (
            summed + mdot(accum, top_part) + place_rows(cross_term, global_rows, 0, panel_width)
        )
        factor_grad = jnp.where(lower_mask, local_adj - 2.0 * image_term, 0.0)
        off_adj = mdot(factor_grad, lower_inverse)
        block_part = mdot(column.T, off_adj)
        block_sum = lax.psum(block_part, "row")
        diag_adj = diag_adjoint(lower_block, lower_inverse, block_adj - block_sum)
        new_cols = jnp.where(lower_mask, 0.5 * off_adj, 0.0) + 0.5 * place_rows(
            diag_adj, global_rows, col_start, B
        )
        accum = accum.at[:, col_start : col_start + B].set(new_cols)
    out_width = panel_width // col_devices
    result = accum + place_rows(accum[:panel_width].T, global_rows, 0, panel_width)
    return lax.dynamic_slice_in_dim(result, col_index * out_width, out_width, 1)


def solution(mesh):
    in_specs = (P("row", "col"), P("row", "col"), P("row", "col"))
    out_specs = P("row", "col")
    return jax.shard_map(
        on_device, mesh=mesh, in_specs=in_specs, out_specs=out_specs, check_vma=False
    )
```

profile of v0, /device:TPU:1, one launch (start us, length us, event | category | flops | bytes accessed | tf_op | source)
XLA Modules:
  0.0 1100.1 jit_solution(11800368647450866560)
XLA Ops:
  7.3 88.2 %all-gather.7.cloned.1.call-done = f32[32,12,1024]{2,1,0:T(8,128)} async-done(((f32[1,12,1024]{2,1,0:T(8,128)}), f32[32,12,1024]{2,1,0:T(8,128)}) %all-gather.7.cloned.1.call-update) | async-done | bytes 1572880 | tf_op jit(solution)/shard_map/all_gather | solution.py:47
  98.2 3.0 copy.25
  107.9 120.4 %all-reduce.24.cloned.1.call-done = (f32[384,384]{1,0:T(8,128)}, f32[384,128]{1,0:T(8,128)}, f32[512,128]{1,0:T(8,128)}, f32[512,128]{1,0:T(8,128)}, f32[512,128]{1,0:T(8,128)}) async-done(((f32[384,384]{1,0:T(8,128)}, f32[384,128]{1,0:T(8,128)}, f32[512,128]{1,0:T(8,128)}, f32[512,128]{1,0:T(8,128)}, f32[512,128]{1,0:T(8,128)}), (f32[384,384]{1,0:T(8,128)}, f32[384,128]{1,0:T(8,128)}, ...) | async-done | bytes 1572880 | tf_op jit(solution)/shard_map/psum | solution.py:12
  228.4 3.7 convolution_bitcast_fusion
  237.8 73.6 %all-gather.5.cloned.1.call-done = f32[32,12,1024]{2,1,0:T(8,128)} async-done(((f32[1,12,1024]{2,1,0:T(8,128)}), f32[32,12,1024]{2,1,0:T(8,128)}) %all-gather.5.cloned.1.call-update) | async-done | bytes 1572880 | tf_op jit(solution)/shard_map/all_gather | solution.py:48
  314.1 3.0 copy.24
  320.0 9.8 custom-call.11
  334.0 141.2 %all-reduce.20.cloned.1.call-done = (f32[1024,128]{1,0:T(8,128)}, f32[1024,128]{1,0:T(8,128)}, f32[1024,128]{1,0:T(8,128)}) async-done(((f32[1024,128]{1,0:T(8,128)}, f32[1024,128]{1,0:T(8,128)}, f32[1024,128]{1,0:T(8,128)}), (f32[1024,128]{1,0:T(8,128)}, f32[1024,128]{1,0:T(8,128)}, f32[1024,128]{1,0:T(8,128)})) %all-reduce.20.cloned.1.call-update) | async-done | bytes 1572880 | tf_op jit(solution)/shard_map/psum | solution.py:79
  480.9 9.8 custom-call.12
  490.9 108.5 %all-reduce.22.cloned.1.call-done = (f32[128,128]{1,0:T(8,128)}, f32[384,384]{1,0:T(8,128)}) async-done(((f32[128,128]{1,0:T(8,128)}, f32[384,384]{1,0:T(8,128)}), (f32[128,128]{1,0:T(8,128)}, f32[384,384]{1,0:T(8,128)})) %all-reduce.22.cloned.1.call-update) | async-done | bytes 655376 | tf_op jit(solution)/shard_map/psum | solution.py:87
  602.4 4.0 gather_fusion.5
  608.3 3.3 fusion.8
  612.2 110.0 %all-reduce.12.cloned.1.call-done = f32[384,128]{1,0:T(8,128)} async-done(((f32[384,128]{1,0:T(8,128)}), f32[384,128]{1,0:T(8,128)}) %all-reduce.12.cloned.1.call-update) | async-done | bytes 196624 | tf_op jit(solution)/shard_map/psum | solution.py:80
  722.2 3.7 gather_fusion.6
  733.1 9.8 custom-call.13
  745.2 91.8 %all-reduce.14.cloned.1.call-done = f32[128,128]{1,0:T(8,128)} async-done(((f32[128,128]{1,0:T(8,128)}), f32[128,128]{1,0:T(8,128)}) %all-reduce.14.cloned.1.call-update) | async-done | bytes 65552 | tf_op jit(solution)/shard_map/psum | solution.py:87
  845.1 5.0 fusion.30
  850.7 108.3 %all-reduce.16.cloned.1.call-done = f32[384,128]{1,0:T(8,128)} async-done(((f32[384,128]{1,0:T(8,128)}), f32[384,128]{1,0:T(8,128)}) %all-reduce.16.cloned.1.call-update) | async-done | bytes 196624 | tf_op jit(solution)/shard_map/psum | solution.py:80
  959.0 3.7 gather_fusion.8
  962.8 3.4 fusion.7
  970.4 103.7 %all-reduce.18.cloned.1.call-done = f32[128,128]{1,0:T(8,128)} async-done(((f32[128,128]{1,0:T(8,128)}), f32[128,128]{1,0:T(8,128)}) %all-reduce.18.cloned.1.call-update) | async-done | bytes 65552 | tf_op jit(solution)/shard_map/psum | solution.py:87
  1077.3 4.0 gather_fusion.9
  1081.3 3.2 fusion.12
  1085.8 4.8 gather_fusion.3
  (103 shorter events, 66.2 us)
Async XLA Ops:
  6.5 221.9 %copy-start = (f32[1024,512]{1,0:T(8,128)S(1)}, f32[1024,512]{1,0:T(8,128)}, u32[]{:S(2)}) copy-start(f32[1024,512]{1,0:T(8,128)} %param.15) | copy-start | bytes 6291460
  6.5 89.1 %all-gather.7.cloned.1.call-start = ((), (), s32[]{:S(2)}) async-start(), calls=%async_computation.5 | async-start | bytes 2162688 | tf_op jit(solution)/shard_map/all_gather | solution.py:47
  7.3 221.1 %all-reduce.24.cloned.1.call-start = ((), (), s32[]{:S(2)}) async-start(), calls=%async_computation.8 | async-start | bytes 3145728 | tf_op jit(solution)/shard_map/psum | solution.py:12
  107.1 204.4 %all-gather.5.cloned.1.call-start = ((), (), s32[]{:S(2)}) async-start(), calls=%async_computation.4 | async-start | bytes 2162688 | tf_op jit(solution)/shard_map/all_gather | solution.py:48
  107.8 367.5 %all-reduce.20.cloned.1.call-start = ((), (), s32[]{:S(2)}) async-start(), calls=%async_computation.6 | async-start | bytes 3145728 | tf_op jit(solution)/shard_map/psum | solution.py:79
  228.4 3.7 copy-start.5
  232.1 2.7 copy-start.4
  237.5 361.9 %all-reduce.22.cloned.1.call-start = ((), (), s32[]{:S(2)}) async-start(), calls=%async_computation.7 | async-start | bytes 1310720 | tf_op jit(solution)/shard_map/psum | solution.py:87
  317.1 12.7 %copy-start.1 = (f32[384,128]{1,0:T(8,128)S(1)}, f32[384,128]{1,0:T(8,128)}, u32[]{:S(2)}) copy-start(f32[384,128]{1,0:T(8,128)} %get-tuple-element.50) | copy-start | bytes 589828
  480.8 241.4 %all-reduce.12.cloned.1.call-start = ((), (), s32[]{:S(2)}) async-start(), calls=%async_computation | async-start | bytes 393216 | tf_op jit(solution)/shard_map/psum | solution.py:80
  611.6 225.3 %all-reduce.14.cloned.1.call-start = ((), (), s32[]{:S(2)}) async-start(), calls=%async_computation.1 | async-start | bytes 131072 | tf_op jit(solution)/shard_map/psum | solution.py:87
  732.4 226.6 %all-reduce.16.cloned.1.call-start = ((), (), s32[]{:S(2)}) async-start(), calls=%async_computation.2 | async-start | bytes 393216 | tf_op jit(solution)/shard_map/psum | solution.py:80
  840.0 2.8 copy-start.2
  850.1 224.1 %all-reduce.18.cloned.1.call-start = ((), (), s32[]{:S(2)}) async-start(), calls=%async_computation.3 | async-start | bytes 131072 | tf_op jit(solution)/shard_map/psum | solution.py:87
  850.7 112.1 %copy-start.3 = (f32[1024,128]{1,0:T(8,128)S(1)}, f32[1024,128]{1,0:T(8,128)}, u32[]{:S(2)}) copy-start(f32[1024,128]{1,0:T(8,128)} %get-tuple-element.46) | copy-start | bytes 1572868
Sparse Core Ops, SparseCore 0:
  10.5 85.0 all-gather.6
  107.2 121.1 all-reduce.23
  232.0 79.3 all-gather.4
  315.4 159.7 all-reduce.19
  480.9 118.3 all-reduce.21
  611.7 110.4 all-reduce.11
  732.5 104.3 all-reduce.13
  850.2 108.7 all-reduce.15
  969.7 104.3 all-reduce.17
where the time goes:
time: 1100 us
  waiting for transfers between devices  947 us (86%)
  other arithmetic  49.3 us (4%)
  local copies, waits for them, and re-layouts  46.8 us (4%)
  matrix products  42 us (4%)
  between operations  13.7 us (1%)
    psum x3, waiting for transfers between devices, on_device(): block_sum = lax.psum(block_part, 'row')  304 us
    psum x2, waiting for transfers between devices, on_device(): cross_term = lax.psum(mdot(accum.T, column), 'row')  218 us
    psum x1, waiting for transfers between devices, on_device(): summed = lax.psum(partial_value, 'col')  141 us
    psum x1, waiting for transfers between devices, broadcast(): return lax.psum(jnp.where(mine, value, jnp.zeros_like(value)), axis)  120 us
    all_gather x1, waiting for transfers between devices, on_device(): lax.all_gather(factor_panels, 'col', axis=1, tiled=True)  88.2 us
    all_gather x1, waiting for transfers between devices, on_device(): lax.all_gather(factor_adj, 'col', axis=1, tiled=True)  73.6 us
    dot_general x22, matrix products, mdot(): jnp.dot(operand, other, precision=lax.Precision.HIGHEST, preferred_elemen...  41.2 us
    another operation x4, other arithmetic, on_device(): jax.scipy.linalg.solve_triangular(lower_block, identity, lower=True)  30.3 us
  transfers between devices with their start and end apart: 9, of which 9 were waited for; matrix products, arithmetic and copies ran while one was open for 5% of the time, Pallas kernels for 0%

commit v1 on v0

v1 whole, which is shorter than its diff:
```python
import functools

import jax
import jax.numpy as jnp
from jax import lax
from jax.experimental import pallas as pl
from jax.experimental.pallas import tpu as pltpu
from jax.sharding import PartitionSpec as P

B = 128
STEPS = 3
PW = STEPS * B
HI = lax.Precision.HIGHEST
X_SIZE, Y_SIZE = 4, 8
Y_GROUPS = [[x * Y_SIZE + y for y in range(Y_SIZE)] for x in range(X_SIZE)]
X_GROUPS = [[x * Y_SIZE + y for x in range(X_SIZE)] for y in range(Y_SIZE)]
PARAMS = pltpu.CompilerParams(vmem_limit_bytes=48 * 1024 * 1024)


def dot(a, b):
    return jnp.dot(a, b, precision=HI, preferred_element_type=jnp.float32)


def dot_nt(a, b):
    return lax.dot_general(
        a, b, (((1,), (1,)), ((), ())), precision=HI, preferred_element_type=jnp.float32
    )


def owner_col(row, half):
    return (2 * (row % 2) + half) * Y_SIZE + row // 2


def product_kernel(f_ref, t_ref, out_ref, ft_ref, acc_ref):
    row = lax.axis_index("row")
    panel = lax.broadcasted_iota(jnp.int32, (PW, B), 0) // B
    for b in range(8):
        part = f_ref[pl.ds(b, PW, stride=8), :]
        if b < STEPS:
            part = jnp.where((row > 0) | (panel < b), part, 0.0)
        ft_ref[:, b * B : (b + 1) * B] = part
    acc_ref[...] = dot(ft_ref[...], t_ref[...])
    for device in range(16):
        for half in range(2):
            first = 12 * owner_col(device, half)
            for b in range(4):
                out_ref[pl.ds(device * 96 + half * 48 + b, 12, stride=4), :] = acc_ref[
                    first : first + 12, b * B : (b + 1) * B
                ]


def sum_kernel(s_ref, a_ref, b_ref):
    odd = lax.axis_index("col") % 2 == 1
    low = jnp.sum(s_ref[:, 0:48, :], axis=0)
    high = jnp.sum(s_ref[:, 48:96, :], axis=0)
    a_ref[...] = jnp.where(odd, high, low)
    b_ref[...] = jnp.where(odd, low, high)


def inverse_kernel(f_ref, l_ref, lt_ref, li_ref, lit_ref, litp_ref):
    @pl.when(lax.axis_index("row") == 0)
    def _():
        rows = lax.broadcasted_iota(jnp.int32, (B, B), 0)
        cols = lax.broadcasted_iota(jnp.int32, (B, B), 1)
        for b in range(STEPS):
            lt_ref[:, b * B : (b + 1) * B] = f_ref[pl.ds(b, PW, stride=8), :]
        zero = jnp.zeros((B, B), jnp.float32)

        def blk(i, j):
            return (slice(i * B, (i + 1) * B), slice(j * B, (j + 1) * B))

        lt = {}
        for i in range(STEPS):
            for j in range(STEPS):
                if i > j:
                    lt_ref[blk(i, j)] = zero
                    continue
                value = lt_ref[blk(i, j)]
                if i == j:
                    value = jnp.where(rows <= cols, value, 0.0)
                    lt_ref[blk(i, j)] = value
                lt[i, j] = value
        inv = {}
        for i in range(STEPS):
            inv[i, i] = jnp.where(rows == cols, 1.0 / lt[i, i], 0.0)
        size = 1
        while size < B:
            mask = (rows // (2 * size) == cols // (2 * size)) & (rows // size < cols // size)
            step = [dot(inv[i, i], jnp.where(mask, lt[i, i], 0.0)) for i in range(STEPS)]
            for i in range(STEPS):
                inv[i, i] = inv[i, i] - dot(step[i], inv[i, i])
            size *= 2
        inv[0, 1] = -dot(dot(inv[0, 0], lt[0, 1]), inv[1, 1])
        inv[1, 2] = -dot(dot(inv[1, 1], lt[1, 2]), inv[2, 2])
        inv[0, 2] = -dot(dot(inv[0, 0], lt[0, 2]) + dot(inv[0, 1], lt[1, 2]), inv[2, 2])
        for i in range(STEPS):
            for j in range(STEPS):
                value = inv.get((i, j), zero)
                lit_ref[blk(i, j)] = value
                litp_ref[pl.ds(4 * i * B + j, B, stride=4), :] = value
                li_ref[blk(j, i)] = value.T if (i, j) in inv else zero
                l_ref[blk(j, i)] = lt[i, j].T if (i, j) in lt else zero
            litp_ref[pl.ds(4 * i * B + 3, B, stride=4), :] = zero


def gram_kernel(ra_ref, rb_ref, g_ref, ft_ref, litp_ref, pay_ref, y_ref, half_ref, ym_ref):
    row, col = lax.axis_index("row"), lax.axis_index("col")
    first = (col // Y_SIZE) % 2 == 0
    ra, rb = ra_ref[...], rb_ref[...]
    half_ref[0:48, :] = jnp.where(first, ra, rb)
    half_ref[48:96, :] = jnp.where(first, rb, ra)
    panel = (12 * col + lax.broadcasted_iota(jnp.int32, (12, B), 0)) // B
    top, diag = [], jnp.zeros((12, B), jnp.float32)
    for b in range(8):
        g = g_ref[pl.ds(b, 12, stride=8), :]
        y = g - 2.0 * half_ref[pl.ds(b // 4 * 48 + b % 4, 12, stride=4), :]
        y_ref[pl.ds(b, 12, stride=8), :] = y
        if b < STEPS:
            top.append(y)
            diag = jnp.where(panel == b, g, diag)
            y = jnp.where(row > 0, y, 0.0)
        ym_ref[:, b * B : (b + 1) * B] = y
    gram = dot_nt(ym_ref[...], ft_ref[...])
    for k in range(STEPS):
        below = jnp.where(row == 0, top[k], 0.0)
        pay_ref[pl.ds(k, 12, stride=4), :] = jnp.where(
            panel >= k, gram[:, k * B : (k + 1) * B], below
        )
    pay_ref[pl.ds(3, 12, stride=4), :] = jnp.where(row == 0, diag, 0.0)
    pay_ref[48:96, :] = litp_ref[pl.ds(pl.multiple_of(48 * col, 16), 48), :]


def tail_kernel(
    w_ref, own_ref, l_ref, lt_ref, li_ref, lit_ref, out_ref, yt_ref, own2_ref, u_ref, wp_ref, cut_ref
):
    row, col = lax.axis_index("row"), lax.axis_index("col")
    for x in range(X_SIZE):
        for b in range(8):
            yt_ref[96 * x : 96 * (x + 1), b * B : (b + 1) * B] = w_ref[
                pl.ds(x * 1152 + 384 + b, 96, stride=8), :
            ]
    for k in range(STEPS):
        own2_ref[:, k * B : (k + 1) * B] = own_ref[pl.ds(k, 12, stride=4), :]
    out_ref[...] = 0.5 * dot(own2_ref[...], yt_ref[...])

    @pl.when(row == 0)
    def _():
        for x in range(X_SIZE):
            for k in range(4):
                u_ref[96 * x : 96 * (x + 1), k * B : (k + 1) * B] = w_ref[
                    pl.ds(x * 1152 + k, 96, stride=4), :
                ]
        rows = lax.broadcasted_iota(jnp.int32, (B, B), 0)
        cols = lax.broadcasted_iota(jnp.int32, (B, B), 1)

        def blk(i, j):
            return (slice(i * B, (i + 1) * B), slice(j * B, (j + 1) * B))

        def low(i, j):
            return l_ref[blk(i, j)]

        wide = lax.broadcasted_iota(jnp.int32, (PW, PW), 0) // B
        tall = lax.broadcasted_iota(jnp.int32, (PW, PW), 1) // B
        zt = jnp.where(wide >= tall, u_ref[:, 0:PW], 0.0)
        yt_ref[:, 0:PW] = dot(lit_ref[...], zt)

        def vt(j, k):
            return yt_ref[blk(j, k)]

        def y_of(j, k):
            return u_ref[blk(k, j)].T

        def g_of(k):
            return u_ref[blk(k, STEPS)]

        def diag_adjoint(k, total_t):
            product_t = dot(total_t, low(k, k))
            halved_t = jnp.where(rows < cols, product_t, jnp.where(rows == cols, 0.5 * product_t, 0.0))
            sandwich = dot(dot(lit_ref[blk(k, k)], halved_t), li_ref[blk(k, k)])
            return 0.5 * (sandwich + sandwich.T)

        diag2 = diag_adjoint(2, g_of(2) - vt(2, 2))
        off21 = dot(y_of(2, 1) - 2.0 * dot(diag2, low(2, 1)) - vt(2, 1), li_ref[blk(1, 1)])
        off12 = off21.T
        diag1 = diag_adjoint(1, g_of(1) - vt(1, 1) - dot(off12, low(2, 1)))
        off20 = dot(
            y_of(2, 0) - dot(off21, low(1, 0)) - 2.0 * dot(diag2, low(2, 0)) - vt(2, 0),
            li_ref[blk(0, 0)],
        )
        off10 = dot(
            y_of(1, 0) - 2.0 * dot(diag1, low(1, 0)) - dot(off12, low(2, 0)) - vt(1, 0),
            li_ref[blk(0, 0)],
        )
        off02, off01 = off20.T, off10.T
        diag0 = diag_adjoint(0, g_of(0) - vt(0, 0) - dot(off01, low(1, 0)) - dot(off02, low(2, 0)))
        whole = {
            (0, 0): diag0, (1, 1): diag1, (2, 2): diag2,
            (1, 0): 0.5 * off10, (2, 0): 0.5 * off20, (2, 1): 0.5 * off21,
            (0, 1): 0.5 * off01, (0, 2): 0.5 * off02, (1, 2): 0.5 * off12,
        }
        for i in range(STEPS):
            for j in range(STEPS):
                wp_ref[pl.ds(4 * i * B + j, B, stride=4), :] = whole[i, j]
        cut_ref[...] = wp_ref[pl.ds(pl.multiple_of(48 * col, 16), 48), :]
        for k in range(STEPS):
            out_ref[:, k * B : (k + 1) * B] = cut_ref[pl.ds(k, 12, stride=4), :]


def f32(*shape):
    return jax.ShapeDtypeStruct(shape, jnp.float32)


def vmem(*shape):
    return pltpu.VMEM(shape, jnp.float32)


def call(kernel, out_shape, *args, scratch=(), flops=0):
    many = isinstance(out_shape, (list, tuple))
    spec = pl.BlockSpec(memory_space=pltpu.VMEM)
    total = sum(a.size for a in args) * 4
    return pl.pallas_call(
        kernel,
        out_shape=out_shape,
        in_specs=[spec] * len(args),
        out_specs=[spec] * len(out_shape) if many else spec,
        scratch_shapes=list(scratch),
        compiler_params=PARAMS,
        cost_estimate=pl.CostEstimate(flops=flops, bytes_accessed=total, transcendentals=0),
    )(*args)


def spread(value, groups):
    count = len(groups[0])
    copies = jnp.broadcast_to(value[None], (count,) + value.shape)
    return lax.all_to_all(copies, "col", 0, 0, axis_index_groups=groups)


def on_device(trail_adj, factor_panels, factor_adj):
    factor = factor_panels.T.reshape(96, B)
    adjoint = factor_adj.T.reshape(96, B)
    near = spread(factor, Y_GROUPS).reshape(Y_SIZE * 96, B)
    panels = spread(near, X_GROUPS).reshape(PW * 8, B)
    partial, ft = call(
        product_kernel, [f32(1536, B), f32(PW, 1024)], panels, trail_adj,
        scratch=[vmem(PW, 512)], flops=12 * 1024 * 512 * PW,
    )
    pieces = lax.all_to_all(partial.reshape(16, 96, B), "row", 0, 0)
    send_a, send_b = call(sum_kernel, [f32(48, B), f32(48, B)], pieces)
    rows, cols = range(16), range(32)
    to_a = [(r * 32 + c, c // 2 * 32 + owner_col(r, c % 2)) for r in rows for c in cols]
    to_b = [(r * 32 + c, c // 2 * 32 + owner_col(r, 1 - c % 2)) for r in rows for c in cols]
    got_a = lax.ppermute(send_a, ("row", "col"), to_a)
    got_b = lax.ppermute(send_b, ("row", "col"), to_b)
    low, low_t, inv, inv_t, inv_tp = call(
        inverse_kernel, [f32(PW, PW)] * 4 + [f32(1536, B)], panels, flops=12 * 60 * B**3,
    )
    payload, own_y = call(
        gram_kernel, [f32(96, B), f32(96, B)], got_a, got_b, adjoint, ft, inv_tp,
        scratch=[vmem(96, B), vmem(12, 1024)], flops=12 * 12 * 1024 * PW,
    )
    all_pay = lax.all_gather(payload, "row", axis=0)
    corner = jnp.sum(all_pay[:, :48], axis=0)
    own = all_pay[0, 48:]
    near = spread(jnp.concatenate([corner, own_y], axis=0), Y_GROUPS)
    near = jnp.concatenate([near[:, :48].reshape(384, B), near[:, 48:].reshape(768, B)], axis=0)
    whole = spread(near, X_GROUPS).reshape(X_SIZE * 1152, B)
    out = call(
        tail_kernel, f32(12, 1024), whole, own, low, low_t, inv, inv_t,
        scratch=[vmem(PW, 1024), vmem(12, PW), vmem(PW, 512), vmem(1536, B), vmem(48, B)],
        flops=12 * 12 * 1024 * PW,
    )
    return out.T


def solution(mesh):
    in_specs = (P("row", "col"), P("row", "col"), P("row", "col"))
    out_specs = P("row", "col")
    return jax.shard_map(
        on_device, mesh=mesh, in_specs=in_specs, out_specs=out_specs, check_vma=False
    )
```

time: 1100 us -> 191 us (0.17)
  the two profiles are of different devices: /device:TPU:1 before, /device:TPU:2 now
where the time goes in v1:
time: 191 us; the launch traced here: 190 us
  blocking collectives  95.6 us (50%)
  waiting for transfers between devices  45.9 us (24%)
  starting transfers between devices  22.1 us (12%)
  Pallas kernels  15.7 us (8%)
  local copies, waits for them, and re-layouts  10.6 us (6%)
    all_to_all x3, blocking collectives, spread(): return lax.all_to_all(copies, 'col', 0, 0, axis_index_groups=groups)  71.6 us
    all_to_all x1, waiting for transfers between devices, spread(): return lax.all_to_all(copies, 'col', 0, 0, axis_index_groups=groups)  25.9 us
    all_gather x1, blocking collectives, on_device(): all_pay = lax.all_gather(payload, 'row', axis=0)  24 us
    all_to_all x1, waiting for transfers between devices, on_device(): pieces = lax.all_to_all(partial.reshape(16, 96, B), 'row', 0, 0)  20 us
    pallas_call x5, Pallas kernels, call(): pl.pallas_call(kernel, out_shape=out_shape, in_specs=[spec] * len(args),...  15.7 us
    all_to_all x1, starting transfers between devices, on_device(): pieces = lax.all_to_all(partial.reshape(16, 96, B), 'row', 0, 0)  10.4 us
    unnamed x22, local copies, waits for them, and re-layouts  5.95 us
    all_to_all x1, starting transfers between devices, spread(): return lax.all_to_all(copies, 'col', 0, 0, axis_index_groups=groups)  5.05 us
  transfers between devices with their start and end apart: 4, of which 2 were waited for; matrix products, arithmetic and copies ran while one was open for 1% of the time, Pallas kernels for 2%

profile of v1, /device:TPU:2, one launch (start us, length us, event | category | flops | bytes accessed | tf_op | source)
XLA Modules:
  0.0 190.2 jit_solution(2209476175752207864)
XLA Ops:
  0.0 0.9 broadcast_in_dim.12
  0.9 21.6 %all_to_all.25 = f32[8,96,128]{2,1,0:T(8,128)S(1)} all-to-all(f32[8,96,128]{2,1,0:T(8,128)S(1)} %broadcast_in_dim.13), channel_id=1, replica_groups={{0,1,2,3,4,5,6,7},{8,9,10,11,12,13,14,15},{16,17,18,19,20,21,22,23},{24..., dimensions={0} | all-to-all | bytes 786432 | tf_op jit(solution)/shard_map/all_to_all | solution.py:235
  22.6 22.6 %all_to_all.26 = f32[4,768,128]{2,1,0:T(8,128)S(1)} all-to-all(f32[4,768,128]{2,1,0:T(8,128)S(1)} %broadcast_in_dim.29), channel_id=1, replica_groups={{0,8,16,24},{1,9,17,25},{2,10,18,26},{3,11,19,27},{4,12,20,28},{5,13,21..., dimensions={0} | all-to-all | bytes 3145728 | tf_op jit(solution)/shard_map/all_to_all | solution.py:235
  45.2 3.7 %shard_map.37 = (f32[1536,128]{1,0:T(8,128)}, f32[384,1024]{1,0:T(8,128)S(1)}) custom-call(f32[3072,128]{1,0:T(8,128)S(1)} %bitcast.13, f32[1024,512]{1,0:T(8,128)S(1)} %copy-done.8), custom_call_target="tpu_custom_call" | custom-call | flops 2415919104 | bytes 3670016 | tf_op jit(solution)/shard_map/pallas_call | solution.py:221
  48.9 10.4 %all-to-all-start.2 = ((f32[16,96,128]{2,1,0:T(8,128)}), f32[16,96,128]{2,1,0:T(8,128)S(1)}, u32[]{:S(2)}, u32[]{:S(2)}) async-start(f32[16,96,128]{2,1,0:T(8,128)} %bitcast.3), calls=%async_computation.2 | async-start | bytes 1572864 | tf_op jit(solution)/shard_map/all_to_all | solution.py:247
  59.3 0.6 reshape.24.g_ref
  59.9 20.0 %all-to-all-done.2.s_ref = f32[16,96,128]{2,1,0:T(8,128)S(1)} async-done(((f32[16,96,128]{2,1,0:T(8,128)}), f32[16,96,128]{2,1,0:T(8,128)S(1)}, u32[]{:S(2)}, u32[]{:S(2)}) %all-to-all-start.2) | async-done | bytes 786464 | tf_op jit(solution)/shard_map/all_to_all | solution.py:247
  80.0 4.7 %collective-permute-start = (f32[48,128]{1,0:T(8,128)S(1)}, f32[48,128]{1,0:T(8,128)S(1)}, u32[]{:S(2)}, u32[]{:S(2)}) collective-permute-start(f32[48,128]{1,0:T(8,128)S(1)} %get-tuple-element.17), channel_id=1, source_target_pairs={{0,0},{1,8},{2,32},{3,40},{4,64},{5,72},{6,96},{7,104},{8,128},{9,... | collective-permute-start | bytes 73736 | tf_op jit(solution)/shard_map/ppermute | solution.py:252
  84.7 1.9 %collective-permute-start.1 = (f32[48,128]{1,0:T(8,128)S(1)}, f32[48,128]{1,0:T(8,128)S(1)}, u32[]{:S(2)}, u32[]{:S(2)}) collective-permute-start(f32[48,128]{1,0:T(8,128)S(1)} %get-tuple-element.18), channel_id=1, source_target_pairs={{0,8},{1,0},{2,40},{3,32},{4,72},{5,64},{6,104},{7,96},{8,136},{9,... | collective-permute-start | bytes 73736 | tf_op jit(solution)/shard_map/ppermute | solution.py:253
  86.7 1.4 copy-done.1
  88.1 4.2 %shard_map.39 = (f32[384,384]{1,0:T(8,128)S(1)}, f32[384,384]{1,0:T(8,128)S(1)}, f32[384,384]{1,0:T(8,128)S(1)}, f32[384,384]{1,0:T(8,128)S(1)}, f32[1536,128]{1,0:T(8,128)S(1)}) custom-call(f32[3072,128]{1,0:T(8,128)S(1)} %bitcast.14), custom_call_target="tpu_custom_call" | custom-call | flops 1509949440 | bytes 1572864 | tf_op jit(solution)/shard_map/pallas_call | solution.py:221
  92.3 0.8 copy-done.4
  93.2 1.4 shard_map.40
  94.5 24.0 %all-gather = f32[1536,128]{1,0:T(8,128)S(1)} all-gather(f32[96,128]{1,0:T(8,128)S(1)} %get-tuple-element.21), channel_id=2, replica_groups=mesh['row'=16,'col'=32] {'row'}, dimensions={0}, use_global_device_ids=true | all-gather | bytes 835584 | tf_op jit(solution)/shard_map/all_gather | solution.py:261
  118.5 0.8 copy-done.9
  119.4 27.5 %all_to_all.27 = f32[8,144,128]{2,1,0:T(8,128)S(1)} all-to-all(f32[8,144,128]{2,1,0:T(8,128)S(1)} %broadcast_in_dim.30), channel_id=1, replica_groups={{0,1,2,3,4,5,6,7},{8,9,10,11,12,13,14,15},{16,17,18,19,20,21,22,23},{24..., dimensions={0} | all-to-all | bytes 1179648 | tf_op jit(solution)/shard_map/all_to_all | solution.py:235
  147.0 1.6 broadcast_in_dim.31
  148.6 5.1 %all-to-all-start.4 = ((f32[4,1152,128]{2,1,0:T(8,128)}), f32[4,1152,128]{2,1,0:T(8,128)S(1)}, u32[]{:S(2)}, u32[]{:S(2)}) async-start(f32[4,1152,128]{2,1,0:T(8,128)} %broadcast_in_dim.31), calls=%async_computation.4 | async-start | bytes 4718592 | tf_op jit(solution)/shard_map/all_to_all | solution.py:235
  153.6 1.3 slice_bitcast_fusion.own_ref
  155.0 25.9 %all-to-all-done.4 = f32[4,1152,128]{2,1,0:T(8,128)S(1)} async-done(((f32[4,1152,128]{2,1,0:T(8,128)}), f32[4,1152,128]{2,1,0:T(8,128)S(1)}, u32[]{:S(2)}, u32[]{:S(2)}) %all-to-all-start.4) | async-done | bytes 2359328 | tf_op jit(solution)/shard_map/all_to_all | solution.py:235
  180.9 1.1 copy-done.3
  181.9 1.1 copy-done.5
  183.0 0.7 copy-done.7
  183.7 6.4 %shard_map.41 = f32[12,1024]{1,0:T(8,128)} custom-call(f32[4608,128]{1,0:T(8,128)S(1)} %bitcast.12, f32[48,128]{1,0:T(8,128)S(1)} %copy-done.7, f32[384,384]{1,0:T(8,128)S(1)} %get-tuple-element.23.l_ref, f32[384,384]{1,0:T(8,128)S(1)} %get-tuple-element.24.lt_ref, f32[384,384]{1,0:T(8,128)S(1)} %copy-done.3, f32[384,384]{1,0:T(8,128)S(1)} %copy-done.5), custom_call_target="tpu_custom_call" | custom-call | flops 56623104 | bytes 4743168 | tf_op jit(solution)/shard_map/pallas_call | solution.py:221
  (27 shorter events, 0.4 us)
Async XLA Ops:
  22.5 22.7 %copy-start.8 = (f32[1024,512]{1,0:T(8,128)S(1)}, f32[1024,512]{1,0:T(8,128)}, u32[]{:S(2)}) copy-start(f32[1024,512]{1,0:T(8,128)} %t_ref.1) | copy-start | bytes 6291460
  45.1 3.7 %copy-start = (f32[4,768,128]{2,1,0:T(8,128)}, f32[4,768,128]{2,1,0:T(8,128)S(1)}, u32[]{:S(2)}) copy-start(f32[4,768,128]{2,1,0:T(8,128)S(1)} %all_to_all.26) | copy-start | bytes 4718596
  45.2 14.1 %copy-start.10 = (f32[1024,12]{0,1:T(8,128)S(1)}, f32[1024,12]{0,1:T(8,128)}, u32[]{:S(2)}) copy-start(f32[1024,12]{0,1:T(8,128)} %param.5) | copy-start | bytes 147460
  48.9 31.1 %all-to-all-start.2 = ((f32[16,96,128]{2,1,0:T(8,128)}), f32[16,96,128]{2,1,0:T(8,128)S(1)}, u32[]{:S(2)}, u32[]{:S(2)}) async-start(f32[16,96,128]{2,1,0:T(8,128)} %bitcast.3), calls=%async_computation.2 | async-start | bytes 1572864 | tf_op jit(solution)/shard_map/all_to_all | solution.py:247
  80.0 13.1 %collective-permute-start = (f32[48,128]{1,0:T(8,128)S(1)}, f32[48,128]{1,0:T(8,128)S(1)}, u32[]{:S(2)}, u32[]{:S(2)}) collective-permute-start(f32[48,128]{1,0:T(8,128)S(1)} %get-tuple-element.17), channel_id=1, source_target_pairs={{0,0},{1,8},{2,32},{3,40},{4,64},{5,72},{6,96},{7,104},{8,128},{9,... | collective-permute-start | bytes 73736 | tf_op jit(solution)/shard_map/ppermute | solution.py:252
  84.7 8.4 %collective-permute-start.1 = (f32[48,128]{1,0:T(8,128)S(1)}, f32[48,128]{1,0:T(8,128)S(1)}, u32[]{:S(2)}, u32[]{:S(2)}) collective-permute-start(f32[48,128]{1,0:T(8,128)S(1)} %get-tuple-element.18), channel_id=1, source_target_pairs={{0,8},{1,0},{2,40},{3,32},{4,72},{5,64},{6,104},{7,96},{8,136},{9,... | collective-permute-start | bytes 73736 | tf_op jit(solution)/shard_map/ppermute | solution.py:253
  86.7 1.4 copy-start.1
  88.1 5.1 %copy-start.6 = (f32[96,128]{1,0:T(8,128)S(1)}, f32[96,128]{1,0:T(8,128)}, u32[]{:S(2)}) copy-start(f32[96,128]{1,0:T(8,128)} %reshape.24.g_ref) | copy-start | bytes 147460
  92.3 0.8 copy-start.4
  93.1 26.3 %copy-start.2 = (f32[384,384]{1,0:T(8,128)}, f32[384,384]{1,0:T(8,128)S(1)}, u32[]{:S(2)}) copy-start(f32[384,384]{1,0:T(8,128)S(1)} %get-tuple-element.25.li_ref) | copy-start | bytes 1769476
  118.5 0.9 copy-start.9
  148.6 32.3 %all-to-all-start.4 = ((f32[4,1152,128]{2,1,0:T(8,128)}), f32[4,1152,128]{2,1,0:T(8,128)S(1)}, u32[]{:S(2)}, u32[]{:S(2)}) async-start(f32[4,1152,128]{2,1,0:T(8,128)} %broadcast_in_dim.31), calls=%async_computation.4 | async-start | bytes 4718592 | tf_op jit(solution)/shard_map/all_to_all | solution.py:235
  180.9 1.1 copy-start.3
  181.9 1.1 copy-start.5
  183.0 0.7 copy-start.7

commit v2 on v1

v2 whole, which is shorter than its diff:
```python
import functools

import jax
import jax.numpy as jnp
from jax import lax
from jax.experimental import pallas as pl
from jax.experimental.pallas import tpu as pltpu
from jax.sharding import PartitionSpec as P

B = 128
STEPS = 3
PW = STEPS * B
HI = lax.Precision.HIGHEST
X_SIZE, Y_SIZE = 4, 8
Y_GROUPS = [[x * Y_SIZE + y for y in range(Y_SIZE)] for x in range(X_SIZE)]
X_GROUPS = [[x * Y_SIZE + y for x in range(X_SIZE)] for y in range(Y_SIZE)]
Z_GROUPS = [[2 * z + core for z in range(8)] for core in range(2)]
PARAMS = pltpu.CompilerParams(vmem_limit_bytes=48 * 1024 * 1024)


def dot(a, b):
    return jnp.dot(a, b, precision=HI, preferred_element_type=jnp.float32)


def dot_nt(a, b):
    return lax.dot_general(
        a, b, (((1,), (1,)), ((), ())), precision=HI, preferred_element_type=jnp.float32
    )


def place(row, col, half):
    x, y = col // Y_SIZE, col % Y_SIZE
    x_to, y_to = (x + 2 * (row % 2) + half) % X_SIZE, (y + row // 2) % Y_SIZE
    return col // 2 * (X_SIZE * Y_SIZE) + x_to * Y_SIZE + y_to


def product_kernel(f_ref, t_ref, send_ref, keep_ref, ft_ref, top_ref, acc_ref, cut_ref, pick_ref):
    row, col = lax.axis_index("row"), lax.axis_index("col")
    x, y = col // Y_SIZE, col % Y_SIZE
    panel = lax.broadcasted_iota(jnp.int32, (PW, B), 0) // B
    for b in range(8):
        part = f_ref[pl.ds(b, PW, stride=8), :]
        if b < STEPS:
            top_ref[:, b * B : (b + 1) * B] = part
            part = jnp.where((row > 0) | (panel < b), part, 0.0)
        ft_ref[:, b * B : (b + 1) * B] = part
    for core, target in ((1 - row % 2, send_ref), (row % 2, keep_ref)):
        for half in range(2):
            first = pl.multiple_of((x + 2 * core + half) % X_SIZE * 96, 8)
            pick_ref[half * 96 : (half + 1) * 96, :] = ft_ref[pl.ds(first, 96), :]
        acc_ref[...] = dot(pick_ref[...], t_ref[...])
        for b in range(4):
            cut_ref[pl.ds(b, PW // 2, stride=4), :] = acc_ref[:, b * B : (b + 1) * B]
        for z in range(8):
            for half in range(2):
                first = pl.multiple_of(half * 384 + (y + z) % Y_SIZE * 48, 16)
                target[z * 96 + half * 48 : z * 96 + half * 48 + 48, :] = cut_ref[pl.ds(first, 48), :]


def sum_kernel(s_ref, a_ref, b_ref):
    odd = lax.axis_index("col") % 2 == 1
    low = jnp.sum(s_ref[:, 0:48, :], axis=0)
    high = jnp.sum(s_ref[:, 48:96, :], axis=0)
    a_ref[...] = jnp.where(odd, high, low)
    b_ref[...] = jnp.where(odd, low, high)


def corner_block(kind, i, j):
    lower = {(0, 0): 0, (1, 0): 1, (1, 1): 2, (2, 0): 3, (2, 1): 4, (2, 2): 5}
    if kind == "l":
        place = lower[i, j]
    elif kind == "lit":
        place = 6 + lower[j, i]
    else:
        place = 12 + i
    return slice(place * B, (place + 1) * B)


def inverse_kernel(top_ref, fac_ref, litp_ref):
    @pl.when(lax.axis_index("row") == 0)
    def _():
        rows = lax.broadcasted_iota(jnp.int32, (B, B), 0)
        cols = lax.broadcasted_iota(jnp.int32, (B, B), 1)
        lt = {}
        for j in range(STEPS):
            for i in range(j + 1):
                value = top_ref[i * B : (i + 1) * B, j * B : (j + 1) * B]
                lt[i, j] = jnp.where(rows <= cols, value, 0.0) if i == j else value
                fac_ref[corner_block("l", j, i)] = lt[i, j].T
        inv = {}
        for i in range(STEPS):
            inv[i, i] = jnp.where(rows == cols, 1.0 / lt[i, i], 0.0)
        size = 1
        while size < B:
            mask = (rows // (2 * size) == cols // (2 * size)) & (rows // size < cols // size)
            step = [dot(inv[i, i], jnp.where(mask, lt[i, i], 0.0)) for i in range(STEPS)]
            for i in range(STEPS):
                inv[i, i] = inv[i, i] - dot(step[i], inv[i, i])
            size *= 2
        inv[0, 1] = -dot(dot(inv[0, 0], lt[0, 1]), inv[1, 1])
        inv[1, 2] = -dot(dot(inv[1, 1], lt[1, 2]), inv[2, 2])
        inv[0, 2] = -dot(dot(inv[0, 0], lt[0, 2]) + dot(inv[0, 1], lt[1, 2]), inv[2, 2])
        zero = jnp.zeros((B, B), jnp.float32)
        for i in range(STEPS):
            for j in range(4):
                litp_ref[pl.ds(4 * i * B + j, B, stride=4), :] = inv.get((i, j), zero)
            for j in range(i, STEPS):
                fac_ref[corner_block("lit", i, j)] = inv[i, j]
            fac_ref[corner_block("li", i, i)] = inv[i, i].T


def gram_kernel(ra_ref, rb_ref, g_ref, ft_ref, litp_ref, pay_ref, y_ref, half_ref, ym_ref):
    row, col = lax.axis_index("row"), lax.axis_index("col")
    first = (col // Y_SIZE + row // 4) % 2 == 0
    ra, rb = ra_ref[...], rb_ref[...]
    half_ref[0:48, :] = jnp.where(first, ra, rb)
    half_ref[48:96, :] = jnp.where(first, rb, ra)
    panel = (12 * col + lax.broadcasted_iota(jnp.int32, (12, B), 0)) // B
    top, diag = [], jnp.zeros((12, B), jnp.float32)
    for b in range(8):
        g = g_ref[pl.ds(b, 12, stride=8), :]
        y = g - 2.0 * half_ref[pl.ds(b // 4 * 48 + b % 4, 12, stride=4), :]
        y_ref[pl.ds(b, 12, stride=8), :] = y
        if b < STEPS:
            top.append(y)
            diag = jnp.where(panel == b, g, diag)
            y = jnp.where(row > 0, y, 0.0)
        ym_ref[:, b * B : (b + 1) * B] = y
    gram = dot_nt(ym_ref[...], ft_ref[...])
    for k in range(STEPS):
        below = jnp.where(row == 0, top[k], 0.0)
        pay_ref[pl.ds(k, 12, stride=4), :] = jnp.where(
            panel >= k, gram[:, k * B : (k + 1) * B], below
        )
    pay_ref[pl.ds(3, 12, stride=4), :] = jnp.where(row == 0, diag, 0.0)
    own = litp_ref[pl.ds(pl.multiple_of(48 * col, 16), 48), :]
    pay_ref[48:96, :] = jnp.where(row == 0, own, 0.0)


def tail_kernel(
    y0_ref, y1_ref, y2_ref, y3_ref, mine_ref, got_ref, w_ref, fac_ref,
    out_ref, yt_ref, own_ref, lit_ref, u_ref, vt_ref, wp_ref, cut_ref,
):
    row = lax.axis_index("row")
    x = lax.axis_index("col") // Y_SIZE
    for step, y_ref in enumerate((y0_ref, y1_ref, y2_ref, y3_ref)):
        first = pl.multiple_of((x + step) % X_SIZE * 96, 8)
        for b in range(8):
            yt_ref[pl.ds(first, 96), b * B : (b + 1) * B] = y_ref[pl.ds(b, 96, stride=8), :]
    own_ref[...] = jnp.where(row < 2, mine_ref[...], got_ref[0])
    for k in range(STEPS):
        lit_ref[:, k * B : (k + 1) * B] = own_ref[pl.ds(k, 12, stride=4), :]
    out_ref[...] = 0.5 * dot(lit_ref[...], yt_ref[...])

    @pl.when(row == 0)
    def _():
        for k in range(4):
            u_ref[:, k * B : (k + 1) * B] = w_ref[pl.ds(k, PW, stride=4), :]
        rows = lax.broadcasted_iota(jnp.int32, (B, B), 0)
        cols = lax.broadcasted_iota(jnp.int32, (B, B), 1)

        def blk(i, j):
            return (slice(i * B, (i + 1) * B), slice(j * B, (j + 1) * B))

        def fac(kind, i, j):
            return fac_ref[corner_block(kind, i, j)]

        for j in range(STEPS):
            for k in range(j + 1):
                terms = [dot(fac("lit", j, i), u_ref[blk(i, k)]) for i in range(j, STEPS)]
                vt_ref[blk(j, k)] = functools.reduce(jnp.add, terms)

        def vt(j, k):
            return vt_ref[blk(j, k)]

        def y_of(j, k):
            return u_ref[blk(k, j)].T

        def g_of(k):
            return u_ref[blk(k, STEPS)]

        def diag_adjoint(k, total_t):
            product_t = dot(total_t, fac("l", k, k))
            halved_t = jnp.where(rows < cols, product_t, jnp.where(rows == cols, 0.5 * product_t, 0.0))
            sandwich = dot(dot(fac("lit", k, k), halved_t), fac("li", k, k))
            return 0.5 * (sandwich + sandwich.T)

        l10, l20, l21 = fac("l", 1, 0), fac("l", 2, 0), fac("l", 2, 1)
        li0, li1 = fac("li", 0, 0), fac("li", 1, 1)
        diag2 = diag_adjoint(2, g_of(2) - vt(2, 2))
        off21 = dot(y_of(2, 1) - 2.0 * dot(diag2, l21) - vt(2, 1), li1)
        off12 = off21.T
        diag1 = diag_adjoint(1, g_of(1) - vt(1, 1) - dot(off12, l21))
        off20 = dot(y_of(2, 0) - dot(off21, l10) - 2.0 * dot(diag2, l20) - vt(2, 0), li0)
        off10 = dot(y_of(1, 0) - 2.0 * dot(diag1, l10) - dot(off12, l20) - vt(1, 0), li0)
        off02, off01 = off20.T, off10.T
        diag0 = diag_adjoint(0, g_of(0) - vt(0, 0) - dot(off01, l10) - dot(off02, l20))
        whole = {
            (0, 0): diag0, (1, 1): diag1, (2, 2): diag2,
            (1, 0): 0.5 * off10, (2, 0): 0.5 * off20, (2, 1): 0.5 * off21,
            (0, 1): 0.5 * off01, (0, 2): 0.5 * off02, (1, 2): 0.5 * off12,
        }
        for i in range(STEPS):
            for j in range(STEPS):
                wp_ref[pl.ds(4 * i * B + j, B, stride=4), :] = whole[i, j]
        start = pl.multiple_of(48 * lax.axis_index("col"), 16)
        cut_ref[...] = wp_ref[pl.ds(start, 48), :]
        for k in range(STEPS):
            out_ref[:, k * B : (k + 1) * B] = cut_ref[pl.ds(k, 12, stride=4), :]


def route_kernel(mine_ref, other_ref, _, out_ref, sum_ref, own_ref):
    mine, other = mine_ref[...], other_ref[...]
    corner = mine[0:48] + other[0:48]
    inverse = mine[48:96] + other[48:96]
    sum_ref[...] = corner
    own_ref[...] = inverse
    out_ref[0] = corner
    for z in range(1, 8):
        out_ref[z] = inverse


def corner_sum_kernel(mine_ref, got_ref, *rest):
    rest[-1][...] = mine_ref[...] + jnp.sum(got_ref[1:], axis=0)


def f32(*shape):
    return jax.ShapeDtypeStruct(shape, jnp.float32)


def vmem(*shape):
    return pltpu.VMEM(shape, jnp.float32)


def call(kernel, out_shape, *args, scratch=(), flops=0, after=()):
    many = isinstance(out_shape, (list, tuple))
    spec = pl.BlockSpec(memory_space=pltpu.VMEM)
    total = sum(a.size for a in args) * 4
    return pl.pallas_call(
        kernel,
        out_shape=out_shape,
        in_specs=[spec] * len(args) + [pl.BlockSpec(memory_space=pl.ANY)] * len(after),
        out_specs=[spec] * len(out_shape) if many else spec,
        scratch_shapes=list(scratch),
        compiler_params=PARAMS,
        cost_estimate=pl.CostEstimate(flops=flops, bytes_accessed=total, transcendentals=0),
    )(*args, *after)


def spread(value, axis, groups):
    count = len(groups[0])
    copies = jnp.broadcast_to(value[None], (count,) + value.shape)
    return lax.all_to_all(copies, axis, 0, 0, axis_index_groups=groups)


def between_cores(value):
    return lax.ppermute(value, "row", [(r, r ^ 1) for r in range(16)])


def from_x(value, step):
    pairs = [((c + step * Y_SIZE) % (X_SIZE * Y_SIZE), c) for c in range(X_SIZE * Y_SIZE)]
    return lax.ppermute(value, "col", pairs)


def on_device(trail_adj, factor_panels, factor_adj):
    factor = factor_panels.T.reshape(96, B)
    adjoint = factor_adj.T.reshape(96, B)
    near = spread(factor, "col", Y_GROUPS).reshape(Y_SIZE * 96, B)
    panels = spread(near, "col", X_GROUPS).reshape(PW * 8, B)
    send, keep, ft, ft_corner = call(
        product_kernel, [f32(768, B), f32(768, B), f32(PW, 1024), f32(PW, PW)], panels, trail_adj,
        scratch=[vmem(PW // 2, 512), vmem(768, B), vmem(PW // 2, 1024)], flops=12 * 1024 * 512 * PW,
    )
    both = (keep + between_cores(send)).reshape(8, 96, B)
    pieces = lax.all_to_all(both, "row", 0, 0, axis_index_groups=Z_GROUPS)
    send_a, send_b = call(sum_kernel, [f32(48, B), f32(48, B)], pieces)
    devices = [(r, c) for r in range(16) for c in range(32)]
    to_a = [(r * 32 + c, place(r, c, c % 2)) for r, c in devices]
    to_b = [(r * 32 + c, place(r, c, 1 - c % 2)) for r, c in devices]
    got_a = lax.ppermute(send_a, ("row", "col"), to_a)
    got_b = lax.ppermute(send_b, ("row", "col"), to_b)
    fac, inv_tp = call(
        inverse_kernel, [f32(15 * B, B), f32(1536, B)], ft_corner, flops=12 * 60 * B**3,
    )
    payload, own_y = call(
        gram_kernel, [f32(96, B), f32(96, B)], got_a, got_b, adjoint, ft, inv_tp,
        scratch=[vmem(96, B), vmem(12, 1024)], flops=12 * 12 * 1024 * PW,
    )
    near_y = spread(own_y, "col", Y_GROUPS).reshape(Y_SIZE * 96, B)
    all_y = [near_y] + [from_x(near_y, step) for step in range(1, X_SIZE)]
    out_u, sum_u, own = call(
        route_kernel, [f32(8, 48, B), f32(48, B), f32(48, B)], payload, between_cores(payload),
        after=[near_y],
    )
    got = lax.all_to_all(out_u, "row", 0, 0, axis_index_groups=Z_GROUPS)
    corner_u = call(corner_sum_kernel, f32(48, B), sum_u, got, after=all_y[1:])
    near_u = spread(corner_u, "col", Y_GROUPS).reshape(Y_SIZE * 48, B)
    all_u = spread(near_u, "col", X_GROUPS).reshape(PW * 4, B)
    out = call(
        tail_kernel, f32(12, 1024), *all_y, own, got, all_u, fac,
        scratch=[
            vmem(PW, 1024), vmem(48, B), vmem(12, PW), vmem(PW, 512), vmem(PW, PW), vmem(1536, B),
            vmem(48, B),
        ],
        flops=12 * 12 * 1024 * PW,
    )
    return out.T


def solution(mesh):
    in_specs = (P("row", "col"), P("row", "col"), P("row", "col"))
    out_specs = P("row", "col")
    return jax.shard_map(
        on_device, mesh=mesh, in_specs=in_specs, out_specs=out_specs, check_vma=False
    )
```

time: 191 us -> 176 us (0.921)
  starting transfers between devices: 22.1 us -> 40.1 us
  waiting for transfers between devices: 45.9 us -> 29.7 us
  blocking collectives: 95.6 us -> 85.9 us
  local copies, waits for them, and re-layouts: 10.6 us -> 1.86 us
    all_gather x1 -> x0, blocking collectives: 24 us -> none  [on_device(): all_pay = lax.all_gather(payload, 'row', axis=0)]
    all_to_all x2, waiting for transfers between devices: 45.9 us -> 26.9 us  [the longest x1 15 us: on_device(): pieces = lax.all_to_all(both, 'row', 0, 0, axis_index_groups=Z_GROUPS)]
    ppermute x0 -> x5, starting transfers between devices: none -> 14.4 us  [the longest x3 10.4 us: from_x(): return lax.ppermute(value, 'col', pairs)]
    all_to_all x3 -> x5, blocking collectives: 71.6 us -> 85.9 us  [the longest x4 70 us: spread(): return lax.all_to_all(copies, axis, 0, 0, axis_index_groups=groups)]
    all_to_all x2, starting transfers between devices: 15.5 us -> 21.8 us  [the longest x1 11.5 us: spread(): return lax.all_to_all(copies, axis, 0, 0, axis_index_groups=groups)]
    unnamed x22 -> x2, local copies, waits for them, and re-layouts: 5.95 us -> 0.01 us
    ppermute x1, starting transfers between devices: 4.71 us -> 1.92 us  [on_device(): got_a = lax.ppermute(send_a, ('row', 'col'), to_a)]
    pallas_call x5 -> x7, Pallas kernels: 15.7 us -> 16.6 us  [call(): pl.pallas_call(kernel, out_shape=out_shape, in_specs=[spec] * len(args) +...]
  transfers between devices with their start and end apart: 4 -> 9, of which waited for: 2 -> 4; matrix products, arithmetic and copies ran while one was open for 1% -> 0% of each run, Pallas kernels for 2% -> 2%
where the time goes in v2:
time: 176 us; the launch traced here: 175 us
  blocking collectives  85.9 us (49%)
  starting transfers between devices  40.1 us (23%)
  waiting for transfers between devices  29.7 us (17%)
  Pallas kernels  16.6 us (9%)
  local copies, waits for them, and re-layouts  1.86 us (1%)
    all_to_all x4, blocking collectives, spread(): return lax.all_to_all(copies, axis, 0, 0, axis_index_groups=groups)  70 us
    pallas_call x7, Pallas kernels, call(): pl.pallas_call(kernel, out_shape=out_shape, in_specs=[spec] * len(args) +...  16.6 us
    all_to_all x1, blocking collectives, on_device(): got = lax.all_to_all(out_u, 'row', 0, 0, axis_index_groups=Z_GROUPS)  15.9 us
    all_to_all x1, waiting for transfers between devices, on_device(): pieces = lax.all_to_all(both, 'row', 0, 0, axis_index_groups=Z_GROUPS)  15 us
    all_to_all x1, waiting for transfers between devices, spread(): return lax.all_to_all(copies, axis, 0, 0, axis_index_groups=groups)  12 us
    all_to_all x1, starting transfers between devices, spread(): return lax.all_to_all(copies, axis, 0, 0, axis_index_groups=groups)  11.5 us
    ppermute x3, starting transfers between devices, from_x(): return lax.ppermute(value, 'col', pairs)  10.4 us
    all_to_all x1, starting transfers between devices, on_device(): pieces = lax.all_to_all(both, 'row', 0, 0, axis_index_groups=Z_GROUPS)  10.3 us
  transfers between devices with their start and end apart: 9, of which 4 were waited for; matrix products, arithmetic and copies ran while one was open for 0% of the time, Pallas kernels for 2%

profile of v2, /device:TPU:2, one launch (start us, length us, event | category | flops | bytes accessed | tf_op | source)
XLA Modules:
  0.0 175.0 jit_solution(5240496004584845910)
XLA Ops:
  0.0 0.9 broadcast_in_dim.16
  0.9 21.6 %all_to_all.35 = f32[8,96,128]{2,1,0:T(8,128)S(1)} all-to-all(f32[8,96,128]{2,1,0:T(8,128)S(1)} %broadcast_in_dim.34), channel_id=1, replica_groups={{0,1,2,3,4,5,6,7},{8,9,10,11,12,13,14,15},{16,17,18,19,20,21,22,23},{24..., dimensions={0} | all-to-all | bytes 786432 | tf_op jit(solution)/shard_map/all_to_all | solution.py:253
  22.6 22.4 %all_to_all.36 = f32[4,768,128]{2,1,0:T(8,128)S(1)} all-to-all(f32[4,768,128]{2,1,0:T(8,128)S(1)} %broadcast_in_dim.36), channel_id=1, replica_groups={{0,8,16,24},{1,9,17,25},{2,10,18,26},{3,11,19,27},{4,12,20,28},{5,13,21..., dimensions={0} | all-to-all | bytes 3145728 | tf_op jit(solution)/shard_map/all_to_all | solution.py:253
  45.0 5.0 %shard_map.37 = (f32[768,128]{1,0:T(8,128)S(1)}, f32[768,128]{1,0:T(8,128)S(1)}, f32[384,1024]{1,0:T(8,128)S(1)}, f32[384,384]{1,0:T(8,128)S(1)}) custom-call(f32[3072,128]{1,0:T(8,128)S(1)} %bitcast.15, f32[1024,512]{1,0:T(8,128)} %t_ref.1), custom_call_target="tpu_custom_call" | custom-call | flops 2415919104 | bytes 3670016 | tf_op jit(solution)/shard_map/pallas_call | solution.py:239
  50.0 2.1 %collective-permute-start = (f32[768,128]{1,0:T(8,128)S(1)}, f32[768,128]{1,0:T(8,128)S(1)}, u32[]{:S(2)}, u32[]{:S(2)}) collective-permute-start(f32[768,128]{1,0:T(8,128)S(1)} %get-tuple-element.19), channel_id=1, source_target_pairs={{0,32},{32,0},{64,96},{96,64},{128,160},{160,128},{192,224},{224,1... | collective-permute-start | bytes 1179656 | tf_op jit(solution)/shard_map/ppermute | solution.py:257
  52.1 1.7 collective-permute-done
  53.7 0.8 add.3
  54.5 10.3 %all-to-all-start.2 = ((f32[8,96,128]{2,1,0:T(8,128)}), f32[8,96,128]{2,1,0:T(8,128)S(1)}, u32[]{:S(2)}, u32[]{:S(2)}) async-start(f32[8,96,128]{2,1,0:T(8,128)} %bitcast.3), calls=%async_computation.2 | async-start | bytes 786432 | tf_op jit(solution)/shard_map/all_to_all | solution.py:275
  64.9 15.0 %all-to-all-done.2.s_ref = f32[8,96,128]{2,1,0:T(8,128)S(1)} async-done(((f32[8,96,128]{2,1,0:T(8,128)}), f32[8,96,128]{2,1,0:T(8,128)S(1)}, u32[]{:S(2)}, u32[]{:S(2)}) %all-to-all-start.2) | async-done | bytes 393248 | tf_op jit(solution)/shard_map/all_to_all | solution.py:275
  79.9 1.9 %collective-permute-start.1 = (f32[48,128]{1,0:T(8,128)S(1)}, f32[48,128]{1,0:T(8,128)S(1)}, u32[]{:S(2)}, u32[]{:S(2)}) collective-permute-start(f32[48,128]{1,0:T(8,128)S(1)} %get-tuple-element.20), channel_id=1, source_target_pairs={{0,0},{1,9},{2,34},{3,43},{4,68},{5,77},{6,102},{7,111},{8,136},{9... | collective-permute-start | bytes 73736 | tf_op jit(solution)/shard_map/ppermute | solution.py:280
  81.8 1.9 %collective-permute-start.2 = (f32[48,128]{1,0:T(8,128)S(1)}, f32[48,128]{1,0:T(8,128)S(1)}, u32[]{:S(2)}, u32[]{:S(2)}) collective-permute-start(f32[48,128]{1,0:T(8,128)S(1)} %get-tuple-element.21), channel_id=1, source_target_pairs={{0,8},{1,1},{2,42},{3,35},{4,76},{5,69},{6,110},{7,103},{8,144},{9... | collective-permute-start | bytes 73736 | tf_op jit(solution)/shard_map/ppermute | solution.py:281
  83.7 4.0 %shard_map.39 = (f32[1920,128]{1,0:T(8,128)S(1)}, f32[1536,128]{1,0:T(8,128)S(1)}) custom-call(f32[384,384]{1,0:T(8,128)S(1)} %get-tuple-element.23.top_ref), custom_call_target="tpu_custom_call" | custom-call | flops 1509949440 | bytes 589824 | tf_op jit(solution)/shard_map/pallas_call | solution.py:239
  87.8 1.1 collective-permute-done.1.ra_ref
  88.8 1.4 shard_map.40
  91.0 11.5 %all-to-all-start.3 = ((f32[8,96,128]{2,1,0:T(8,128)}), f32[8,96,128]{2,1,0:T(8,128)S(1)}, u32[]{:S(2)}, u32[]{:S(2)}) async-start(f32[8,96,128]{2,1,0:T(8,128)} %broadcast_in_dim.37), calls=%async_computation.3 | async-start | bytes 786432 | tf_op jit(solution)/shard_map/all_to_all | solution.py:253
  102.5 1.9 %collective-permute-start.6 = (f32[96,128]{1,0:T(8,128)S(1)}, f32[96,128]{1,0:T(8,128)S(1)}, u32[]{:S(2)}, u32[]{:S(2)}) collective-permute-start(f32[96,128]{1,0:T(8,128)S(1)} %get-tuple-element.26.mine_ref), channel_id=1, source_target_pairs={{0,32},{32,0},{64,96},{96,64},{128,160},{160,128},{192,224},{224,1... | collective-permute-start | bytes 147464 | tf_op jit(solution)/shard_map/ppermute | solution.py:257
  104.4 12.0 %all-to-all-done.3 = f32[8,96,128]{2,1,0:T(8,128)S(1)} async-done(((f32[8,96,128]{2,1,0:T(8,128)}), f32[8,96,128]{2,1,0:T(8,128)S(1)}, u32[]{:S(2)}, u32[]{:S(2)}) %all-to-all-start.3) | async-done | bytes 393248 | tf_op jit(solution)/shard_map/all_to_all | solution.py:253
  116.4 1.9 %collective-permute-start.3 = (f32[768,128]{1,0:T(8,128)S(1)}, f32[768,128]{1,0:T(8,128)S(1)}, u32[]{:S(2)}, u32[]{:S(2)}) collective-permute-start(f32[768,128]{1,0:T(8,128)S(1)} %bitcast.9), channel_id=1, source_target_pairs={{8,0},{9,1},{10,2},{11,3},{12,4},{13,5},{14,6},{15,7},{16,8},{17,9... | collective-permute-start | bytes 1179656 | tf_op jit(solution)/shard_map/ppermute | solution.py:262
  118.3 5.4 %collective-permute-start.4 = (f32[768,128]{1,0:T(8,128)S(1)}, f32[768,128]{1,0:T(8,128)S(1)}, u32[]{:S(2)}, u32[]{:S(2)}) collective-permute-start(f32[768,128]{1,0:T(8,128)S(1)} %bitcast.10), channel_id=1, source_target_pairs={{16,0},{17,1},{18,2},{19,3},{20,4},{21,5},{22,6},{23,7},{24,8},{25... | collective-permute-start | bytes 1179656 | tf_op jit(solution)/shard_map/ppermute | solution.py:262
  123.7 3.2 %collective-permute-start.5 = (f32[768,128]{1,0:T(8,128)S(1)}, f32[768,128]{1,0:T(8,128)S(1)}, u32[]{:S(2)}, u32[]{:S(2)}) collective-permute-start(f32[768,128]{1,0:T(8,128)S(1)} %bitcast.11), channel_id=1, source_target_pairs={{24,0},{25,1},{26,2},{27,3},{28,4},{29,5},{30,6},{31,7},{0,8},{1,9... | collective-permute-start | bytes 1179656 | tf_op jit(solution)/shard_map/ppermute | solution.py:262
  126.9 15.9 %all_to_all.37.got_ref = f32[8,48,128]{2,1,0:T(8,128)S(1)} all-to-all(f32[8,48,128]{2,1,0:T(8,128)S(1)} %get-tuple-element.28), channel_id=1, replica_groups={{0,64,128,192,256,320,384,448},{32,96,160,224,288,352,416,480},{1,65,12..., dimensions={0} | all-to-all | bytes 393216 | tf_op jit(solution)/shard_map/all_to_all | solution.py:295
  142.8 12.2 %all_to_all.38 = f32[8,48,128]{2,1,0:T(8,128)S(1)} all-to-all(f32[8,48,128]{2,1,0:T(8,128)S(1)} %broadcast_in_dim.38), channel_id=1, replica_groups={{0,1,2,3,4,5,6,7},{8,9,10,11,12,13,14,15},{16,17,18,19,20,21,22,23},{24..., dimensions={0} | all-to-all | bytes 393216 | tf_op jit(solution)/shard_map/all_to_all | solution.py:253
  155.1 13.8 %all_to_all.39 = f32[4,384,128]{2,1,0:T(8,128)S(1)} all-to-all(f32[4,384,128]{2,1,0:T(8,128)S(1)} %broadcast_in_dim.40), channel_id=1, replica_groups={{0,8,16,24},{1,9,17,25},{2,10,18,26},{3,11,19,27},{4,12,20,28},{5,13,21..., dimensions={0} | all-to-all | bytes 1572864 | tf_op jit(solution)/shard_map/all_to_all | solution.py:253
  168.9 6.2 %shard_map.43 = f32[12,1024]{1,0:T(8,128)} custom-call(f32[768,128]{1,0:T(8,128)S(1)} %bitcast.13, f32[768,128]{1,0:T(8,128)S(1)} %collective-permute-done.3.rest_0_.y1_ref, f32[768,128]{1,0:T(8,128)S(1)} %collective-permute-done.4.rest_1_.y2_ref, f32[768,128]{1,0:T(8,128)S(1)} %collective-permute-done.5.rest_2_.y3_ref, ...), custom_call_target="tpu_custom_call" | custom-call | flops 56623104 | bytes 3563520 | tf_op jit(solution)/shard_map/pallas_call | solution.py:239
  (16 shorter events, 1.1 us)
Async XLA Ops:
  50.0 14.9 %copy-start = (f32[1024,12]{0,1:T(8,128)S(1)}, f32[1024,12]{0,1:T(8,128)}, u32[]{:S(2)}) copy-start(f32[1024,12]{0,1:T(8,128)} %param.5) | copy-start | bytes 147460
  50.0 3.7 %collective-permute-start = (f32[768,128]{1,0:T(8,128)S(1)}, f32[768,128]{1,0:T(8,128)S(1)}, u32[]{:S(2)}, u32[]{:S(2)}) collective-permute-start(f32[768,128]{1,0:T(8,128)S(1)} %get-tuple-element.19), channel_id=1, source_target_pairs={{0,32},{32,0},{64,96},{96,64},{128,160},{160,128},{192,224},{224,1... | collective-permute-start | bytes 1179656 | tf_op jit(solution)/shard_map/ppermute | solution.py:257
  54.5 25.3 %all-to-all-start.2 = ((f32[8,96,128]{2,1,0:T(8,128)}), f32[8,96,128]{2,1,0:T(8,128)S(1)}, u32[]{:S(2)}, u32[]{:S(2)}) async-start(f32[8,96,128]{2,1,0:T(8,128)} %bitcast.3), calls=%async_computation.2 | async-start | bytes 786432 | tf_op jit(solution)/shard_map/all_to_all | solution.py:275
  79.9 9.0 %collective-permute-start.1 = (f32[48,128]{1,0:T(8,128)S(1)}, f32[48,128]{1,0:T(8,128)S(1)}, u32[]{:S(2)}, u32[]{:S(2)}) collective-permute-start(f32[48,128]{1,0:T(8,128)S(1)} %get-tuple-element.20), channel_id=1, source_target_pairs={{0,0},{1,9},{2,34},{3,43},{4,68},{5,77},{6,102},{7,111},{8,136},{9... | collective-permute-start | bytes 73736 | tf_op jit(solution)/shard_map/ppermute | solution.py:280
  81.8 7.0 %collective-permute-start.2 = (f32[48,128]{1,0:T(8,128)S(1)}, f32[48,128]{1,0:T(8,128)S(1)}, u32[]{:S(2)}, u32[]{:S(2)}) collective-permute-start(f32[48,128]{1,0:T(8,128)S(1)} %get-tuple-element.21), channel_id=1, source_target_pairs={{0,8},{1,1},{2,42},{3,35},{4,76},{5,69},{6,110},{7,103},{8,144},{9... | collective-permute-start | bytes 73736 | tf_op jit(solution)/shard_map/ppermute | solution.py:281
  91.0 25.4 %all-to-all-start.3 = ((f32[8,96,128]{2,1,0:T(8,128)}), f32[8,96,128]{2,1,0:T(8,128)S(1)}, u32[]{:S(2)}, u32[]{:S(2)}) async-start(f32[8,96,128]{2,1,0:T(8,128)} %broadcast_in_dim.37), calls=%async_computation.3 | async-start | bytes 786432 | tf_op jit(solution)/shard_map/all_to_all | solution.py:253
  102.5 24.4 %collective-permute-start.6 = (f32[96,128]{1,0:T(8,128)S(1)}, f32[96,128]{1,0:T(8,128)S(1)}, u32[]{:S(2)}, u32[]{:S(2)}) collective-permute-start(f32[96,128]{1,0:T(8,128)S(1)} %get-tuple-element.26.mine_ref), channel_id=1, source_target_pairs={{0,32},{32,0},{64,96},{96,64},{128,160},{160,128},{192,224},{224,1... | collective-permute-start | bytes 147464 | tf_op jit(solution)/shard_map/ppermute | solution.py:257
  116.4 26.4 %collective-permute-start.3 = (f32[768,128]{1,0:T(8,128)S(1)}, f32[768,128]{1,0:T(8,128)S(1)}, u32[]{:S(2)}, u32[]{:S(2)}) collective-permute-start(f32[768,128]{1,0:T(8,128)S(1)} %bitcast.9), channel_id=1, source_target_pairs={{8,0},{9,1},{10,2},{11,3},{12,4},{13,5},{14,6},{15,7},{16,8},{17,9... | collective-permute-start | bytes 1179656 | tf_op jit(solution)/shard_map/ppermute | solution.py:262
  118.3 24.5 %collective-permute-start.4 = (f32[768,128]{1,0:T(8,128)S(1)}, f32[768,128]{1,0:T(8,128)S(1)}, u32[]{:S(2)}, u32[]{:S(2)}) collective-permute-start(f32[768,128]{1,0:T(8,128)S(1)} %bitcast.10), channel_id=1, source_target_pairs={{16,0},{17,1},{18,2},{19,3},{20,4},{21,5},{22,6},{23,7},{24,8},{25... | collective-permute-start | bytes 1179656 | tf_op jit(solution)/shard_map/ppermute | solution.py:262
  123.7 19.1 %collective-permute-start.5 = (f32[768,128]{1,0:T(8,128)S(1)}, f32[768,128]{1,0:T(8,128)S(1)}, u32[]{:S(2)}, u32[]{:S(2)}) collective-permute-start(f32[768,128]{1,0:T(8,128)S(1)} %bitcast.11), channel_id=1, source_target_pairs={{24,0},{25,1},{26,2},{27,3},{28,4},{29,5},{30,6},{31,7},{0,8},{1,9... | collective-permute-start | bytes 1179656 | tf_op jit(solution)/shard_map/ppermute | solution.py:262

commit v3 on v2

--- a/solution.py
+++ b/solution.py
@@ -34,7 +34,7 @@
     return col // 2 * (X_SIZE * Y_SIZE) + x_to * Y_SIZE + y_to
 
 
-def product_kernel(f_ref, t_ref, send_ref, keep_ref, ft_ref, top_ref, acc_ref, cut_ref, pick_ref):
+def product_kernel(f_ref, t_ref, send_ref, keep_ref, ft_ref, top_ref, acc_ref, cut_ref):
     row, col = lax.axis_index("row"), lax.axis_index("col")
     x, y = col // Y_SIZE, col % Y_SIZE
     panel = lax.broadcasted_iota(jnp.int32, (PW, B), 0) // B
@@ -44,16 +44,14 @@
             top_ref[:, b * B : (b + 1) * B] = part
             part = jnp.where((row > 0) | (panel < b), part, 0.0)
         ft_ref[:, b * B : (b + 1) * B] = part
+    acc_ref[...] = dot(ft_ref[...], t_ref[...])
+    for b in range(4):
+        cut_ref[pl.ds(b, PW, stride=4), :] = acc_ref[:, b * B : (b + 1) * B]
     for core, target in ((1 - row % 2, send_ref), (row % 2, keep_ref)):
-        for half in range(2):
-            first = pl.multiple_of((x + 2 * core + half) % X_SIZE * 96, 8)
-            pick_ref[half * 96 : (half + 1) * 96, :] = ft_ref[pl.ds(first, 96), :]
-        acc_ref[...] = dot(pick_ref[...], t_ref[...])
-        for b in range(4):
-            cut_ref[pl.ds(b, PW // 2, stride=4), :] = acc_ref[:, b * B : (b + 1) * B]
         for z in range(8):
             for half in range(2):
-                first = pl.multiple_of(half * 384 + (y + z) % Y_SIZE * 48, 16)
+                x_to, y_to = (x + 2 * core + half) % X_SIZE, (y + z) % Y_SIZE
+                first = pl.multiple_of((x_to * Y_SIZE + y_to) * 48, 16)
                 target[z * 96 + half * 48 : z * 96 + half * 48 + 48, :] = cut_ref[pl.ds(first, 48), :]
 
 
@@ -120,7 +118,8 @@
     for b in range(8):
         g = g_ref[pl.ds(b, 12, stride=8), :]
         y = g - 2.0 * half_ref[pl.ds(b // 4 * 48 + b % 4, 12, stride=4), :]
-        y_ref[pl.ds(b, 12, stride=8), :] = y
+        y_ref[b, 0:12, :] = y
+        y_ref[b, 12:16, :] = jnp.zeros((4, B), jnp.float32)
         if b < STEPS:
             top.append(y)
             diag = jnp.where(panel == b, g, diag)
@@ -137,25 +136,14 @@
     pay_ref[48:96, :] = jnp.where(row == 0, own, 0.0)
 
 
-def tail_kernel(
-    y0_ref, y1_ref, y2_ref, y3_ref, mine_ref, got_ref, w_ref, fac_ref,
-    out_ref, yt_ref, own_ref, lit_ref, u_ref, vt_ref, wp_ref, cut_ref,
-):
-    row = lax.axis_index("row")
-    x = lax.axis_index("col") // Y_SIZE
-    for step, y_ref in enumerate((y0_ref, y1_ref, y2_ref, y3_ref)):
-        first = pl.multiple_of((x + step) % X_SIZE * 96, 8)
-        for b in range(8):
-            yt_ref[pl.ds(first, 96), b * B : (b + 1) * B] = y_ref[pl.ds(b, 96, stride=8), :]
-    own_ref[...] = jnp.where(row < 2, mine_ref[...], got_ref[0])
-    for k in range(STEPS):
-        lit_ref[:, k * B : (k + 1) * B] = own_ref[pl.ds(k, 12, stride=4), :]
-    out_ref[...] = 0.5 * dot(lit_ref[...], yt_ref[...])
-
-    @pl.when(row == 0)
+def corner_kernel(w_ref, fac_ref, out_ref, u_ref, vt_ref, wp_ref, cut_ref):
+    @pl.when(lax.axis_index("row") == 0)
     def _():
-        for k in range(4):
-            u_ref[:, k * B : (k + 1) * B] = w_ref[pl.ds(k, PW, stride=4), :]
+        for x in range(X_SIZE):
+            for k in range(4):
+                u_ref[96 * x : 96 * (x + 1), k * B : (k + 1) * B] = w_ref[
+                    pl.ds(480 * x + k, 96, stride=4), :
+                ]
         rows = lax.broadcasted_iota(jnp.int32, (B, B), 0)
         cols = lax.broadcasted_iota(jnp.int32, (B, B), 1)
 
@@ -209,7 +197,7 @@
             out_ref[:, k * B : (k + 1) * B] = cut_ref[pl.ds(k, 12, stride=4), :]
 
 
-def route_kernel(mine_ref, other_ref, _, out_ref, sum_ref, own_ref):
+def route_kernel(mine_ref, other_ref, out_ref, sum_ref, own_ref):
     mine, other = mine_ref[...], other_ref[...]
     corner = mine[0:48] + other[0:48]
     inverse = mine[48:96] + other[48:96]
@@ -220,8 +208,43 @@
         out_ref[z] = inverse
 
 
-def corner_sum_kernel(mine_ref, got_ref, *rest):
-    rest[-1][...] = mine_ref[...] + jnp.sum(got_ref[1:], axis=0)
+def pack_y_kernel(sum_ref, own_ref, got_ref, y_ref, out_ref):
+    corner = sum_ref[...] + jnp.sum(got_ref[1:], axis=0)
+    inverse = jnp.where(lax.axis_index("row") < 2, own_ref[...], got_ref[0])
+    for y in range(Y_SIZE):
+        out_ref[y, 0:48, :] = corner
+        out_ref[y, 48:96, :] = inverse
+        out_ref[y, 96:112, :] = y_ref[y]
+
+
+def pack_x_kernel(near_ref, out_ref):
+    for x in range(X_SIZE):
+        for y in range(Y_SIZE):
+            out_ref[x, 48 * y : 48 * (y + 1), :] = near_ref[y, 0:48, :]
+            out_ref[x, 384 + 12 * y : 384 + 12 * (y + 1), :] = near_ref[y, 96:108, :]
+
+
+def solve_kernel(near_ref, w_ref, out_ref, yt_ref, lit_ref):
+    for x in range(X_SIZE):
+        yt_ref[96 * x : 96 * (x + 1), :] = w_ref[480 * x + 384 : 480 * (x + 1), :]
+    for y in range(Y_SIZE):
+        for k in range(STEPS):
+            lit_ref[12 * y : 12 * (y + 1), k * B : (k + 1) * B] = near_ref[
+                y, pl.ds(48 + k, 12, stride=4), :
+            ]
+    yt_ref[0:96, :] = 0.5 * dot(lit_ref[...], yt_ref[...])
+    for y in range(Y_SIZE):
+        out_ref[y, 0:12, :] = yt_ref[12 * y : 12 * (y + 1), :]
+        out_ref[y, 12:16, :] = jnp.zeros((4, B), jnp.float32)
+
+
+def output_kernel(x_ref, corner_ref, out_ref):
+    for b in range(8):
+        out_ref[:, b * B : (b + 1) * B] = x_ref[b, 0:12, :]
+
+    @pl.when(lax.axis_index("row") == 0)
+    def _():
+        out_ref[:, 0:PW] = corner_ref[...]
 
 
 def f32(*shape):
@@ -232,19 +255,19 @@
     return pltpu.VMEM(shape, jnp.float32)
 
 
-def call(kernel, out_shape, *args, scratch=(), flops=0, after=()):
+def call(kernel, out_shape, *args, scratch=(), flops=0):
     many = isinstance(out_shape, (list, tuple))
     spec = pl.BlockSpec(memory_space=pltpu.VMEM)
     total = sum(a.size for a in args) * 4
     return pl.pallas_call(
         kernel,
         out_shape=out_shape,
-        in_specs=[spec] * len(args) + [pl.BlockSpec(memory_space=pl.ANY)] * len(after),
+        in_specs=[spec] * len(args),
         out_specs=[spec] * len(out_shape) if many else spec,
         scratch_shapes=list(scratch),
         compiler_params=PARAMS,
         cost_estimate=pl.CostEstimate(flops=flops, bytes_accessed=total, transcendentals=0),
-    )(*args, *after)
+    )(*args)
 
 
 def spread(value, axis, groups):
@@ -255,11 +278,6 @@
 
 def between_cores(value):
     return lax.ppermute(value, "row", [(r, r ^ 1) for r in range(16)])
-
-
-def from_x(value, step):
-    pairs = [((c + step * Y_SIZE) % (X_SIZE * Y_SIZE), c) for c in range(X_SIZE * Y_SIZE)]
-    return lax.ppermute(value, "col", pairs)
 
 
 def on_device(trail_adj, factor_panels, factor_adj):
@@ -269,7 +287,7 @@
     panels = spread(near, "col", X_GROUPS).reshape(PW * 8, B)
     send, keep, ft, ft_corner = call(
         product_kernel, [f32(768, B), f32(768, B), f32(PW, 1024), f32(PW, PW)], panels, trail_adj,
-        scratch=[vmem(PW // 2, 512), vmem(768, B), vmem(PW // 2, 1024)], flops=12 * 1024 * 512 * PW,
+        scratch=[vmem(PW, 512), vmem(1536, B)], flops=12 * 1024 * 512 * PW,
     )
     both = (keep + between_cores(send)).reshape(8, 96, B)
     pieces = lax.all_to_all(both, "row", 0, 0, axis_index_groups=Z_GROUPS)
@@ -283,27 +301,27 @@
         inverse_kernel, [f32(15 * B, B), f32(1536, B)], ft_corner, flops=12 * 60 * B**3,
     )
     payload, own_y = call(
-        gram_kernel, [f32(96, B), f32(96, B)], got_a, got_b, adjoint, ft, inv_tp,
+        gram_kernel, [f32(96, B), f32(8, 16, B)], got_a, got_b, adjoint, ft, inv_tp,
         scratch=[vmem(96, B), vmem(12, 1024)], flops=12 * 12 * 1024 * PW,
     )
-    near_y = spread(own_y, "col", Y_GROUPS).reshape(Y_SIZE * 96, B)
-    all_y = [near_y] + [from_x(near_y, step) for step in range(1, X_SIZE)]
     out_u, sum_u, own = call(
         route_kernel, [f32(8, 48, B), f32(48, B), f32(48, B)], payload, between_cores(payload),
-        after=[near_y],
     )
     got = lax.all_to_all(out_u, "row", 0, 0, axis_index_groups=Z_GROUPS)
-    corner_u = call(corner_sum_kernel, f32(48, B), sum_u, got, after=all_y[1:])
-    near_u = spread(corner_u, "col", Y_GROUPS).reshape(Y_SIZE * 48, B)
-    all_u = spread(near_u, "col", X_GROUPS).reshape(PW * 4, B)
-    out = call(
-        tail_kernel, f32(12, 1024), *all_y, own, got, all_u, fac,
-        scratch=[
-            vmem(PW, 1024), vmem(48, B), vmem(12, PW), vmem(PW, 512), vmem(PW, PW), vmem(1536, B),
-            vmem(48, B),
-        ],
-        flops=12 * 12 * 1024 * PW,
-    )
+    near = call(pack_y_kernel, f32(8, 112, B), sum_u, own, got, own_y)
+    near = lax.all_to_all(near, "col", 0, 0, axis_index_groups=Y_GROUPS)
+    wide = call(pack_x_kernel, f32(4, 480, B), near)
+    wide = lax.all_to_all(wide, "col", 0, 0, axis_index_groups=X_GROUPS).reshape(4 * 480, B)
+    solved = call(
+        solve_kernel, f32(8, 16, B), near, wide,
+        scratch=[vmem(PW, B), vmem(96, PW)], flops=12 * 96 * B * PW,
+    )
+    rows_x = lax.all_to_all(solved, "col", 0, 0, axis_index_groups=Y_GROUPS)
+    corner = call(
+        corner_kernel, f32(12, PW), wide, fac,
+        scratch=[vmem(PW, 512), vmem(PW, PW), vmem(1536, B), vmem(48, B)], flops=12 * 60 * B**3,
+    )
+    out = call(output_kernel, f32(12, 1024), rows_x, corner)
     return out.T
 
 

time: 176 us -> 165 us (0.938)
  the two profiles are of different devices: /device:TPU:2 before, /device:TPU:1 now
where the time goes in v3:
time: 165 us; the launch traced here: 163 us
  blocking collectives  91.1 us (55%)
  waiting for transfers between devices  32.3 us (20%)
  starting transfers between devices  29.6 us (18%)
  Pallas kernels  7.5 us (5%)
  local copies, waits for them, and re-layouts  2.06 us (1%)
    all_to_all x2, blocking collectives, spread(): return lax.all_to_all(copies, axis, 0, 0, axis_index_groups=groups)  43.1 us
    all_to_all x1, blocking collectives, on_device(): near = lax.all_to_all(near, 'col', 0, 0, axis_index_groups=Y_GROUPS)  17.9 us
    all_to_all x1, blocking collectives, on_device(): got = lax.all_to_all(out_u, 'row', 0, 0, axis_index_groups=Z_GROUPS)  17.5 us
    all_to_all x1, waiting for transfers between devices, on_device(): pieces = lax.all_to_all(both, 'row', 0, 0, axis_index_groups=Z_GROUPS)  15.1 us
    all_to_all x1, blocking collectives, on_device(): lax.all_to_all(wide, 'col', 0, 0, axis_index_groups=X_GROUPS)  12.6 us
    all_to_all x1, starting transfers between devices, on_device(): pieces = lax.all_to_all(both, 'row', 0, 0, axis_index_groups=Z_GROUPS)  10 us
    pallas_call x10, Pallas kernels, call(): pl.pallas_call(kernel, out_shape=out_shape, in_specs=[spec] * len(args),...  7.5 us
    all_to_all x1, waiting for transfers between devices, on_device(): rows_x = lax.all_to_all(solved, 'col', 0, 0, axis_index_groups=Y_GROUPS)  7.32 us
  transfers between devices with their start and end apart: 6, of which 6 were waited for; matrix products, arithmetic and copies ran while one was open for 0% of the time, Pallas kernels for 0%

profile of v3, /device:TPU:1, one launch (start us, length us, event | category | flops | bytes accessed | tf_op | source)
XLA Modules:
  0.0 163.4 jit_solution(12391537370731285187)
XLA Ops:
  0.0 0.9 broadcast_in_dim.14
  0.9 19.8 %all_to_all.35 = f32[8,96,128]{2,1,0:T(8,128)S(1)} all-to-all(f32[8,96,128]{2,1,0:T(8,128)S(1)} %broadcast_in_dim.15), channel_id=1, replica_groups={{0,1,2,3,4,5,6,7},{8,9,10,11,12,13,14,15},{16,17,18,19,20,21,22,23},{24..., dimensions={0} | all-to-all | bytes 786432 | tf_op jit(solution)/shard_map/all_to_all | solution.py:276
  20.8 23.3 %all_to_all.36 = f32[4,768,128]{2,1,0:T(8,128)S(1)} all-to-all(f32[4,768,128]{2,1,0:T(8,128)S(1)} %broadcast_in_dim.17), channel_id=1, replica_groups={{0,8,16,24},{1,9,17,25},{2,10,18,26},{3,11,19,27},{4,12,20,28},{5,13,21..., dimensions={0} | all-to-all | bytes 3145728 | tf_op jit(solution)/shard_map/all_to_all | solution.py:276
  44.1 4.4 %shard_map.37 = (f32[768,128]{1,0:T(8,128)S(1)}, f32[768,128]{1,0:T(8,128)S(1)}, f32[384,1024]{1,0:T(8,128)S(1)}, f32[384,384]{1,0:T(8,128)S(1)}) custom-call(f32[3072,128]{1,0:T(8,128)S(1)} %bitcast.9, f32[1024,512]{1,0:T(8,128)} %t_ref.1), custom_call_target="tpu_custom_call" | custom-call | flops 2415919104 | bytes 3670016 | tf_op jit(solution)/shard_map/pallas_call | solution.py:262
  48.6 5.4 %collective-permute-start = (f32[768,128]{1,0:T(8,128)S(1)}, f32[768,128]{1,0:T(8,128)S(1)}, u32[]{:S(2)}, u32[]{:S(2)}) collective-permute-start(f32[768,128]{1,0:T(8,128)S(1)} %get-tuple-element.19), channel_id=1, source_target_pairs={{0,32},{32,0},{64,96},{96,64},{128,160},{160,128},{192,224},{224,1... | collective-permute-start | bytes 1179656 | tf_op jit(solution)/shard_map/ppermute | solution.py:280
  53.9 1.3 collective-permute-done
  55.3 0.8 add.3
  56.0 10.0 %all-to-all-start.2 = ((f32[8,96,128]{2,1,0:T(8,128)}), f32[8,96,128]{2,1,0:T(8,128)S(1)}, u32[]{:S(2)}, u32[]{:S(2)}) async-start(f32[8,96,128]{2,1,0:T(8,128)} %bitcast.3), calls=%async_computation.2 | async-start | bytes 786432 | tf_op jit(solution)/shard_map/all_to_all | solution.py:293
  66.1 15.1 %all-to-all-done.2.s_ref = f32[8,96,128]{2,1,0:T(8,128)S(1)} async-done(((f32[8,96,128]{2,1,0:T(8,128)}), f32[8,96,128]{2,1,0:T(8,128)S(1)}, u32[]{:S(2)}, u32[]{:S(2)}) %all-to-all-start.2) | async-done | bytes 393248 | tf_op jit(solution)/shard_map/all_to_all | solution.py:293
  81.3 2.8 %collective-permute-start.1 = (f32[48,128]{1,0:T(8,128)S(1)}, f32[48,128]{1,0:T(8,128)S(1)}, u32[]{:S(2)}, u32[]{:S(2)}) collective-permute-start(f32[48,128]{1,0:T(8,128)S(1)} %get-tuple-element.20), channel_id=1, source_target_pairs={{0,0},{1,9},{2,34},{3,43},{4,68},{5,77},{6,102},{7,111},{8,136},{9... | collective-permute-start | bytes 73736 | tf_op jit(solution)/shard_map/ppermute | solution.py:298
  84.1 2.6 %collective-permute-start.2 = (f32[48,128]{1,0:T(8,128)S(1)}, f32[48,128]{1,0:T(8,128)S(1)}, u32[]{:S(2)}, u32[]{:S(2)}) collective-permute-start(f32[48,128]{1,0:T(8,128)S(1)} %get-tuple-element.21), channel_id=1, source_target_pairs={{0,8},{1,1},{2,42},{3,35},{4,76},{5,69},{6,110},{7,103},{8,144},{9... | collective-permute-start | bytes 73736 | tf_op jit(solution)/shard_map/ppermute | solution.py:299
  86.7 1.1 copy-done.1
  87.8 2.6 %collective-permute-done.1.ra_ref = f32[48,128]{1,0:T(8,128)S(1)} collective-permute-done((f32[48,128]{1,0:T(8,128)S(1)}, f32[48,128]{1,0:T(8,128)S(1)}, u32[]{:S(2)}, u32[]{:S(2)}) %collective-permute-start.1) | collective-permute-done | bytes 24608 | tf_op jit(solution)/shard_map/ppermute | solution.py:298
  90.4 4.7 %collective-permute-done.2.rb_ref = f32[48,128]{1,0:T(8,128)S(1)} collective-permute-done((f32[48,128]{1,0:T(8,128)S(1)}, f32[48,128]{1,0:T(8,128)S(1)}, u32[]{:S(2)}, u32[]{:S(2)}) %collective-permute-start.2) | collective-permute-done | bytes 24608 | tf_op jit(solution)/shard_map/ppermute | solution.py:299
  95.1 1.4 shard_map.40
  96.5 1.9 %collective-permute-start.3 = (f32[96,128]{1,0:T(8,128)S(1)}, f32[96,128]{1,0:T(8,128)S(1)}, u32[]{:S(2)}, u32[]{:S(2)}) collective-permute-start(f32[96,128]{1,0:T(8,128)S(1)} %get-tuple-element.25.mine_ref), channel_id=1, source_target_pairs={{0,32},{32,0},{64,96},{96,64},{128,160},{160,128},{192,224},{224,1... | collective-permute-start | bytes 147464 | tf_op jit(solution)/shard_map/ppermute | solution.py:280
  98.4 1.2 collective-permute-done.3.other_ref
  99.6 17.5 %all_to_all.37.got_ref = f32[8,48,128]{2,1,0:T(8,128)S(1)} all-to-all(f32[8,48,128]{2,1,0:T(8,128)S(1)} %get-tuple-element.28), channel_id=1, replica_groups={{0,64,128,192,256,320,384,448},{32,96,160,224,288,352,416,480},{1,65,12..., dimensions={0} | all-to-all | bytes 393216 | tf_op jit(solution)/shard_map/all_to_all | solution.py:310
  117.2 17.9 %all_to_all.38.near_ref = f32[8,112,128]{2,1,0:T(8,128)S(1)} all-to-all(f32[8,112,128]{2,1,0:T(8,128)S(1)} %shard_map.42), channel_id=1, replica_groups={{0,1,2,3,4,5,6,7},{8,9,10,11,12,13,14,15},{16,17,18,19,20,21,22,23},{24..., dimensions={0} | all-to-all | bytes 917504 | tf_op jit(solution)/shard_map/all_to_all | solution.py:312
  135.1 12.6 %all_to_all.39 = f32[4,480,128]{2,1,0:T(8,128)S(1)} all-to-all(f32[4,480,128]{2,1,0:T(8,128)S(1)} %shard_map.43), channel_id=1, replica_groups={{0,8,16,24},{1,9,17,25},{2,10,18,26},{3,11,19,27},{4,12,20,28},{5,13,21..., dimensions={0} | all-to-all | bytes 1966080 | tf_op jit(solution)/shard_map/all_to_all | solution.py:314
  147.7 0.9 shard_map.44
  148.7 6.8 %all-to-all-start.6 = ((f32[8,16,128]{2,1,0:T(8,128)}), f32[8,16,128]{2,1,0:T(8,128)S(1)}, u32[]{:S(2)}, u32[]{:S(2)}) async-start(f32[8,16,128]{2,1,0:T(8,128)} %shard_map.44), calls=%async_computation.6 | async-start | bytes 131072 | tf_op jit(solution)/shard_map/all_to_all | solution.py:319
  155.5 7.3 %all-to-all-done.6.x_ref = f32[8,16,128]{2,1,0:T(8,128)S(1)} async-done(((f32[8,16,128]{2,1,0:T(8,128)}), f32[8,16,128]{2,1,0:T(8,128)S(1)}, u32[]{:S(2)}, u32[]{:S(2)}) %all-to-all-start.6) | async-done | bytes 65568 | tf_op jit(solution)/shard_map/all_to_all | solution.py:319
  162.8 0.6 shard_map.46
  (14 shorter events, 0.3 us)
Async XLA Ops:
  48.5 7.5 %copy-start = (f32[384,384]{1,0:T(8,128)}, f32[384,384]{1,0:T(8,128)S(1)}, u32[]{:S(2)}) copy-start(f32[384,384]{1,0:T(8,128)S(1)} %get-tuple-element.23.top_ref) | copy-start | bytes 1769476
  48.5 17.5 %copy-start.2 = (f32[1024,12]{0,1:T(8,128)S(1)}, f32[1024,12]{0,1:T(8,128)}, u32[]{:S(2)}) copy-start(f32[1024,12]{0,1:T(8,128)} %param.5) | copy-start | bytes 147460
  48.6 6.7 %collective-permute-start = (f32[768,128]{1,0:T(8,128)S(1)}, f32[768,128]{1,0:T(8,128)S(1)}, u32[]{:S(2)}, u32[]{:S(2)}) collective-permute-start(f32[768,128]{1,0:T(8,128)S(1)} %get-tuple-element.19), channel_id=1, source_target_pairs={{0,32},{32,0},{64,96},{96,64},{128,160},{160,128},{192,224},{224,1... | collective-permute-start | bytes 1179656 | tf_op jit(solution)/shard_map/ppermute | solution.py:280
  56.0 25.2 %all-to-all-start.2 = ((f32[8,96,128]{2,1,0:T(8,128)}), f32[8,96,128]{2,1,0:T(8,128)S(1)}, u32[]{:S(2)}, u32[]{:S(2)}) async-start(f32[8,96,128]{2,1,0:T(8,128)} %bitcast.3), calls=%async_computation.2 | async-start | bytes 786432 | tf_op jit(solution)/shard_map/all_to_all | solution.py:293
  81.3 9.1 %collective-permute-start.1 = (f32[48,128]{1,0:T(8,128)S(1)}, f32[48,128]{1,0:T(8,128)S(1)}, u32[]{:S(2)}, u32[]{:S(2)}) collective-permute-start(f32[48,128]{1,0:T(8,128)S(1)} %get-tuple-element.20), channel_id=1, source_target_pairs={{0,0},{1,9},{2,34},{3,43},{4,68},{5,77},{6,102},{7,111},{8,136},{9... | collective-permute-start | bytes 73736 | tf_op jit(solution)/shard_map/ppermute | solution.py:298
  84.1 11.0 %collective-permute-start.2 = (f32[48,128]{1,0:T(8,128)S(1)}, f32[48,128]{1,0:T(8,128)S(1)}, u32[]{:S(2)}, u32[]{:S(2)}) collective-permute-start(f32[48,128]{1,0:T(8,128)S(1)} %get-tuple-element.21), channel_id=1, source_target_pairs={{0,8},{1,1},{2,42},{3,35},{4,76},{5,69},{6,110},{7,103},{8,144},{9... | collective-permute-start | bytes 73736 | tf_op jit(solution)/shard_map/ppermute | solution.py:299
  86.7 1.1 copy-start.1
  96.5 3.1 %collective-permute-start.3 = (f32[96,128]{1,0:T(8,128)S(1)}, f32[96,128]{1,0:T(8,128)S(1)}, u32[]{:S(2)}, u32[]{:S(2)}) collective-permute-start(f32[96,128]{1,0:T(8,128)S(1)} %get-tuple-element.25.mine_ref), channel_id=1, source_target_pairs={{0,32},{32,0},{64,96},{96,64},{128,160},{160,128},{192,224},{224,1... | collective-permute-start | bytes 147464 | tf_op jit(solution)/shard_map/ppermute | solution.py:280
  148.7 14.2 %all-to-all-start.6 = ((f32[8,16,128]{2,1,0:T(8,128)}), f32[8,16,128]{2,1,0:T(8,128)S(1)}, u32[]{:S(2)}, u32[]{:S(2)}) async-start(f32[8,16,128]{2,1,0:T(8,128)} %shard_map.44), calls=%async_computation.6 | async-start | bytes 131072 | tf_op jit(solution)/shard_map/all_to_all | solution.py:319

commit v4 on v3

--- a/solution.py
+++ b/solution.py
@@ -22,6 +22,10 @@
     return jnp.dot(a, b, precision=HI, preferred_element_type=jnp.float32)
 
 
+def dot_bf16(a, b):
+    return jnp.dot(a, b, preferred_element_type=jnp.float32)
+
+
 def dot_nt(a, b):
     return lax.dot_general(
         a, b, (((1,), (1,)), ((), ())), precision=HI, preferred_element_type=jnp.float32
@@ -32,6 +36,11 @@
     x, y = col // Y_SIZE, col % Y_SIZE
     x_to, y_to = (x + 2 * (row % 2) + half) % X_SIZE, (y + row // 2) % Y_SIZE
     return col // 2 * (X_SIZE * Y_SIZE) + x_to * Y_SIZE + y_to
+
+
+def split(value):
+    high = value.astype(jnp.bfloat16)
+    return high, (value - high.astype(jnp.float32)).astype(jnp.bfloat16)
 
 
 def product_kernel(f_ref, t_ref, send_ref, keep_ref, ft_ref, top_ref, acc_ref, cut_ref):
@@ -44,7 +53,9 @@
             top_ref[:, b * B : (b + 1) * B] = part
             part = jnp.where((row > 0) | (panel < b), part, 0.0)
         ft_ref[:, b * B : (b + 1) * B] = part
-    acc_ref[...] = dot(ft_ref[...], t_ref[...])
+    fh, fl = split(ft_ref[...])
+    th, tl = split(t_ref[...])
+    acc_ref[...] = dot_bf16(fh, tl) + dot_bf16(fl, th) + dot_bf16(fh, th)
     for b in range(4):
         cut_ref[pl.ds(b, PW, stride=4), :] = acc_ref[:, b * B : (b + 1) * B]
     for core, target in ((1 - row % 2, send_ref), (row % 2, keep_ref)):
@@ -116,7 +127,7 @@
     panel = (12 * col + lax.broadcasted_iota(jnp.int32, (12, B), 0)) // B
     top, diag = [], jnp.zeros((12, B), jnp.float32)
     for b in range(8):
-        g = g_ref[pl.ds(b, 12, stride=8), :]
+        g = g_ref[:, b * B : (b + 1) * B]
         y = g - 2.0 * half_ref[pl.ds(b // 4 * 48 + b % 4, 12, stride=4), :]
         y_ref[b, 0:12, :] = y
         y_ref[b, 12:16, :] = jnp.zeros((4, B), jnp.float32)
@@ -128,21 +139,22 @@
     gram = dot_nt(ym_ref[...], ft_ref[...])
     for k in range(STEPS):
         below = jnp.where(row == 0, top[k], 0.0)
-        pay_ref[pl.ds(k, 12, stride=4), :] = jnp.where(
+        pay_ref[pl.ds(24 * (k // 2) + k % 2, 12, stride=2), :] = jnp.where(
             panel >= k, gram[:, k * B : (k + 1) * B], below
         )
-    pay_ref[pl.ds(3, 12, stride=4), :] = jnp.where(row == 0, diag, 0.0)
+    pay_ref[pl.ds(25, 12, stride=2), :] = jnp.where(row == 0, diag, 0.0)
     own = litp_ref[pl.ds(pl.multiple_of(48 * col, 16), 48), :]
     pay_ref[48:96, :] = jnp.where(row == 0, own, 0.0)
 
 
-def corner_kernel(w_ref, fac_ref, out_ref, u_ref, vt_ref, wp_ref, cut_ref):
+def corner_kernel(w_ref, other_ref, fac_ref, out_ref, u_ref, vt_ref, wp_ref, cut_ref):
     @pl.when(lax.axis_index("row") == 0)
     def _():
         for x in range(X_SIZE):
             for k in range(4):
-                u_ref[96 * x : 96 * (x + 1), k * B : (k + 1) * B] = w_ref[
-                    pl.ds(480 * x + k, 96, stride=4), :
+                half_ref = w_ref if k < 2 else other_ref
+                u_ref[96 * x : 96 * (x + 1), k * B : (k + 1) * B] = half_ref[
+                    pl.ds(288 * x + k % 2, 96, stride=2), :
                 ]
         rows = lax.broadcasted_iota(jnp.int32, (B, B), 0)
         cols = lax.broadcasted_iota(jnp.int32, (B, B), 1)
@@ -209,28 +221,30 @@
 
 
 def pack_y_kernel(sum_ref, own_ref, got_ref, y_ref, out_ref):
+    row = lax.axis_index("row")
     corner = sum_ref[...] + jnp.sum(got_ref[1:], axis=0)
-    inverse = jnp.where(lax.axis_index("row") < 2, own_ref[...], got_ref[0])
+    corner = jnp.where(row % 2 == 0, corner[0:24], corner[24:48])
+    inverse = jnp.where(row < 2, own_ref[...], got_ref[0])
     for y in range(Y_SIZE):
-        out_ref[y, 0:48, :] = corner
-        out_ref[y, 48:96, :] = inverse
-        out_ref[y, 96:112, :] = y_ref[y]
+        out_ref[y, 0:24, :] = corner
+        out_ref[y, 24:72, :] = inverse
+        out_ref[y, 72:88, :] = y_ref[y]
 
 
 def pack_x_kernel(near_ref, out_ref):
     for x in range(X_SIZE):
         for y in range(Y_SIZE):
-            out_ref[x, 48 * y : 48 * (y + 1), :] = near_ref[y, 0:48, :]
-            out_ref[x, 384 + 12 * y : 384 + 12 * (y + 1), :] = near_ref[y, 96:108, :]
+            out_ref[x, 24 * y : 24 * (y + 1), :] = near_ref[y, 0:24, :]
+            out_ref[x, 192 + 12 * y : 192 + 12 * (y + 1), :] = near_ref[y, 72:84, :]
 
 
 def solve_kernel(near_ref, w_ref, out_ref, yt_ref, lit_ref):
     for x in range(X_SIZE):
-        yt_ref[96 * x : 96 * (x + 1), :] = w_ref[480 * x + 384 : 480 * (x + 1), :]
+        yt_ref[96 * x : 96 * (x + 1), :] = w_ref[288 * x + 192 : 288 * (x + 1), :]
     for y in range(Y_SIZE):
         for k in range(STEPS):
             lit_ref[12 * y : 12 * (y + 1), k * B : (k + 1) * B] = near_ref[
-                y, pl.ds(48 + k, 12, stride=4), :
+                y, pl.ds(24 + k, 12, stride=4), :
             ]
     yt_ref[0:96, :] = 0.5 * dot(lit_ref[...], yt_ref[...])
     for y in range(Y_SIZE):
@@ -282,7 +296,6 @@
 
 def on_device(trail_adj, factor_panels, factor_adj):
     factor = factor_panels.T.reshape(96, B)
-    adjoint = factor_adj.T.reshape(96, B)
     near = spread(factor, "col", Y_GROUPS).reshape(Y_SIZE * 96, B)
     panels = spread(near, "col", X_GROUPS).reshape(PW * 8, B)
     send, keep, ft, ft_corner = call(
@@ -301,24 +314,25 @@
         inverse_kernel, [f32(15 * B, B), f32(1536, B)], ft_corner, flops=12 * 60 * B**3,
     )
     payload, own_y = call(
-        gram_kernel, [f32(96, B), f32(8, 16, B)], got_a, got_b, adjoint, ft, inv_tp,
+        gram_kernel, [f32(96, B), f32(8, 16, B)], got_a, got_b, factor_adj.T, ft, inv_tp,
         scratch=[vmem(96, B), vmem(12, 1024)], flops=12 * 12 * 1024 * PW,
     )
     out_u, sum_u, own = call(
         route_kernel, [f32(8, 48, B), f32(48, B), f32(48, B)], payload, between_cores(payload),
     )
     got = lax.all_to_all(out_u, "row", 0, 0, axis_index_groups=Z_GROUPS)
-    near = call(pack_y_kernel, f32(8, 112, B), sum_u, own, got, own_y)
+    near = call(pack_y_kernel, f32(8, 88, B), sum_u, own, got, own_y)
     near = lax.all_to_all(near, "col", 0, 0, axis_index_groups=Y_GROUPS)
-    wide = call(pack_x_kernel, f32(4, 480, B), near)
-    wide = lax.all_to_all(wide, "col", 0, 0, axis_index_groups=X_GROUPS).reshape(4 * 480, B)
+    wide = call(pack_x_kernel, f32(4, 288, B), near)
+    wide = lax.all_to_all(wide, "col", 0, 0, axis_index_groups=X_GROUPS).reshape(4 * 288, B)
+    other = between_cores(wide)
     solved = call(
         solve_kernel, f32(8, 16, B), near, wide,
         scratch=[vmem(PW, B), vmem(96, PW)], flops=12 * 96 * B * PW,
     )
     rows_x = lax.all_to_all(solved, "col", 0, 0, axis_index_groups=Y_GROUPS)
     corner = call(
-        corner_kernel, f32(12, PW), wide, fac,
+        corner_kernel, f32(12, PW), wide, other, fac,
         scratch=[vmem(PW, 512), vmem(PW, PW), vmem(1536, B), vmem(48, B)], flops=12 * 60 * B**3,
     )
     out = call(output_kernel, f32(12, 1024), rows_x, corner)

time: 165 us -> 160 us (0.970)
  blocking collectives: 91.1 us -> 110 us
  waiting for transfers between devices: 32.3 us -> 18.6 us
  starting transfers between devices: 29.6 us -> 23.9 us
    all_to_all x0 -> x1, blocking collectives: none -> 23.7 us  [on_device(): pieces = lax.all_to_all(both, 'row', 0, 0, axis_index_groups=Z_GROUPS)]
    all_to_all x1 -> x0, waiting for transfers between devices: 15.1 us -> none  [on_device(): pieces = lax.all_to_all(both, 'row', 0, 0, axis_index_groups=Z_GROUPS)]
    all_to_all x1 -> x0, starting transfers between devices: 10 us -> none  [on_device(): pieces = lax.all_to_all(both, 'row', 0, 0, axis_index_groups=Z_GROUPS)]
    ppermute x2 -> x3, starting transfers between devices: 7.28 us -> 13.9 us  [between_cores(): return lax.ppermute(value, 'row', [(r, r ^ 1) for r in range(16)])]
    all_to_all x1, starting transfers between devices: 6.83 us -> 3.35 us  [on_device(): rows_x = lax.all_to_all(solved, 'col', 0, 0, axis_index_groups=Y_GROUPS)]
    all_to_all x1, blocking collectives: 12.6 us -> 9.67 us  [on_device(): lax.all_to_all(wide, 'col', 0, 0, axis_index_groups=X_GROUPS)]
  transfers between devices with their start and end apart: 6 -> 6, of which waited for: 6 -> 5; matrix products, arithmetic and copies ran while one was open for 0% -> 0% of each run, Pallas kernels for 0% -> 1%
where the time goes in v4:
time: 160 us
  blocking collectives  110 us (69%)
  starting transfers between devices  23.9 us (15%)
  waiting for transfers between devices  18.6 us (12%)
  Pallas kernels  6.29 us (4%)
    all_to_all x2, blocking collectives, spread(): return lax.all_to_all(copies, axis, 0, 0, axis_index_groups=groups)  43.1 us
    all_to_all x1, blocking collectives, on_device(): pieces = lax.all_to_all(both, 'row', 0, 0, axis_index_groups=Z_GROUPS)  23.7 us
    all_to_all x1, blocking collectives, on_device(): got = lax.all_to_all(out_u, 'row', 0, 0, axis_index_groups=Z_GROUPS)  17.1 us
    all_to_all x1, blocking collectives, on_device(): near = lax.all_to_all(near, 'col', 0, 0, axis_index_groups=Y_GROUPS)  16.3 us
    ppermute x3, starting transfers between devices, between_cores(): return lax.ppermute(value, 'row', [(r, r ^ 1) for r in range(16)])  13.9 us
    all_to_all x1, blocking collectives, on_device(): lax.all_to_all(wide, 'col', 0, 0, axis_index_groups=X_GROUPS)  9.67 us
    all_to_all x1, waiting for transfers between devices, on_device(): rows_x = lax.all_to_all(solved, 'col', 0, 0, axis_index_groups=Y_GROUPS)  7.24 us
    pallas_call x10, Pallas kernels, call(): pl.pallas_call(kernel, out_shape=out_shape, in_specs=[spec] * len(args),...  6.29 us
  transfers between devices with their start and end apart: 6, of which 5 were waited for; matrix products, arithmetic and copies ran while one was open for 0% of the time, Pallas kernels for 1%

profile of v4, /device:TPU:1, one launch (start us, length us, event | category | flops | bytes accessed | tf_op | source)
XLA Modules:
  0.0 159.8 jit_solution(11177654860189871729)
XLA Ops:
  0.0 0.9 broadcast_in_dim.14
  0.9 19.8 %all_to_all.35 = f32[8,96,128]{2,1,0:T(8,128)S(1)} all-to-all(f32[8,96,128]{2,1,0:T(8,128)S(1)} %broadcast_in_dim.15), channel_id=1, replica_groups={{0,1,2,3,4,5,6,7},{8,9,10,11,12,13,14,15},{16,17,18,19,20,21,22,23},{24..., dimensions={0} | all-to-all | bytes 786432 | tf_op jit(solution)/shard_map/all_to_all | solution.py:290
  20.7 0.1 broadcast_in_dim.17
  20.8 23.3 %all_to_all.36 = f32[4,768,128]{2,1,0:T(8,128)S(1)} all-to-all(f32[4,768,128]{2,1,0:T(8,128)S(1)} %broadcast_in_dim.17), channel_id=1, replica_groups={{0,8,16,24},{1,9,17,25},{2,10,18,26},{3,11,19,27},{4,12,20,28},{5,13,21..., dimensions={0} | all-to-all | bytes 3145728 | tf_op jit(solution)/shard_map/all_to_all | solution.py:290
  44.1 3.2 %shard_map.37 = (f32[768,128]{1,0:T(8,128)S(1)}, f32[768,128]{1,0:T(8,128)S(1)}, f32[384,1024]{1,0:T(8,128)S(1)}, f32[384,384]{1,0:T(8,128)S(1)}) custom-call(f32[3072,128]{1,0:T(8,128)S(1)} %bitcast.10, f32[1024,512]{1,0:T(8,128)} %t_ref.1), custom_call_target="tpu_custom_call" | custom-call | flops 2415919104 | bytes 3670016 | tf_op jit(solution)/shard_map/pallas_call | solution.py:276
  47.3 5.2 %collective-permute-start = (f32[768,128]{1,0:T(8,128)S(1)}, f32[768,128]{1,0:T(8,128)S(1)}, u32[]{:S(2)}, u32[]{:S(2)}) collective-permute-start(f32[768,128]{1,0:T(8,128)S(1)} %get-tuple-element.19), channel_id=1, source_target_pairs={{0,32},{32,0},{64,96},{96,64},{128,160},{160,128},{192,224},{224,1... | collective-permute-start | bytes 1179656 | tf_op jit(solution)/shard_map/ppermute | solution.py:294
  52.6 1.3 collective-permute-done
  53.9 23.7 %all_to_all.37.s_ref = f32[8,96,128]{2,1,0:T(8,128)S(1)} all-to-all(f32[8,96,128]{2,1,0:T(8,128)S(1)} %bitcast.12), channel_id=1, replica_groups={{0,64,128,192,256,320,384,448},{32,96,160,224,288,352,416,480},{1,65,12..., dimensions={0} | all-to-all | bytes 786432 | tf_op jit(solution)/shard_map/all_to_all | solution.py:306
  77.7 4.1 %collective-permute-start.1 = (f32[48,128]{1,0:T(8,128)S(1)}, f32[48,128]{1,0:T(8,128)S(1)}, u32[]{:S(2)}, u32[]{:S(2)}) collective-permute-start(f32[48,128]{1,0:T(8,128)S(1)} %get-tuple-element.20), channel_id=1, source_target_pairs={{0,0},{1,9},{2,34},{3,43},{4,68},{5,77},{6,102},{7,111},{8,136},{9... | collective-permute-start | bytes 73736 | tf_op jit(solution)/shard_map/ppermute | solution.py:311
  81.8 2.5 %collective-permute-start.2 = (f32[48,128]{1,0:T(8,128)S(1)}, f32[48,128]{1,0:T(8,128)S(1)}, u32[]{:S(2)}, u32[]{:S(2)}) collective-permute-start(f32[48,128]{1,0:T(8,128)S(1)} %get-tuple-element.21), channel_id=1, source_target_pairs={{0,8},{1,1},{2,42},{3,35},{4,76},{5,69},{6,110},{7,103},{8,144},{9... | collective-permute-start | bytes 73736 | tf_op jit(solution)/shard_map/ppermute | solution.py:312
  84.3 0.0 copy-start
  84.4 2.9 %collective-permute-done.1.ra_ref = f32[48,128]{1,0:T(8,128)S(1)} collective-permute-done((f32[48,128]{1,0:T(8,128)S(1)}, f32[48,128]{1,0:T(8,128)S(1)}, u32[]{:S(2)}, u32[]{:S(2)}) %collective-permute-start.1) | collective-permute-done | bytes 24608 | tf_op jit(solution)/shard_map/ppermute | solution.py:311
  87.3 5.9 %collective-permute-done.2.rb_ref = f32[48,128]{1,0:T(8,128)S(1)} collective-permute-done((f32[48,128]{1,0:T(8,128)S(1)}, f32[48,128]{1,0:T(8,128)S(1)}, u32[]{:S(2)}, u32[]{:S(2)}) %collective-permute-start.2) | collective-permute-done | bytes 24608 | tf_op jit(solution)/shard_map/ppermute | solution.py:312
  93.2 1.4 shard_map.40
  94.6 1.9 %collective-permute-start.3 = (f32[96,128]{1,0:T(8,128)S(1)}, f32[96,128]{1,0:T(8,128)S(1)}, u32[]{:S(2)}, u32[]{:S(2)}) collective-permute-start(f32[96,128]{1,0:T(8,128)S(1)} %get-tuple-element.25.mine_ref), channel_id=1, source_target_pairs={{0,32},{32,0},{64,96},{96,64},{128,160},{160,128},{192,224},{224,1... | collective-permute-start | bytes 147464 | tf_op jit(solution)/shard_map/ppermute | solution.py:294
  96.5 1.2 collective-permute-done.3.other_ref
  97.7 17.1 %all_to_all.38.got_ref = f32[8,48,128]{2,1,0:T(8,128)S(1)} all-to-all(f32[8,48,128]{2,1,0:T(8,128)S(1)} %get-tuple-element.28), channel_id=1, replica_groups={{0,64,128,192,256,320,384,448},{32,96,160,224,288,352,416,480},{1,65,12..., dimensions={0} | all-to-all | bytes 393216 | tf_op jit(solution)/shard_map/all_to_all | solution.py:323
  114.9 16.3 %all_to_all.39.near_ref = f32[8,88,128]{2,1,0:T(8,128)S(1)} all-to-all(f32[8,88,128]{2,1,0:T(8,128)S(1)} %shard_map.42), channel_id=1, replica_groups={{0,1,2,3,4,5,6,7},{8,9,10,11,12,13,14,15},{16,17,18,19,20,21,22,23},{24..., dimensions={0} | all-to-all | bytes 720896 | tf_op jit(solution)/shard_map/all_to_all | solution.py:325
  131.2 9.7 %all_to_all.40 = f32[4,288,128]{2,1,0:T(8,128)S(1)} all-to-all(f32[4,288,128]{2,1,0:T(8,128)S(1)} %shard_map.43), channel_id=1, replica_groups={{0,8,16,24},{1,9,17,25},{2,10,18,26},{3,11,19,27},{4,12,20,28},{5,13,21..., dimensions={0} | all-to-all | bytes 1179648 | tf_op jit(solution)/shard_map/all_to_all | solution.py:327
  140.9 6.7 %collective-permute-start.4 = (f32[1152,128]{1,0:T(8,128)S(1)}, f32[1152,128]{1,0:T(8,128)S(1)}, u32[]{:S(2)}, u32[]{:S(2)}) collective-permute-start(f32[1152,128]{1,0:T(8,128)S(1)} %bitcast.7), channel_id=1, source_target_pairs={{0,32},{32,0},{64,96},{96,64},{128,160},{160,128},{192,224},{224,1... | collective-permute-start | bytes 1769480 | tf_op jit(solution)/shard_map/ppermute | solution.py:294
  147.6 0.9 shard_map.44
  148.6 3.4 %all-to-all-start.6 = ((f32[8,16,128]{2,1,0:T(8,128)}), f32[8,16,128]{2,1,0:T(8,128)S(1)}, u32[]{:S(2)}, u32[]{:S(2)}) async-start(f32[8,16,128]{2,1,0:T(8,128)} %shard_map.44), calls=%async_computation.6 | async-start | bytes 131072 | tf_op jit(solution)/shard_map/all_to_all | solution.py:333
  152.0 7.2 %all-to-all-done.6.x_ref = f32[8,16,128]{2,1,0:T(8,128)S(1)} async-done(((f32[8,16,128]{2,1,0:T(8,128)}), f32[8,16,128]{2,1,0:T(8,128)S(1)}, u32[]{:S(2)}, u32[]{:S(2)}) %all-to-all-start.6) | async-done | bytes 65568 | tf_op jit(solution)/shard_map/all_to_all | solution.py:333
  159.2 0.6 shard_map.46
  (10 shorter events, 0.2 us)
Async XLA Ops:
  47.3 6.6 %collective-permute-start = (f32[768,128]{1,0:T(8,128)S(1)}, f32[768,128]{1,0:T(8,128)S(1)}, u32[]{:S(2)}, u32[]{:S(2)}) collective-permute-start(f32[768,128]{1,0:T(8,128)S(1)} %get-tuple-element.19), channel_id=1, source_target_pairs={{0,32},{32,0},{64,96},{96,64},{128,160},{160,128},{192,224},{224,1... | collective-permute-start | bytes 1179656 | tf_op jit(solution)/shard_map/ppermute | solution.py:294
  77.7 9.6 %collective-permute-start.1 = (f32[48,128]{1,0:T(8,128)S(1)}, f32[48,128]{1,0:T(8,128)S(1)}, u32[]{:S(2)}, u32[]{:S(2)}) collective-permute-start(f32[48,128]{1,0:T(8,128)S(1)} %get-tuple-element.20), channel_id=1, source_target_pairs={{0,0},{1,9},{2,34},{3,43},{4,68},{5,77},{6,102},{7,111},{8,136},{9... | collective-permute-start | bytes 73736 | tf_op jit(solution)/shard_map/ppermute | solution.py:311
  81.8 11.4 %collective-permute-start.2 = (f32[48,128]{1,0:T(8,128)S(1)}, f32[48,128]{1,0:T(8,128)S(1)}, u32[]{:S(2)}, u32[]{:S(2)}) collective-permute-start(f32[48,128]{1,0:T(8,128)S(1)} %get-tuple-element.21), channel_id=1, source_target_pairs={{0,8},{1,1},{2,42},{3,35},{4,76},{5,69},{6,110},{7,103},{8,144},{9... | collective-permute-start | bytes 73736 | tf_op jit(solution)/shard_map/ppermute | solution.py:312
  84.3 8.9 %copy-start = (f32[1024,12]{0,1:T(8,128)S(1)}, f32[1024,12]{0,1:T(8,128)}, u32[]{:S(2)}) copy-start(f32[1024,12]{0,1:T(8,128)} %param.5) | copy-start | bytes 147460
  94.6 3.1 %collective-permute-start.3 = (f32[96,128]{1,0:T(8,128)S(1)}, f32[96,128]{1,0:T(8,128)S(1)}, u32[]{:S(2)}, u32[]{:S(2)}) collective-permute-start(f32[96,128]{1,0:T(8,128)S(1)} %get-tuple-element.25.mine_ref), channel_id=1, source_target_pairs={{0,32},{32,0},{64,96},{96,64},{128,160},{160,128},{192,224},{224,1... | collective-permute-start | bytes 147464 | tf_op jit(solution)/shard_map/ppermute | solution.py:294
  140.9 11.0 %collective-permute-start.4 = (f32[1152,128]{1,0:T(8,128)S(1)}, f32[1152,128]{1,0:T(8,128)S(1)}, u32[]{:S(2)}, u32[]{:S(2)}) collective-permute-start(f32[1152,128]{1,0:T(8,128)S(1)} %bitcast.7), channel_id=1, source_target_pairs={{0,32},{32,0},{64,96},{96,64},{128,160},{160,128},{192,224},{224,1... | collective-permute-start | bytes 1769480 | tf_op jit(solution)/shard_map/ppermute | solution.py:294
  148.6 10.6 %all-to-all-start.6 = ((f32[8,16,128]{2,1,0:T(8,128)}), f32[8,16,128]{2,1,0:T(8,128)S(1)}, u32[]{:S(2)}, u32[]{:S(2)}) async-start(f32[8,16,128]{2,1,0:T(8,128)} %shard_map.44), calls=%async_computation.6 | async-start | bytes 131072 | tf_op jit(solution)/shard_map/all_to_all | solution.py:333

commit v5 on v4

--- a/solution.py
+++ b/solution.py
@@ -27,9 +27,7 @@
 
 
 def dot_nt(a, b):
-    return lax.dot_general(
-        a, b, (((1,), (1,)), ((), ())), precision=HI, preferred_element_type=jnp.float32
-    )
+    return lax.dot_general(a, b, (((1,), (1,)), ((), ())), preferred_element_type=jnp.float32)
 
 
 def place(row, col, half):
@@ -43,7 +41,11 @@
     return high, (value - high.astype(jnp.float32)).astype(jnp.bfloat16)
 
 
-def product_kernel(f_ref, t_ref, send_ref, keep_ref, ft_ref, top_ref, acc_ref, cut_ref):
+def add_kernel(a_ref, b_ref, _, out_ref):
+    out_ref[...] = a_ref[...] + b_ref[...]
+
+
+def product_kernel(f_ref, t_ref, send_ref, keep_ref, fh_ref, fl_ref, top_ref, acc_ref, cut_ref):
     row, col = lax.axis_index("row"), lax.axis_index("col")
     x, y = col // Y_SIZE, col % Y_SIZE
     panel = lax.broadcasted_iota(jnp.int32, (PW, B), 0) // B
@@ -52,8 +54,8 @@
         if b < STEPS:
             top_ref[:, b * B : (b + 1) * B] = part
             part = jnp.where((row > 0) | (panel < b), part, 0.0)
-        ft_ref[:, b * B : (b + 1) * B] = part
-    fh, fl = split(ft_ref[...])
+        fh_ref[:, b * B : (b + 1) * B], fl_ref[:, b * B : (b + 1) * B] = split(part)
+    fh, fl = fh_ref[...], fl_ref[...]
     th, tl = split(t_ref[...])
     acc_ref[...] = dot_bf16(fh, tl) + dot_bf16(fl, th) + dot_bf16(fh, th)
     for b in range(4):
@@ -118,7 +120,7 @@
             fac_ref[corner_block("li", i, i)] = inv[i, i].T
 
 
-def gram_kernel(ra_ref, rb_ref, g_ref, ft_ref, litp_ref, pay_ref, y_ref, half_ref, ym_ref):
+def gram_kernel(ra_ref, rb_ref, g_ref, fh_ref, fl_ref, litp_ref, pay_ref, y_ref, half_ref, ym_ref, own_ref):
     row, col = lax.axis_index("row"), lax.axis_index("col")
     first = (col // Y_SIZE + row // 4) % 2 == 0
     ra, rb = ra_ref[...], rb_ref[...]
@@ -136,25 +138,31 @@
             diag = jnp.where(panel == b, g, diag)
             y = jnp.where(row > 0, y, 0.0)
         ym_ref[:, b * B : (b + 1) * B] = y
-    gram = dot_nt(ym_ref[...], ft_ref[...])
+    yh, yl = split(ym_ref[...])
+    fh = fh_ref[...]
+    gram = dot_nt(yh, fl_ref[...]) + dot_nt(yl, fh) + dot_nt(yh, fh)
     for k in range(STEPS):
         below = jnp.where(row == 0, top[k], 0.0)
-        pay_ref[pl.ds(24 * (k // 2) + k % 2, 12, stride=2), :] = jnp.where(
-            panel >= k, gram[:, k * B : (k + 1) * B], below
-        )
-    pay_ref[pl.ds(25, 12, stride=2), :] = jnp.where(row == 0, diag, 0.0)
-    own = litp_ref[pl.ds(pl.multiple_of(48 * col, 16), 48), :]
-    pay_ref[48:96, :] = jnp.where(row == 0, own, 0.0)
-
-
-def corner_kernel(w_ref, other_ref, fac_ref, out_ref, u_ref, vt_ref, wp_ref, cut_ref):
+        part = jnp.where(panel >= k, gram[:, k * B : (k + 1) * B], below)
+        if k < 2:
+            pay_ref[pl.ds(k, 12, stride=2), :] = part
+        else:
+            pay_ref[24:36, :] = part
+    pay_ref[36:48, :] = jnp.where(row == 0, diag, 0.0)
+    own_ref[...] = jnp.where(row == 0, litp_ref[pl.ds(pl.multiple_of(48 * col, 16), 48), :], 0.0)
+    for k in range(STEPS):
+        pay_ref[pl.ds(48 + k, 12, stride=3), :] = own_ref[pl.ds(k, 12, stride=4), :]
+    pay_ref[84:88, :] = jnp.zeros((4, B), jnp.float32)
+
+
+def corner_kernel(mine_ref, other_ref, fac_ref, out_ref, u_ref, vt_ref, wp_ref, cut_ref):
     @pl.when(lax.axis_index("row") == 0)
     def _():
         for x in range(X_SIZE):
             for k in range(4):
-                half_ref = w_ref if k < 2 else other_ref
+                half_ref = mine_ref if k < 2 else other_ref
                 u_ref[96 * x : 96 * (x + 1), k * B : (k + 1) * B] = half_ref[
-                    pl.ds(288 * x + k % 2, 96, stride=2), :
+                    pl.ds(192 * x + k % 2, 96, stride=2), :
                 ]
         rows = lax.broadcasted_iota(jnp.int32, (B, B), 0)
         cols = lax.broadcasted_iota(jnp.int32, (B, B), 1)
@@ -209,47 +217,52 @@
             out_ref[:, k * B : (k + 1) * B] = cut_ref[pl.ds(k, 12, stride=4), :]
 
 
-def route_kernel(mine_ref, other_ref, out_ref, sum_ref, own_ref):
-    mine, other = mine_ref[...], other_ref[...]
-    corner = mine[0:48] + other[0:48]
-    inverse = mine[48:96] + other[48:96]
-    sum_ref[...] = corner
-    own_ref[...] = inverse
-    out_ref[0] = corner
+def route_kernel(mine_ref, other_ref, out_ref, sum_ref):
+    total = mine_ref[...] + other_ref[...]
+    sum_ref[...] = total
+    out_ref[0] = total[0:40]
     for z in range(1, 8):
-        out_ref[z] = inverse
-
-
-def pack_y_kernel(sum_ref, own_ref, got_ref, y_ref, out_ref):
+        out_ref[z] = total[48:88]
+
+
+def pack_y_kernel(sum_ref, got_ref, y_ref, out_ref):
     row = lax.axis_index("row")
-    corner = sum_ref[...] + jnp.sum(got_ref[1:], axis=0)
-    corner = jnp.where(row % 2 == 0, corner[0:24], corner[24:48])
-    inverse = jnp.where(row < 2, own_ref[...], got_ref[0])
+    corner = sum_ref[0:36, :] + jnp.sum(got_ref[1:, 0:36, :], axis=0)
+    inverse = jnp.where(row < 2, sum_ref[48:84, :], got_ref[0, 0:36, :])
+    first, second = corner[24:36], sum_ref[36:48, :]
     for y in range(Y_SIZE):
-        out_ref[y, 0:24, :] = corner
-        out_ref[y, 24:72, :] = inverse
-        out_ref[y, 72:88, :] = y_ref[y]
+        out_ref[y, pl.ds(0, 12, stride=2), :] = first
+        out_ref[y, pl.ds(1, 12, stride=2), :] = second
+        out_ref[y, 24:60, :] = inverse
+        out_ref[y, 60:72, :] = y_ref[y, 0:12, :]
+
+    @pl.when(row % 2 == 0)
+    def _():
+        for y in range(Y_SIZE):
+            out_ref[y, 0:24, :] = corner[0:24]
 
 
 def pack_x_kernel(near_ref, out_ref):
     for x in range(X_SIZE):
         for y in range(Y_SIZE):
             out_ref[x, 24 * y : 24 * (y + 1), :] = near_ref[y, 0:24, :]
-            out_ref[x, 192 + 12 * y : 192 + 12 * (y + 1), :] = near_ref[y, 72:84, :]
-
-
-def solve_kernel(near_ref, w_ref, out_ref, yt_ref, lit_ref):
+            out_ref[x, 192 + 12 * y : 192 + 12 * (y + 1), :] = near_ref[y, 60:72, :]
+
+
+def solve_kernel(near_ref, w_ref, out_ref, half_ref, yt_ref, lit_ref):
     for x in range(X_SIZE):
         yt_ref[96 * x : 96 * (x + 1), :] = w_ref[288 * x + 192 : 288 * (x + 1), :]
     for y in range(Y_SIZE):
         for k in range(STEPS):
             lit_ref[12 * y : 12 * (y + 1), k * B : (k + 1) * B] = near_ref[
-                y, pl.ds(24 + k, 12, stride=4), :
+                y, pl.ds(24 + k, 12, stride=3), :
             ]
     yt_ref[0:96, :] = 0.5 * dot(lit_ref[...], yt_ref[...])
     for y in range(Y_SIZE):
         out_ref[y, 0:12, :] = yt_ref[12 * y : 12 * (y + 1), :]
         out_ref[y, 12:16, :] = jnp.zeros((4, B), jnp.float32)
+    for x in range(X_SIZE):
+        half_ref[192 * x : 192 * (x + 1), :] = w_ref[288 * x : 288 * x + 192, :]
 
 
 def output_kernel(x_ref, corner_ref, out_ref):
@@ -265,23 +278,27 @@
     return jax.ShapeDtypeStruct(shape, jnp.float32)
 
 
+def bf16(*shape):
+    return jax.ShapeDtypeStruct(shape, jnp.bfloat16)
+
+
 def vmem(*shape):
     return pltpu.VMEM(shape, jnp.float32)
 
 
-def call(kernel, out_shape, *args, scratch=(), flops=0):
+def call(kernel, out_shape, *args, scratch=(), flops=0, after=()):
     many = isinstance(out_shape, (list, tuple))
     spec = pl.BlockSpec(memory_space=pltpu.VMEM)
     total = sum(a.size for a in args) * 4
     return pl.pallas_call(
         kernel,
         out_shape=out_shape,
-        in_specs=[spec] * len(args),
+        in_specs=[spec] * len(args) + [pl.BlockSpec(memory_space=pl.ANY)] * len(after),
         out_specs=[spec] * len(out_shape) if many else spec,
         scratch_shapes=list(scratch),
         compiler_params=PARAMS,
         cost_estimate=pl.CostEstimate(flops=flops, bytes_accessed=total, transcendentals=0),
-    )(*args)
+    )(*args, *after)
 
 
 def spread(value, axis, groups):
@@ -298,11 +315,14 @@
     factor = factor_panels.T.reshape(96, B)
     near = spread(factor, "col", Y_GROUPS).reshape(Y_SIZE * 96, B)
     panels = spread(near, "col", X_GROUPS).reshape(PW * 8, B)
-    send, keep, ft, ft_corner = call(
-        product_kernel, [f32(768, B), f32(768, B), f32(PW, 1024), f32(PW, PW)], panels, trail_adj,
+    send, keep, panel_high, panel_low, ft_corner = call(
+        product_kernel, [f32(768, B), f32(768, B), bf16(PW, 1024), bf16(PW, 1024), f32(PW, PW)], panels, trail_adj,
         scratch=[vmem(PW, 512), vmem(1536, B)], flops=12 * 1024 * 512 * PW,
     )
-    both = (keep + between_cores(send)).reshape(8, 96, B)
+    fac, inv_tp = call(
+        inverse_kernel, [f32(15 * B, B), f32(1536, B)], ft_corner, flops=12 * 60 * B**3,
+    )
+    both = call(add_kernel, f32(768, B), keep, between_cores(send), after=[inv_tp]).reshape(8, 96, B)
     pieces = lax.all_to_all(both, "row", 0, 0, axis_index_groups=Z_GROUPS)
     send_a, send_b = call(sum_kernel, [f32(48, B), f32(48, B)], pieces)
     devices = [(r, c) for r in range(16) for c in range(32)]
@@ -310,30 +330,26 @@
     to_b = [(r * 32 + c, place(r, c, 1 - c % 2)) for r, c in devices]
     got_a = lax.ppermute(send_a, ("row", "col"), to_a)
     got_b = lax.ppermute(send_b, ("row", "col"), to_b)
-    fac, inv_tp = call(
-        inverse_kernel, [f32(15 * B, B), f32(1536, B)], ft_corner, flops=12 * 60 * B**3,
-    )
     payload, own_y = call(
-        gram_kernel, [f32(96, B), f32(8, 16, B)], got_a, got_b, factor_adj.T, ft, inv_tp,
-        scratch=[vmem(96, B), vmem(12, 1024)], flops=12 * 12 * 1024 * PW,
-    )
-    out_u, sum_u, own = call(
-        route_kernel, [f32(8, 48, B), f32(48, B), f32(48, B)], payload, between_cores(payload),
+        gram_kernel, [f32(88, B), f32(8, 16, B)], got_a, got_b, factor_adj.T, panel_high, panel_low, inv_tp,
+        scratch=[vmem(96, B), vmem(12, 1024), vmem(48, B)], flops=12 * 12 * 1024 * PW,
+    )
+    out_u, sum_u = call(
+        route_kernel, [f32(8, 40, B), f32(88, B)], payload, between_cores(payload),
     )
     got = lax.all_to_all(out_u, "row", 0, 0, axis_index_groups=Z_GROUPS)
-    near = call(pack_y_kernel, f32(8, 88, B), sum_u, own, got, own_y)
+    near = call(pack_y_kernel, f32(8, 72, B), sum_u, got, own_y)
     near = lax.all_to_all(near, "col", 0, 0, axis_index_groups=Y_GROUPS)
     wide = call(pack_x_kernel, f32(4, 288, B), near)
     wide = lax.all_to_all(wide, "col", 0, 0, axis_index_groups=X_GROUPS).reshape(4 * 288, B)
-    other = between_cores(wide)
-    solved = call(
-        solve_kernel, f32(8, 16, B), near, wide,
+    solved, half = call(
+        solve_kernel, [f32(8, 16, B), f32(768, B)], near, wide,
         scratch=[vmem(PW, B), vmem(96, PW)], flops=12 * 96 * B * PW,
     )
     rows_x = lax.all_to_all(solved, "col", 0, 0, axis_index_groups=Y_GROUPS)
     corner = call(
-        corner_kernel, f32(12, PW), wide, other, fac,
-        scratch=[vmem(PW, 512), vmem(PW, PW), vmem(1536, B), vmem(48, B)], flops=12 * 60 * B**3,
+        corner_kernel, f32(12, PW), half, between_cores(half), fac,
+        scratch=[vmem(PW, 512), vmem(PW, PW), vmem(1536, B), vmem(48, B)],
     )
     out = call(output_kernel, f32(12, 1024), rows_x, corner)
     return out.T

time: 160 us -> 158 us (0.988)
  blocking collectives: 110 us -> 108 us
    pallas_call x10 -> x11, Pallas kernels: 6.29 us -> 5.76 us  [call(): pl.pallas_call(kernel, out_shape=out_shape, in_specs=[spec] * len(args) +...]
  transfers between devices with their start and end apart: 6 -> 6, of which waited for: 5 -> 5; matrix products, arithmetic and copies ran while one was open for 0% -> 0% of each run, Pallas kernels for 1% -> 0%
where the time goes in v5:
time: 158 us; the launch traced here: 157 us
  blocking collectives  108 us (68%)
  starting transfers between devices  23.9 us (15%)
  waiting for transfers between devices  18.6 us (12%)
  Pallas kernels  5.76 us (4%)
    all_to_all x2, blocking collectives, spread(): return lax.all_to_all(copies, axis, 0, 0, axis_index_groups=groups)  43.1 us
    all_to_all x1, blocking collectives, on_device(): pieces = lax.all_to_all(both, 'row', 0, 0, axis_index_groups=Z_GROUPS)  23.7 us
    all_to_all x1, blocking collectives, on_device(): got = lax.all_to_all(out_u, 'row', 0, 0, axis_index_groups=Z_GROUPS)  16.3 us
    all_to_all x1, blocking collectives, on_device(): near = lax.all_to_all(near, 'col', 0, 0, axis_index_groups=Y_GROUPS)  14.9 us
    ppermute x3, starting transfers between devices, between_cores(): return lax.ppermute(value, 'row', [(r, r ^ 1) for r in range(16)])  13.9 us
    all_to_all x1, blocking collectives, on_device(): lax.all_to_all(wide, 'col', 0, 0, axis_index_groups=X_GROUPS)  9.67 us
    all_to_all x1, waiting for transfers between devices, on_device(): rows_x = lax.all_to_all(solved, 'col', 0, 0, axis_index_groups=Y_GROUPS)  7.24 us
    ppermute x1, waiting for transfers between devices, on_device(): got_b = lax.ppermute(send_b, ('row', 'col'), to_b)  5.93 us
  transfers between devices with their start and end apart: 6, of which 5 were waited for; matrix products, arithmetic and copies ran while one was open for 0% of the time, Pallas kernels for 0%

profile of v5, /device:TPU:1, one launch (start us, length us, event | category | flops | bytes accessed | tf_op | source)
XLA Modules:
  0.0 157.1 jit_solution(11361277995753637139)
XLA Ops:
  0.0 0.9 broadcast_in_dim.14
  0.9 19.8 %all_to_all.35 = f32[8,96,128]{2,1,0:T(8,128)S(1)} all-to-all(f32[8,96,128]{2,1,0:T(8,128)S(1)} %broadcast_in_dim.15), channel_id=1, replica_groups={{0,1,2,3,4,5,6,7},{8,9,10,11,12,13,14,15},{16,17,18,19,20,21,22,23},{24..., dimensions={0} | all-to-all | bytes 786432 | tf_op jit(solution)/shard_map/all_to_all | solution.py:307
  20.7 0.1 broadcast_in_dim.17
  20.8 23.3 %all_to_all.36 = f32[4,768,128]{2,1,0:T(8,128)S(1)} all-to-all(f32[4,768,128]{2,1,0:T(8,128)S(1)} %broadcast_in_dim.17), channel_id=1, replica_groups={{0,8,16,24},{1,9,17,25},{2,10,18,26},{3,11,19,27},{4,12,20,28},{5,13,21..., dimensions={0} | all-to-all | bytes 3145728 | tf_op jit(solution)/shard_map/all_to_all | solution.py:307
  44.1 3.2 %shard_map.37 = (f32[768,128]{1,0:T(8,128)S(1)}, f32[768,128]{1,0:T(8,128)S(1)}, bf16[384,1024]{1,0:T(8,128)(2,1)S(1)}, bf16[384,1024]{1,0:T(8,128)(2,1)S(1)}, f32[384,384]{1,0:T(8,128)S(1)}) custom-call(f32[3072,128]{1,0:T(8,128)S(1)} %bitcast.8, f32[1024,512]{1,0:T(8,128)} %t_ref.1), custom_call_target="tpu_custom_call" | custom-call | flops 2415919104 | bytes 3670016 | tf_op jit(solution)/shard_map/pallas_call | solution.py:293
  47.4 5.2 %collective-permute-start = (f32[768,128]{1,0:T(8,128)S(1)}, f32[768,128]{1,0:T(8,128)S(1)}, u32[]{:S(2)}, u32[]{:S(2)}) collective-permute-start(f32[768,128]{1,0:T(8,128)S(1)} %get-tuple-element.21), channel_id=1, source_target_pairs={{0,32},{32,0},{64,96},{96,64},{128,160},{160,128},{192,224},{224,1... | collective-permute-start | bytes 1179656 | tf_op jit(solution)/shard_map/ppermute | solution.py:311
  52.6 1.3 collective-permute-done.b_ref
  53.9 0.1 shard_map.39
  54.0 23.7 %all_to_all.37.s_ref = f32[8,96,128]{2,1,0:T(8,128)S(1)} all-to-all(f32[8,96,128]{2,1,0:T(8,128)S(1)} %bitcast.9), channel_id=1, replica_groups={{0,64,128,192,256,320,384,448},{32,96,160,224,288,352,416,480},{1,65,12..., dimensions={0} | all-to-all | bytes 786432 | tf_op jit(solution)/shard_map/all_to_all | solution.py:326
  77.7 4.1 %collective-permute-start.1 = (f32[48,128]{1,0:T(8,128)S(1)}, f32[48,128]{1,0:T(8,128)S(1)}, u32[]{:S(2)}, u32[]{:S(2)}) collective-permute-start(f32[48,128]{1,0:T(8,128)S(1)} %get-tuple-element.24), channel_id=1, source_target_pairs={{0,0},{1,9},{2,34},{3,43},{4,68},{5,77},{6,102},{7,111},{8,136},{9... | collective-permute-start | bytes 73736 | tf_op jit(solution)/shard_map/ppermute | solution.py:331
  81.8 2.5 %collective-permute-start.2 = (f32[48,128]{1,0:T(8,128)S(1)}, f32[48,128]{1,0:T(8,128)S(1)}, u32[]{:S(2)}, u32[]{:S(2)}) collective-permute-start(f32[48,128]{1,0:T(8,128)S(1)} %get-tuple-element.25), channel_id=1, source_target_pairs={{0,8},{1,1},{2,42},{3,35},{4,76},{5,69},{6,110},{7,103},{8,144},{9... | collective-permute-start | bytes 73736 | tf_op jit(solution)/shard_map/ppermute | solution.py:332
  84.4 3.0 %collective-permute-done.1.ra_ref = f32[48,128]{1,0:T(8,128)S(1)} collective-permute-done((f32[48,128]{1,0:T(8,128)S(1)}, f32[48,128]{1,0:T(8,128)S(1)}, u32[]{:S(2)}, u32[]{:S(2)}) %collective-permute-start.1) | collective-permute-done | bytes 24608 | tf_op jit(solution)/shard_map/ppermute | solution.py:331
  87.4 5.9 %collective-permute-done.2.rb_ref = f32[48,128]{1,0:T(8,128)S(1)} collective-permute-done((f32[48,128]{1,0:T(8,128)S(1)}, f32[48,128]{1,0:T(8,128)S(1)}, u32[]{:S(2)}, u32[]{:S(2)}) %collective-permute-start.2) | collective-permute-done | bytes 24608 | tf_op jit(solution)/shard_map/ppermute | solution.py:332
  93.3 0.7 shard_map.41
  94.0 1.9 %collective-permute-start.3 = (f32[88,128]{1,0:T(8,128)S(1)}, f32[88,128]{1,0:T(8,128)S(1)}, u32[]{:S(2)}, u32[]{:S(2)}) collective-permute-start(f32[88,128]{1,0:T(8,128)S(1)} %get-tuple-element.28.mine_ref), channel_id=1, source_target_pairs={{0,32},{32,0},{64,96},{96,64},{128,160},{160,128},{192,224},{224,1... | collective-permute-start | bytes 135176 | tf_op jit(solution)/shard_map/ppermute | solution.py:311
  95.9 1.2 collective-permute-done.3.other_ref
  97.1 16.3 %all_to_all.38.got_ref = f32[8,40,128]{2,1,0:T(8,128)S(1)} all-to-all(f32[8,40,128]{2,1,0:T(8,128)S(1)} %get-tuple-element.30), channel_id=1, replica_groups={{0,64,128,192,256,320,384,448},{32,96,160,224,288,352,416,480},{1,65,12..., dimensions={0} | all-to-all | bytes 327680 | tf_op jit(solution)/shard_map/all_to_all | solution.py:340
  113.5 14.9 %all_to_all.39.near_ref = f32[8,72,128]{2,1,0:T(8,128)S(1)} all-to-all(f32[8,72,128]{2,1,0:T(8,128)S(1)} %shard_map.43), channel_id=1, replica_groups={{0,1,2,3,4,5,6,7},{8,9,10,11,12,13,14,15},{16,17,18,19,20,21,22,23},{24..., dimensions={0} | all-to-all | bytes 589824 | tf_op jit(solution)/shard_map/all_to_all | solution.py:342
  128.4 9.7 %all_to_all.40 = f32[4,288,128]{2,1,0:T(8,128)S(1)} all-to-all(f32[4,288,128]{2,1,0:T(8,128)S(1)} %shard_map.44), channel_id=1, replica_groups={{0,8,16,24},{1,9,17,25},{2,10,18,26},{3,11,19,27},{4,12,20,28},{5,13,21..., dimensions={0} | all-to-all | bytes 1179648 | tf_op jit(solution)/shard_map/all_to_all | solution.py:344
  138.0 0.9 shard_map.45
  139.0 6.8 %collective-permute-start.4 = (f32[768,128]{1,0:T(8,128)S(1)}, f32[768,128]{1,0:T(8,128)S(1)}, u32[]{:S(2)}, u32[]{:S(2)}) collective-permute-start(f32[768,128]{1,0:T(8,128)S(1)} %get-tuple-element.33.mine_ref), channel_id=1, source_target_pairs={{0,32},{32,0},{64,96},{96,64},{128,160},{160,128},{192,224},{224,1... | collective-permute-start | bytes 1179656 | tf_op jit(solution)/shard_map/ppermute | solution.py:311
  145.8 3.4 %all-to-all-start.6 = ((f32[8,16,128]{2,1,0:T(8,128)}), f32[8,16,128]{2,1,0:T(8,128)S(1)}, u32[]{:S(2)}, u32[]{:S(2)}) async-start(f32[8,16,128]{2,1,0:T(8,128)} %get-tuple-element.32), calls=%async_computation.6 | async-start | bytes 131072 | tf_op jit(solution)/shard_map/all_to_all | solution.py:349
  149.2 7.2 %all-to-all-done.6.x_ref = f32[8,16,128]{2,1,0:T(8,128)S(1)} async-done(((f32[8,16,128]{2,1,0:T(8,128)}), f32[8,16,128]{2,1,0:T(8,128)S(1)}, u32[]{:S(2)}, u32[]{:S(2)}) %all-to-all-start.6) | async-done | bytes 65568 | tf_op jit(solution)/shard_map/all_to_all | solution.py:349
  156.4 0.6 shard_map.47
  (10 shorter events, 0.2 us)
Async XLA Ops:
  47.4 6.6 %collective-permute-start = (f32[768,128]{1,0:T(8,128)S(1)}, f32[768,128]{1,0:T(8,128)S(1)}, u32[]{:S(2)}, u32[]{:S(2)}) collective-permute-start(f32[768,128]{1,0:T(8,128)S(1)} %get-tuple-element.21), channel_id=1, source_target_pairs={{0,32},{32,0},{64,96},{96,64},{128,160},{160,128},{192,224},{224,1... | collective-permute-start | bytes 1179656 | tf_op jit(solution)/shard_map/ppermute | solution.py:311
  53.9 39.3 %copy-start = (f32[1024,12]{0,1:T(8,128)S(1)}, f32[1024,12]{0,1:T(8,128)}, u32[]{:S(2)}) copy-start(f32[1024,12]{0,1:T(8,128)} %param.5) | copy-start | bytes 147460
  77.7 9.6 %collective-permute-start.1 = (f32[48,128]{1,0:T(8,128)S(1)}, f32[48,128]{1,0:T(8,128)S(1)}, u32[]{:S(2)}, u32[]{:S(2)}) collective-permute-start(f32[48,128]{1,0:T(8,128)S(1)} %get-tuple-element.24), channel_id=1, source_target_pairs={{0,0},{1,9},{2,34},{3,43},{4,68},{5,77},{6,102},{7,111},{8,136},{9... | collective-permute-start | bytes 73736 | tf_op jit(solution)/shard_map/ppermute | solution.py:331
  81.8 11.4 %collective-permute-start.2 = (f32[48,128]{1,0:T(8,128)S(1)}, f32[48,128]{1,0:T(8,128)S(1)}, u32[]{:S(2)}, u32[]{:S(2)}) collective-permute-start(f32[48,128]{1,0:T(8,128)S(1)} %get-tuple-element.25), channel_id=1, source_target_pairs={{0,8},{1,1},{2,42},{3,35},{4,76},{5,69},{6,110},{7,103},{8,144},{9... | collective-permute-start | bytes 73736 | tf_op jit(solution)/shard_map/ppermute | solution.py:332
  94.0 3.1 %collective-permute-start.3 = (f32[88,128]{1,0:T(8,128)S(1)}, f32[88,128]{1,0:T(8,128)S(1)}, u32[]{:S(2)}, u32[]{:S(2)}) collective-permute-start(f32[88,128]{1,0:T(8,128)S(1)} %get-tuple-element.28.mine_ref), channel_id=1, source_target_pairs={{0,32},{32,0},{64,96},{96,64},{128,160},{160,128},{192,224},{224,1... | collective-permute-start | bytes 135176 | tf_op jit(solution)/shard_map/ppermute | solution.py:311
  139.0 10.1 %collective-permute-start.4 = (f32[768,128]{1,0:T(8,128)S(1)}, f32[768,128]{1,0:T(8,128)S(1)}, u32[]{:S(2)}, u32[]{:S(2)}) collective-permute-start(f32[768,128]{1,0:T(8,128)S(1)} %get-tuple-element.33.mine_ref), channel_id=1, source_target_pairs={{0,32},{32,0},{64,96},{96,64},{128,160},{160,128},{192,224},{224,1... | collective-permute-start | bytes 1179656 | tf_op jit(solution)/shard_map/ppermute | solution.py:311
  145.8 10.6 %all-to-all-start.6 = ((f32[8,16,128]{2,1,0:T(8,128)}), f32[8,16,128]{2,1,0:T(8,128)S(1)}, u32[]{:S(2)}, u32[]{:S(2)}) async-start(f32[8,16,128]{2,1,0:T(8,128)} %get-tuple-element.32), calls=%async_computation.6 | async-start | bytes 131072 | tf_op jit(solution)/shard_map/all_to_all | solution.py:349

commit v6 on v5

--- a/solution.py
+++ b/solution.py
@@ -32,7 +32,7 @@
 
 def place(row, col, half):
     x, y = col // Y_SIZE, col % Y_SIZE
-    x_to, y_to = (x + 2 * (row % 2) + half) % X_SIZE, (y + row // 2) % Y_SIZE
+    x_to, y_to = (x + 2 * (row % 2) + half) % X_SIZE, (y + row // 2 + 12 - col // 4) % Y_SIZE
     return col // 2 * (X_SIZE * Y_SIZE) + x_to * Y_SIZE + y_to
 
 
@@ -45,7 +45,16 @@
     out_ref[...] = a_ref[...] + b_ref[...]
 
 
-def product_kernel(f_ref, t_ref, send_ref, keep_ref, fh_ref, fl_ref, top_ref, acc_ref, cut_ref):
+def product_kernel(
+    f_ref, t_hbm_ref, send_ref, keep_ref, fh_ref, fl_ref, top_ref, acc_ref, cut_ref, t_ref, sems
+):
+    parts = [pl.ds(256 * q, 256) for q in range(4)]
+    copies = [
+        pltpu.make_async_copy(t_hbm_ref.at[part], t_ref.at[part], sems.at[q])
+        for q, part in enumerate(parts)
+    ]
+    for copy in copies:
+        copy.start()
     row, col = lax.axis_index("row"), lax.axis_index("col")
     x, y = col // Y_SIZE, col % Y_SIZE
     panel = lax.broadcasted_iota(jnp.int32, (PW, B), 0) // B
@@ -55,15 +64,18 @@
             top_ref[:, b * B : (b + 1) * B] = part
             part = jnp.where((row > 0) | (panel < b), part, 0.0)
         fh_ref[:, b * B : (b + 1) * B], fl_ref[:, b * B : (b + 1) * B] = split(part)
-    fh, fl = fh_ref[...], fl_ref[...]
-    th, tl = split(t_ref[...])
-    acc_ref[...] = dot_bf16(fh, tl) + dot_bf16(fl, th) + dot_bf16(fh, th)
+    for q, part in enumerate(parts):
+        copies[q].wait()
+        fh, fl = fh_ref[:, part], fl_ref[:, part]
+        th, tl = split(t_ref[part, :])
+        term = dot_bf16(fh, tl) + dot_bf16(fl, th) + dot_bf16(fh, th)
+        acc_ref[...] = term if q == 0 else acc_ref[...] + term
     for b in range(4):
         cut_ref[pl.ds(b, PW, stride=4), :] = acc_ref[:, b * B : (b + 1) * B]
     for core, target in ((1 - row % 2, send_ref), (row % 2, keep_ref)):
         for z in range(8):
             for half in range(2):
-                x_to, y_to = (x + 2 * core + half) % X_SIZE, (y + z) % Y_SIZE
+                x_to, y_to = (x + 2 * core + half) % X_SIZE, (y + z + 12 - col // 4) % Y_SIZE
                 first = pl.multiple_of((x_to * Y_SIZE + y_to) * 48, 16)
                 target[z * 96 + half * 48 : z * 96 + half * 48 + 48, :] = cut_ref[pl.ds(first, 48), :]
 
@@ -316,8 +328,9 @@
     near = spread(factor, "col", Y_GROUPS).reshape(Y_SIZE * 96, B)
     panels = spread(near, "col", X_GROUPS).reshape(PW * 8, B)
     send, keep, panel_high, panel_low, ft_corner = call(
-        product_kernel, [f32(768, B), f32(768, B), bf16(PW, 1024), bf16(PW, 1024), f32(PW, PW)], panels, trail_adj,
-        scratch=[vmem(PW, 512), vmem(1536, B)], flops=12 * 1024 * 512 * PW,
+        product_kernel, [f32(768, B), f32(768, B), bf16(PW, 1024), bf16(PW, 1024), f32(PW, PW)], panels,
+        scratch=[vmem(PW, 512), vmem(1536, B), vmem(1024, 512), pltpu.SemaphoreType.DMA((4,))],
+        after=[trail_adj], flops=12 * 1024 * 512 * PW,
     )
     fac, inv_tp = call(
         inverse_kernel, [f32(15 * B, B), f32(1536, B)], ft_corner, flops=12 * 60 * B**3,

time: 158 us -> 154 us (0.975)
  waiting for transfers between devices: 18.6 us -> 14.2 us
  starting transfers between devices: 23.9 us -> 26.1 us
    ppermute x1, waiting for transfers between devices: 2.96 us -> 0.01 us  [on_device(): got_a = lax.ppermute(send_a, ('row', 'col'), to_a)]
  transfers between devices with their start and end apart: 6 -> 6, of which waited for: 5 -> 4; matrix products, arithmetic and copies ran while one was open for 0% -> 0% of each run, Pallas kernels for 0% -> 0%
where the time goes in v6:
time: 154 us
  blocking collectives  107 us (69%)
  starting transfers between devices  26.1 us (17%)
  waiting for transfers between devices  14.2 us (9%)
  Pallas kernels  5.21 us (3%)
    all_to_all x2, blocking collectives, spread(): return lax.all_to_all(copies, axis, 0, 0, axis_index_groups=groups)  43.1 us
    all_to_all x1, blocking collectives, on_device(): pieces = lax.all_to_all(both, 'row', 0, 0, axis_index_groups=Z_GROUPS)  23.7 us
    all_to_all x1, blocking collectives, on_device(): got = lax.all_to_all(out_u, 'row', 0, 0, axis_index_groups=Z_GROUPS)  16.1 us
    ppermute x3, starting transfers between devices, between_cores(): return lax.ppermute(value, 'row', [(r, r ^ 1) for r in range(16)])  14.2 us
    all_to_all x1, blocking collectives, on_device(): near = lax.all_to_all(near, 'col', 0, 0, axis_index_groups=Y_GROUPS)  14.1 us
    all_to_all x1, blocking collectives, on_device(): lax.all_to_all(wide, 'col', 0, 0, axis_index_groups=X_GROUPS)  10 us
    all_to_all x1, waiting for transfers between devices, on_device(): rows_x = lax.all_to_all(solved, 'col', 0, 0, axis_index_groups=Y_GROUPS)  7.24 us
    pallas_call x11, Pallas kernels, call(): pl.pallas_call(kernel, out_shape=out_shape, in_specs=[spec] * len(args) +...  5.21 us
  transfers between devices with their start and end apart: 6, of which 4 were waited for; matrix products, arithmetic and copies ran while one was open for 0% of the time, Pallas kernels for 0%

profile of v6, /device:TPU:1, one launch (start us, length us, event | category | flops | bytes accessed | tf_op | source)
XLA Modules:
  0.0 153.6 jit_solution(12194387419317873493)
XLA Ops:
  0.0 0.9 broadcast_in_dim.14
  0.9 19.8 %all_to_all.35 = f32[8,96,128]{2,1,0:T(8,128)S(1)} all-to-all(f32[8,96,128]{2,1,0:T(8,128)S(1)} %broadcast_in_dim.15), channel_id=1, replica_groups={{0,1,2,3,4,5,6,7},{8,9,10,11,12,13,14,15},{16,17,18,19,20,21,22,23},{24..., dimensions={0} | all-to-all | bytes 786432 | tf_op jit(solution)/shard_map/all_to_all | solution.py:319
  20.7 0.1 broadcast_in_dim.17
  20.8 23.3 %all_to_all.36 = f32[4,768,128]{2,1,0:T(8,128)S(1)} all-to-all(f32[4,768,128]{2,1,0:T(8,128)S(1)} %broadcast_in_dim.17), channel_id=1, replica_groups={{0,8,16,24},{1,9,17,25},{2,10,18,26},{3,11,19,27},{4,12,20,28},{5,13,21..., dimensions={0} | all-to-all | bytes 3145728 | tf_op jit(solution)/shard_map/all_to_all | solution.py:319
  44.1 2.7 %shard_map.37 = (f32[768,128]{1,0:T(8,128)S(1)}, f32[768,128]{1,0:T(8,128)S(1)}, bf16[384,1024]{1,0:T(8,128)(2,1)S(1)}, bf16[384,1024]{1,0:T(8,128)(2,1)S(1)}, f32[384,384]{1,0:T(8,128)S(1)}) custom-call(f32[3072,128]{1,0:T(8,128)S(1)} %bitcast.8, f32[1024,512]{1,0:T(8,128)} %t_hbm_ref.1), custom_call_target="tpu_custom_call" | custom-call | flops 2415919104 | bytes 1572864 | tf_op jit(solution)/shard_map/pallas_call | solution.py:305
  46.8 5.2 %collective-permute-start = (f32[768,128]{1,0:T(8,128)S(1)}, f32[768,128]{1,0:T(8,128)S(1)}, u32[]{:S(2)}, u32[]{:S(2)}) collective-permute-start(f32[768,128]{1,0:T(8,128)S(1)} %get-tuple-element.21), channel_id=1, source_target_pairs={{0,32},{32,0},{64,96},{96,64},{128,160},{160,128},{192,224},{224,1... | collective-permute-start | bytes 1179656 | tf_op jit(solution)/shard_map/ppermute | solution.py:323
  52.1 1.3 collective-permute-done.b_ref
  53.4 0.1 shard_map.39
  53.4 23.7 %all_to_all.37.s_ref = f32[8,96,128]{2,1,0:T(8,128)S(1)} all-to-all(f32[8,96,128]{2,1,0:T(8,128)S(1)} %bitcast.9), channel_id=1, replica_groups={{0,64,128,192,256,320,384,448},{32,96,160,224,288,352,416,480},{1,65,12..., dimensions={0} | all-to-all | bytes 786432 | tf_op jit(solution)/shard_map/all_to_all | solution.py:339
  77.2 5.2 %collective-permute-start.1 = (f32[48,128]{1,0:T(8,128)S(1)}, f32[48,128]{1,0:T(8,128)S(1)}, u32[]{:S(2)}, u32[]{:S(2)}) collective-permute-start(f32[48,128]{1,0:T(8,128)S(1)} %get-tuple-element.24), channel_id=1, source_target_pairs={{0,4},{1,13},{2,38},{3,47},{4,71},{5,72},{6,97},{7,106},{8,138},{9... | collective-permute-start | bytes 73736 | tf_op jit(solution)/shard_map/ppermute | solution.py:344
  82.4 3.3 %collective-permute-start.2 = (f32[48,128]{1,0:T(8,128)S(1)}, f32[48,128]{1,0:T(8,128)S(1)}, u32[]{:S(2)}, u32[]{:S(2)}) collective-permute-start(f32[48,128]{1,0:T(8,128)S(1)} %get-tuple-element.25), channel_id=1, source_target_pairs={{0,12},{1,5},{2,46},{3,39},{4,79},{5,64},{6,105},{7,98},{8,146},{9... | collective-permute-start | bytes 73736 | tf_op jit(solution)/shard_map/ppermute | solution.py:345
  85.7 4.8 %collective-permute-done.2.rb_ref = f32[48,128]{1,0:T(8,128)S(1)} collective-permute-done((f32[48,128]{1,0:T(8,128)S(1)}, f32[48,128]{1,0:T(8,128)S(1)}, u32[]{:S(2)}, u32[]{:S(2)}) %collective-permute-start.2) | collective-permute-done | bytes 24608 | tf_op jit(solution)/shard_map/ppermute | solution.py:345
  90.5 0.7 shard_map.41
  91.3 2.6 %collective-permute-start.3 = (f32[88,128]{1,0:T(8,128)S(1)}, f32[88,128]{1,0:T(8,128)S(1)}, u32[]{:S(2)}, u32[]{:S(2)}) collective-permute-start(f32[88,128]{1,0:T(8,128)S(1)} %get-tuple-element.28.mine_ref), channel_id=1, source_target_pairs={{0,32},{32,0},{64,96},{96,64},{128,160},{160,128},{192,224},{224,1... | collective-permute-start | bytes 135176 | tf_op jit(solution)/shard_map/ppermute | solution.py:323
  93.8 0.9 collective-permute-done.3.other_ref
  94.7 16.1 %all_to_all.38.got_ref = f32[8,40,128]{2,1,0:T(8,128)S(1)} all-to-all(f32[8,40,128]{2,1,0:T(8,128)S(1)} %get-tuple-element.30), channel_id=1, replica_groups={{0,64,128,192,256,320,384,448},{32,96,160,224,288,352,416,480},{1,65,12..., dimensions={0} | all-to-all | bytes 327680 | tf_op jit(solution)/shard_map/all_to_all | solution.py:353
  110.8 14.1 %all_to_all.39.near_ref = f32[8,72,128]{2,1,0:T(8,128)S(1)} all-to-all(f32[8,72,128]{2,1,0:T(8,128)S(1)} %shard_map.43), channel_id=1, replica_groups={{0,1,2,3,4,5,6,7},{8,9,10,11,12,13,14,15},{16,17,18,19,20,21,22,23},{24..., dimensions={0} | all-to-all | bytes 589824 | tf_op jit(solution)/shard_map/all_to_all | solution.py:355
  125.0 10.0 %all_to_all.40 = f32[4,288,128]{2,1,0:T(8,128)S(1)} all-to-all(f32[4,288,128]{2,1,0:T(8,128)S(1)} %shard_map.44), channel_id=1, replica_groups={{0,8,16,24},{1,9,17,25},{2,10,18,26},{3,11,19,27},{4,12,20,28},{5,13,21..., dimensions={0} | all-to-all | bytes 1179648 | tf_op jit(solution)/shard_map/all_to_all | solution.py:357
  135.0 0.9 shard_map.45
  135.9 6.4 %collective-permute-start.4 = (f32[768,128]{1,0:T(8,128)S(1)}, f32[768,128]{1,0:T(8,128)S(1)}, u32[]{:S(2)}, u32[]{:S(2)}) collective-permute-start(f32[768,128]{1,0:T(8,128)S(1)} %get-tuple-element.33.mine_ref), channel_id=1, source_target_pairs={{0,32},{32,0},{64,96},{96,64},{128,160},{160,128},{192,224},{224,1... | collective-permute-start | bytes 1179656 | tf_op jit(solution)/shard_map/ppermute | solution.py:323
  142.4 3.4 %all-to-all-start.6 = ((f32[8,16,128]{2,1,0:T(8,128)}), f32[8,16,128]{2,1,0:T(8,128)S(1)}, u32[]{:S(2)}, u32[]{:S(2)}) async-start(f32[8,16,128]{2,1,0:T(8,128)} %get-tuple-element.32), calls=%async_computation.6 | async-start | bytes 131072 | tf_op jit(solution)/shard_map/all_to_all | solution.py:362
  145.7 0.0 collective-permute-done.4.other_ref
  145.8 7.2 %all-to-all-done.6.x_ref = f32[8,16,128]{2,1,0:T(8,128)S(1)} async-done(((f32[8,16,128]{2,1,0:T(8,128)}), f32[8,16,128]{2,1,0:T(8,128)S(1)}, u32[]{:S(2)}, u32[]{:S(2)}) %all-to-all-start.6) | async-done | bytes 65568 | tf_op jit(solution)/shard_map/all_to_all | solution.py:362
  153.0 0.6 shard_map.47
  (10 shorter events, 0.2 us)
Async XLA Ops:
  46.8 6.6 %collective-permute-start = (f32[768,128]{1,0:T(8,128)S(1)}, f32[768,128]{1,0:T(8,128)S(1)}, u32[]{:S(2)}, u32[]{:S(2)}) collective-permute-start(f32[768,128]{1,0:T(8,128)S(1)} %get-tuple-element.21), channel_id=1, source_target_pairs={{0,32},{32,0},{64,96},{96,64},{128,160},{160,128},{192,224},{224,1... | collective-permute-start | bytes 1179656 | tf_op jit(solution)/shard_map/ppermute | solution.py:323
  53.4 37.2 %copy-start = (f32[1024,12]{0,1:T(8,128)S(1)}, f32[1024,12]{0,1:T(8,128)}, u32[]{:S(2)}) copy-start(f32[1024,12]{0,1:T(8,128)} %param.5) | copy-start | bytes 147460
  77.2 8.5 %collective-permute-start.1 = (f32[48,128]{1,0:T(8,128)S(1)}, f32[48,128]{1,0:T(8,128)S(1)}, u32[]{:S(2)}, u32[]{:S(2)}) collective-permute-start(f32[48,128]{1,0:T(8,128)S(1)} %get-tuple-element.24), channel_id=1, source_target_pairs={{0,4},{1,13},{2,38},{3,47},{4,71},{5,72},{6,97},{7,106},{8,138},{9... | collective-permute-start | bytes 73736 | tf_op jit(solution)/shard_map/ppermute | solution.py:344
  82.4 8.1 %collective-permute-start.2 = (f32[48,128]{1,0:T(8,128)S(1)}, f32[48,128]{1,0:T(8,128)S(1)}, u32[]{:S(2)}, u32[]{:S(2)}) collective-permute-start(f32[48,128]{1,0:T(8,128)S(1)} %get-tuple-element.25), channel_id=1, source_target_pairs={{0,12},{1,5},{2,46},{3,39},{4,79},{5,64},{6,105},{7,98},{8,146},{9... | collective-permute-start | bytes 73736 | tf_op jit(solution)/shard_map/ppermute | solution.py:345
  91.3 3.4 %collective-permute-start.3 = (f32[88,128]{1,0:T(8,128)S(1)}, f32[88,128]{1,0:T(8,128)S(1)}, u32[]{:S(2)}, u32[]{:S(2)}) collective-permute-start(f32[88,128]{1,0:T(8,128)S(1)} %get-tuple-element.28.mine_ref), channel_id=1, source_target_pairs={{0,32},{32,0},{64,96},{96,64},{128,160},{160,128},{192,224},{224,1... | collective-permute-start | bytes 135176 | tf_op jit(solution)/shard_map/ppermute | solution.py:323
  135.9 9.8 %collective-permute-start.4 = (f32[768,128]{1,0:T(8,128)S(1)}, f32[768,128]{1,0:T(8,128)S(1)}, u32[]{:S(2)}, u32[]{:S(2)}) collective-permute-start(f32[768,128]{1,0:T(8,128)S(1)} %get-tuple-element.33.mine_ref), channel_id=1, source_target_pairs={{0,32},{32,0},{64,96},{96,64},{128,160},{160,128},{192,224},{224,1... | collective-permute-start | bytes 1179656 | tf_op jit(solution)/shard_map/ppermute | solution.py:323
  142.4 10.6 %all-to-all-start.6 = ((f32[8,16,128]{2,1,0:T(8,128)}), f32[8,16,128]{2,1,0:T(8,128)S(1)}, u32[]{:S(2)}, u32[]{:S(2)}) async-start(f32[8,16,128]{2,1,0:T(8,128)} %get-tuple-element.32), calls=%async_computation.6 | async-start | bytes 131072 | tf_op jit(solution)/shard_map/all_to_all | solution.py:362

commit v7 on v6

--- a/solution.py
+++ b/solution.py
@@ -361,7 +361,7 @@
     )
     rows_x = lax.all_to_all(solved, "col", 0, 0, axis_index_groups=Y_GROUPS)
     corner = call(
-        corner_kernel, f32(12, PW), half, between_cores(half), fac,
+        corner_kernel, f32(12, PW), half, lax.ppermute(half, "row", [(1, 0)]), fac,
         scratch=[vmem(PW, 512), vmem(PW, PW), vmem(1536, B), vmem(48, B)],
     )
     out = call(output_kernel, f32(12, 1024), rows_x, corner)

time: 154 us -> 155 us (level)
    ppermute x0 -> x1, starting transfers between devices: none -> 6.45 us  [on_device(): lax.ppermute(half, 'row', [(1, 0)])]
    ppermute x3 -> x2, starting transfers between devices: 14.2 us -> 7.78 us  [between_cores(): return lax.ppermute(value, 'row', [(r, r ^ 1) for r in range(16)])]
where the time goes in v7:
time: 155 us; the launch traced here: 154 us
  blocking collectives  107 us (69%)
  starting transfers between devices  26.1 us (17%)
  waiting for transfers between devices  14.9 us (10%)
  Pallas kernels  5.21 us (3%)
    all_to_all x2, blocking collectives, spread(): return lax.all_to_all(copies, axis, 0, 0, axis_index_groups=groups)  43.1 us
    all_to_all x1, blocking collectives, on_device(): pieces = lax.all_to_all(both, 'row', 0, 0, axis_index_groups=Z_GROUPS)  23.7 us
    all_to_all x1, blocking collectives, on_device(): got = lax.all_to_all(out_u, 'row', 0, 0, axis_index_groups=Z_GROUPS)  16.1 us
    all_to_all x1, blocking collectives, on_device(): near = lax.all_to_all(near, 'col', 0, 0, axis_index_groups=Y_GROUPS)  14.1 us
    all_to_all x1, blocking collectives, on_device(): lax.all_to_all(wide, 'col', 0, 0, axis_index_groups=X_GROUPS)  10 us
    all_to_all x1, waiting for transfers between devices, on_device(): rows_x = lax.all_to_all(solved, 'col', 0, 0, axis_index_groups=Y_GROUPS)  7.91 us
    ppermute x2, starting transfers between devices, between_cores(): return lax.ppermute(value, 'row', [(r, r ^ 1) for r in range(16)])  7.78 us
    ppermute x1, starting transfers between devices, on_device(): lax.ppermute(half, 'row', [(1, 0)])  6.45 us
  transfers between devices with their start and end apart: 6, of which 4 were waited for; matrix products, arithmetic and copies ran while one was open for 0% of the time, Pallas kernels for 0%

profile of v7, /device:TPU:1, one launch (start us, length us, event | category | flops | bytes accessed | tf_op | source)
XLA Modules:
  0.0 154.3 jit_solution(9471240479832870799)
XLA Ops:
  0.0 0.9 broadcast_in_dim.14
  0.9 19.8 %all_to_all.35 = f32[8,96,128]{2,1,0:T(8,128)S(1)} all-to-all(f32[8,96,128]{2,1,0:T(8,128)S(1)} %broadcast_in_dim.15), channel_id=1, replica_groups={{0,1,2,3,4,5,6,7},{8,9,10,11,12,13,14,15},{16,17,18,19,20,21,22,23},{24..., dimensions={0} | all-to-all | bytes 786432 | tf_op jit(solution)/shard_map/all_to_all | solution.py:319
  20.7 0.1 broadcast_in_dim.17
  20.8 23.3 %all_to_all.36 = f32[4,768,128]{2,1,0:T(8,128)S(1)} all-to-all(f32[4,768,128]{2,1,0:T(8,128)S(1)} %broadcast_in_dim.17), channel_id=1, replica_groups={{0,8,16,24},{1,9,17,25},{2,10,18,26},{3,11,19,27},{4,12,20,28},{5,13,21..., dimensions={0} | all-to-all | bytes 3145728 | tf_op jit(solution)/shard_map/all_to_all | solution.py:319
  44.1 2.7 %shard_map.37 = (f32[768,128]{1,0:T(8,128)S(1)}, f32[768,128]{1,0:T(8,128)S(1)}, bf16[384,1024]{1,0:T(8,128)(2,1)S(1)}, bf16[384,1024]{1,0:T(8,128)(2,1)S(1)}, f32[384,384]{1,0:T(8,128)S(1)}) custom-call(f32[3072,128]{1,0:T(8,128)S(1)} %bitcast.8, f32[1024,512]{1,0:T(8,128)} %t_hbm_ref.1), custom_call_target="tpu_custom_call" | custom-call | flops 2415919104 | bytes 1572864 | tf_op jit(solution)/shard_map/pallas_call | solution.py:305
  46.8 5.2 %collective-permute-start = (f32[768,128]{1,0:T(8,128)S(1)}, f32[768,128]{1,0:T(8,128)S(1)}, u32[]{:S(2)}, u32[]{:S(2)}) collective-permute-start(f32[768,128]{1,0:T(8,128)S(1)} %get-tuple-element.21), channel_id=1, source_target_pairs={{0,32},{32,0},{64,96},{96,64},{128,160},{160,128},{192,224},{224,1... | collective-permute-start | bytes 1179656 | tf_op jit(solution)/shard_map/ppermute | solution.py:323
  52.1 1.3 collective-permute-done.b_ref
  53.4 0.1 shard_map.39
  53.4 23.7 %all_to_all.37.s_ref = f32[8,96,128]{2,1,0:T(8,128)S(1)} all-to-all(f32[8,96,128]{2,1,0:T(8,128)S(1)} %bitcast.9), channel_id=1, replica_groups={{0,64,128,192,256,320,384,448},{32,96,160,224,288,352,416,480},{1,65,12..., dimensions={0} | all-to-all | bytes 786432 | tf_op jit(solution)/shard_map/all_to_all | solution.py:339
  77.2 5.2 %collective-permute-start.1 = (f32[48,128]{1,0:T(8,128)S(1)}, f32[48,128]{1,0:T(8,128)S(1)}, u32[]{:S(2)}, u32[]{:S(2)}) collective-permute-start(f32[48,128]{1,0:T(8,128)S(1)} %get-tuple-element.24), channel_id=1, source_target_pairs={{0,4},{1,13},{2,38},{3,47},{4,71},{5,72},{6,97},{7,106},{8,138},{9... | collective-permute-start | bytes 73736 | tf_op jit(solution)/shard_map/ppermute | solution.py:344
  82.4 3.3 %collective-permute-start.2 = (f32[48,128]{1,0:T(8,128)S(1)}, f32[48,128]{1,0:T(8,128)S(1)}, u32[]{:S(2)}, u32[]{:S(2)}) collective-permute-start(f32[48,128]{1,0:T(8,128)S(1)} %get-tuple-element.25), channel_id=1, source_target_pairs={{0,12},{1,5},{2,46},{3,39},{4,79},{5,64},{6,105},{7,98},{8,146},{9... | collective-permute-start | bytes 73736 | tf_op jit(solution)/shard_map/ppermute | solution.py:345
  85.7 4.8 %collective-permute-done.2.rb_ref = f32[48,128]{1,0:T(8,128)S(1)} collective-permute-done((f32[48,128]{1,0:T(8,128)S(1)}, f32[48,128]{1,0:T(8,128)S(1)}, u32[]{:S(2)}, u32[]{:S(2)}) %collective-permute-start.2) | collective-permute-done | bytes 24608 | tf_op jit(solution)/shard_map/ppermute | solution.py:345
  90.5 0.7 shard_map.41
  91.3 2.6 %collective-permute-start.3 = (f32[88,128]{1,0:T(8,128)S(1)}, f32[88,128]{1,0:T(8,128)S(1)}, u32[]{:S(2)}, u32[]{:S(2)}) collective-permute-start(f32[88,128]{1,0:T(8,128)S(1)} %get-tuple-element.28.mine_ref), channel_id=1, source_target_pairs={{0,32},{32,0},{64,96},{96,64},{128,160},{160,128},{192,224},{224,1... | collective-permute-start | bytes 135176 | tf_op jit(solution)/shard_map/ppermute | solution.py:323
  93.8 0.9 collective-permute-done.3.other_ref
  94.7 16.1 %all_to_all.38.got_ref = f32[8,40,128]{2,1,0:T(8,128)S(1)} all-to-all(f32[8,40,128]{2,1,0:T(8,128)S(1)} %get-tuple-element.30), channel_id=1, replica_groups={{0,64,128,192,256,320,384,448},{32,96,160,224,288,352,416,480},{1,65,12..., dimensions={0} | all-to-all | bytes 327680 | tf_op jit(solution)/shard_map/all_to_all | solution.py:353
  110.8 14.1 %all_to_all.39.near_ref = f32[8,72,128]{2,1,0:T(8,128)S(1)} all-to-all(f32[8,72,128]{2,1,0:T(8,128)S(1)} %shard_map.43), channel_id=1, replica_groups={{0,1,2,3,4,5,6,7},{8,9,10,11,12,13,14,15},{16,17,18,19,20,21,22,23},{24..., dimensions={0} | all-to-all | bytes 589824 | tf_op jit(solution)/shard_map/all_to_all | solution.py:355
  125.0 10.0 %all_to_all.40 = f32[4,288,128]{2,1,0:T(8,128)S(1)} all-to-all(f32[4,288,128]{2,1,0:T(8,128)S(1)} %shard_map.44), channel_id=1, replica_groups={{0,8,16,24},{1,9,17,25},{2,10,18,26},{3,11,19,27},{4,12,20,28},{5,13,21..., dimensions={0} | all-to-all | bytes 1179648 | tf_op jit(solution)/shard_map/all_to_all | solution.py:357
  135.0 0.9 shard_map.45
  135.9 6.4 %collective-permute-start.4 = (f32[768,128]{1,0:T(8,128)S(1)}, f32[768,128]{1,0:T(8,128)S(1)}, u32[]{:S(2)}, u32[]{:S(2)}) collective-permute-start(f32[768,128]{1,0:T(8,128)S(1)} %get-tuple-element.33.mine_ref), channel_id=1, source_target_pairs={{32,0},{33,1},{34,2},{35,3},{36,4},{37,5},{38,6},{39,7},{40,8},{41... | collective-permute-start | bytes 1179656 | tf_op jit(solution)/shard_map/ppermute | solution.py:364
  142.4 3.4 %all-to-all-start.6 = ((f32[8,16,128]{2,1,0:T(8,128)}), f32[8,16,128]{2,1,0:T(8,128)S(1)}, u32[]{:S(2)}, u32[]{:S(2)}) async-start(f32[8,16,128]{2,1,0:T(8,128)} %get-tuple-element.32), calls=%async_computation.6 | async-start | bytes 131072 | tf_op jit(solution)/shard_map/all_to_all | solution.py:362
  145.7 0.0 collective-permute-done.4.other_ref
  145.8 7.9 %all-to-all-done.6.x_ref = f32[8,16,128]{2,1,0:T(8,128)S(1)} async-done(((f32[8,16,128]{2,1,0:T(8,128)}), f32[8,16,128]{2,1,0:T(8,128)S(1)}, u32[]{:S(2)}, u32[]{:S(2)}) %all-to-all-start.6) | async-done | bytes 65568 | tf_op jit(solution)/shard_map/all_to_all | solution.py:362
  153.7 0.6 shard_map.47
  (10 shorter events, 0.2 us)
Async XLA Ops:
  46.8 6.6 %collective-permute-start = (f32[768,128]{1,0:T(8,128)S(1)}, f32[768,128]{1,0:T(8,128)S(1)}, u32[]{:S(2)}, u32[]{:S(2)}) collective-permute-start(f32[768,128]{1,0:T(8,128)S(1)} %get-tuple-element.21), channel_id=1, source_target_pairs={{0,32},{32,0},{64,96},{96,64},{128,160},{160,128},{192,224},{224,1... | collective-permute-start | bytes 1179656 | tf_op jit(solution)/shard_map/ppermute | solution.py:323
  53.4 37.2 %copy-start = (f32[1024,12]{0,1:T(8,128)S(1)}, f32[1024,12]{0,1:T(8,128)}, u32[]{:S(2)}) copy-start(f32[1024,12]{0,1:T(8,128)} %param.5) | copy-start | bytes 147460
  77.2 8.5 %collective-permute-start.1 = (f32[48,128]{1,0:T(8,128)S(1)}, f32[48,128]{1,0:T(8,128)S(1)}, u32[]{:S(2)}, u32[]{:S(2)}) collective-permute-start(f32[48,128]{1,0:T(8,128)S(1)} %get-tuple-element.24), channel_id=1, source_target_pairs={{0,4},{1,13},{2,38},{3,47},{4,71},{5,72},{6,97},{7,106},{8,138},{9... | collective-permute-start | bytes 73736 | tf_op jit(solution)/shard_map/ppermute | solution.py:344
  82.4 8.1 %collective-permute-start.2 = (f32[48,128]{1,0:T(8,128)S(1)}, f32[48,128]{1,0:T(8,128)S(1)}, u32[]{:S(2)}, u32[]{:S(2)}) collective-permute-start(f32[48,128]{1,0:T(8,128)S(1)} %get-tuple-element.25), channel_id=1, source_target_pairs={{0,12},{1,5},{2,46},{3,39},{4,79},{5,64},{6,105},{7,98},{8,146},{9... | collective-permute-start | bytes 73736 | tf_op jit(solution)/shard_map/ppermute | solution.py:345
  91.3 3.4 %collective-permute-start.3 = (f32[88,128]{1,0:T(8,128)S(1)}, f32[88,128]{1,0:T(8,128)S(1)}, u32[]{:S(2)}, u32[]{:S(2)}) collective-permute-start(f32[88,128]{1,0:T(8,128)S(1)} %get-tuple-element.28.mine_ref), channel_id=1, source_target_pairs={{0,32},{32,0},{64,96},{96,64},{128,160},{160,128},{192,224},{224,1... | collective-permute-start | bytes 135176 | tf_op jit(solution)/shard_map/ppermute | solution.py:323
  135.9 9.8 %collective-permute-start.4 = (f32[768,128]{1,0:T(8,128)S(1)}, f32[768,128]{1,0:T(8,128)S(1)}, u32[]{:S(2)}, u32[]{:S(2)}) collective-permute-start(f32[768,128]{1,0:T(8,128)S(1)} %get-tuple-element.33.mine_ref), channel_id=1, source_target_pairs={{32,0},{33,1},{34,2},{35,3},{36,4},{37,5},{38,6},{39,7},{40,8},{41... | collective-permute-start | bytes 1179656 | tf_op jit(solution)/shard_map/ppermute | solution.py:364
  142.4 11.3 %all-to-all-start.6 = ((f32[8,16,128]{2,1,0:T(8,128)}), f32[8,16,128]{2,1,0:T(8,128)S(1)}, u32[]{:S(2)}, u32[]{:S(2)}) async-start(f32[8,16,128]{2,1,0:T(8,128)} %get-tuple-element.32), calls=%async_computation.6 | async-start | bytes 131072 | tf_op jit(solution)/shard_map/all_to_all | solution.py:362

commit v8 on v6

--- a/solution.py
+++ b/solution.py
@@ -30,9 +30,9 @@
     return lax.dot_general(a, b, (((1,), (1,)), ((), ())), preferred_element_type=jnp.float32)
 
 
-def place(row, col, half):
+def place(row, col):
     x, y = col // Y_SIZE, col % Y_SIZE
-    x_to, y_to = (x + 2 * (row % 2) + half) % X_SIZE, (y + row // 2 + 12 - col // 4) % Y_SIZE
+    x_to, y_to = (x + 2 * (row % 2) + y % 2) % X_SIZE, (y // 2 * 2 + row // 2 + 12 - col // 4) % Y_SIZE
     return col // 2 * (X_SIZE * Y_SIZE) + x_to * Y_SIZE + y_to
 
 
@@ -75,17 +75,24 @@
     for core, target in ((1 - row % 2, send_ref), (row % 2, keep_ref)):
         for z in range(8):
             for half in range(2):
-                x_to, y_to = (x + 2 * core + half) % X_SIZE, (y + z + 12 - col // 4) % Y_SIZE
+                x_to, y_to = (x + 2 * core + half) % X_SIZE, (y // 2 * 2 + z + 12 - col // 4) % Y_SIZE
                 first = pl.multiple_of((x_to * Y_SIZE + y_to) * 48, 16)
                 target[z * 96 + half * 48 : z * 96 + half * 48 + 48, :] = cut_ref[pl.ds(first, 48), :]
 
 
-def sum_kernel(s_ref, a_ref, b_ref):
+def sum_kernel(s_ref, keep_ref, swap_ref):
     odd = lax.axis_index("col") % 2 == 1
     low = jnp.sum(s_ref[:, 0:48, :], axis=0)
     high = jnp.sum(s_ref[:, 48:96, :], axis=0)
-    a_ref[...] = jnp.where(odd, high, low)
-    b_ref[...] = jnp.where(odd, low, high)
+    keep_ref[...] = jnp.where(odd, high, low)
+    swap_ref[...] = jnp.where(odd, low, high)
+
+
+def join_kernel(keep_ref, got_ref, out_ref):
+    odd = lax.axis_index("col") % 2 == 1
+    keep, got = keep_ref[...], got_ref[...]
+    out_ref[0:48, :] = jnp.where(odd, got, keep)
+    out_ref[48:96, :] = jnp.where(odd, keep, got)
 
 
 def corner_block(kind, i, j):
@@ -132,17 +139,13 @@
             fac_ref[corner_block("li", i, i)] = inv[i, i].T
 
 
-def gram_kernel(ra_ref, rb_ref, g_ref, fh_ref, fl_ref, litp_ref, pay_ref, y_ref, half_ref, ym_ref, own_ref):
+def gram_kernel(tc_ref, g_ref, fh_ref, fl_ref, litp_ref, pay_ref, y_ref, ym_ref, own_ref):
     row, col = lax.axis_index("row"), lax.axis_index("col")
-    first = (col // Y_SIZE + row // 4) % 2 == 0
-    ra, rb = ra_ref[...], rb_ref[...]
-    half_ref[0:48, :] = jnp.where(first, ra, rb)
-    half_ref[48:96, :] = jnp.where(first, rb, ra)
     panel = (12 * col + lax.broadcasted_iota(jnp.int32, (12, B), 0)) // B
     top, diag = [], jnp.zeros((12, B), jnp.float32)
     for b in range(8):
         g = g_ref[:, b * B : (b + 1) * B]
-        y = g - 2.0 * half_ref[pl.ds(b // 4 * 48 + b % 4, 12, stride=4), :]
+        y = g - 2.0 * tc_ref[pl.ds(b // 4 * 48 + b % 4, 12, stride=4), :]
         y_ref[b, 0:12, :] = y
         y_ref[b, 12:16, :] = jnp.zeros((4, B), jnp.float32)
         if b < STEPS:
@@ -261,7 +264,12 @@
             out_ref[x, 192 + 12 * y : 192 + 12 * (y + 1), :] = near_ref[y, 60:72, :]
 
 
-def solve_kernel(near_ref, w_ref, out_ref, half_ref, yt_ref, lit_ref):
+def half_kernel(w_ref, _, half_ref):
+    for x in range(X_SIZE):
+        half_ref[192 * x : 192 * (x + 1), :] = w_ref[288 * x : 288 * x + 192, :]
+
+
+def solve_kernel(near_ref, w_ref, out_ref, yt_ref, lit_ref):
     for x in range(X_SIZE):
         yt_ref[96 * x : 96 * (x + 1), :] = w_ref[288 * x + 192 : 288 * (x + 1), :]
     for y in range(Y_SIZE):
@@ -269,12 +277,12 @@
             lit_ref[12 * y : 12 * (y + 1), k * B : (k + 1) * B] = near_ref[
                 y, pl.ds(24 + k, 12, stride=3), :
             ]
-    yt_ref[0:96, :] = 0.5 * dot(lit_ref[...], yt_ref[...])
+    lh, ll = split(lit_ref[...])
+    yh, yl = split(yt_ref[...])
+    yt_ref[0:96, :] = 0.5 * (dot_bf16(lh, yl) + dot_bf16(ll, yh) + dot_bf16(lh, yh))
     for y in range(Y_SIZE):
         out_ref[y, 0:12, :] = yt_ref[12 * y : 12 * (y + 1), :]
         out_ref[y, 12:16, :] = jnp.zeros((4, B), jnp.float32)
-    for x in range(X_SIZE):
-        half_ref[192 * x : 192 * (x + 1), :] = w_ref[288 * x : 288 * x + 192, :]
 
 
 def output_kernel(x_ref, corner_ref, out_ref):
@@ -337,15 +345,14 @@
     )
     both = call(add_kernel, f32(768, B), keep, between_cores(send), after=[inv_tp]).reshape(8, 96, B)
     pieces = lax.all_to_all(both, "row", 0, 0, axis_index_groups=Z_GROUPS)
-    send_a, send_b = call(sum_kernel, [f32(48, B), f32(48, B)], pieces)
-    devices = [(r, c) for r in range(16) for c in range(32)]
-    to_a = [(r * 32 + c, place(r, c, c % 2)) for r, c in devices]
-    to_b = [(r * 32 + c, place(r, c, 1 - c % 2)) for r, c in devices]
-    got_a = lax.ppermute(send_a, ("row", "col"), to_a)
-    got_b = lax.ppermute(send_b, ("row", "col"), to_b)
+    keep, swap = call(sum_kernel, [f32(48, B), f32(48, B)], pieces)
+    swapped = lax.ppermute(swap, "col", [(c, c ^ 1) for c in range(32)])
+    product = call(join_kernel, f32(96, B), keep, swapped)
+    moves = [(r * 32 + c, place(r, c)) for r in range(16) for c in range(32)]
+    product = lax.ppermute(product, ("row", "col"), moves)
     payload, own_y = call(
-        gram_kernel, [f32(88, B), f32(8, 16, B)], got_a, got_b, factor_adj.T, panel_high, panel_low, inv_tp,
-        scratch=[vmem(96, B), vmem(12, 1024), vmem(48, B)], flops=12 * 12 * 1024 * PW,
+        gram_kernel, [f32(88, B), f32(8, 16, B)], product, factor_adj.T, panel_high, panel_low, inv_tp,
+        scratch=[vmem(12, 1024), vmem(48, B)], flops=12 * 12 * 1024 * PW,
     )
     out_u, sum_u = call(
         route_kernel, [f32(8, 40, B), f32(88, B)], payload, between_cores(payload),
@@ -355,10 +362,11 @@
     near = lax.all_to_all(near, "col", 0, 0, axis_index_groups=Y_GROUPS)
     wide = call(pack_x_kernel, f32(4, 288, B), near)
     wide = lax.all_to_all(wide, "col", 0, 0, axis_index_groups=X_GROUPS).reshape(4 * 288, B)
-    solved, half = call(
-        solve_kernel, [f32(8, 16, B), f32(768, B)], near, wide,
+    solved = call(
+        solve_kernel, f32(8, 16, B), near, wide,
         scratch=[vmem(PW, B), vmem(96, PW)], flops=12 * 96 * B * PW,
     )
+    half = call(half_kernel, f32(768, B), wide, after=[solved], flops=10**10)
     rows_x = lax.all_to_all(solved, "col", 0, 0, axis_index_groups=Y_GROUPS)
     corner = call(
         corner_kernel, f32(12, PW), half, between_cores(half), fac,

time: 154 us -> 154 us (level)
  blocking collectives: 107 us -> 103 us
  starting transfers between devices: 26.1 us -> 29.9 us
    ppermute x3, starting transfers between devices: 14.2 us -> 18.3 us  [between_cores(): return lax.ppermute(value, 'row', [(r, r ^ 1) for r in range(16)])]
    all_to_all x1, blocking collectives: 16.1 us -> 12.7 us  [on_device(): got = lax.all_to_all(out_u, 'row', 0, 0, axis_index_groups=Z_GROUPS)]
    pallas_call x11 -> x13, Pallas kernels: 5.21 us -> 5.15 us  [call(): pl.pallas_call(kernel, out_shape=out_shape, in_specs=[spec] * len(args) +...]
  transfers between devices with their start and end apart: 6 -> 6, of which waited for: 4 -> 5; matrix products, arithmetic and copies ran while one was open for 0% -> 0% of each run, Pallas kernels for 0% -> 0%
where the time goes in v8:
time: 154 us; the launch traced here: 153 us
  blocking collectives  103 us (67%)
  starting transfers between devices  29.9 us (19%)
  waiting for transfers between devices  14 us (9%)
  Pallas kernels  5.15 us (3%)
    all_to_all x2, blocking collectives, spread(): return lax.all_to_all(copies, axis, 0, 0, axis_index_groups=groups)  43.1 us
    all_to_all x1, blocking collectives, on_device(): pieces = lax.all_to_all(both, 'row', 0, 0, axis_index_groups=Z_GROUPS)  23.7 us
    ppermute x3, starting transfers between devices, between_cores(): return lax.ppermute(value, 'row', [(r, r ^ 1) for r in range(16)])  18.3 us
    all_to_all x1, blocking collectives, on_device(): near = lax.all_to_all(near, 'col', 0, 0, axis_index_groups=Y_GROUPS)  13 us
    all_to_all x1, blocking collectives, on_device(): got = lax.all_to_all(out_u, 'row', 0, 0, axis_index_groups=Z_GROUPS)  12.7 us
    all_to_all x1, blocking collectives, on_device(): lax.all_to_all(wide, 'col', 0, 0, axis_index_groups=X_GROUPS)  10.7 us
    all_to_all x1, waiting for transfers between devices, on_device(): rows_x = lax.all_to_all(solved, 'col', 0, 0, axis_index_groups=Y_GROUPS)  7.24 us
    ppermute x1, starting transfers between devices, on_device(): product = lax.ppermute(product, ('row', 'col'), moves)  6.34 us
  transfers between devices with their start and end apart: 6, of which 5 were waited for; matrix products, arithmetic and copies ran while one was open for 0% of the time, Pallas kernels for 0%

profile of v8, /device:TPU:1, one launch (start us, length us, event | category | flops | bytes accessed | tf_op | source)
XLA Modules:
  0.0 153.3 jit_solution(16774029977334440210)
XLA Ops:
  0.0 0.9 broadcast_in_dim.14
  0.9 19.8 %all_to_all.35 = f32[8,96,128]{2,1,0:T(8,128)S(1)} all-to-all(f32[8,96,128]{2,1,0:T(8,128)S(1)} %broadcast_in_dim.15), channel_id=1, replica_groups={{0,1,2,3,4,5,6,7},{8,9,10,11,12,13,14,15},{16,17,18,19,20,21,22,23},{24..., dimensions={0} | all-to-all | bytes 786432 | tf_op jit(solution)/shard_map/all_to_all | solution.py:327
  20.7 0.1 broadcast_in_dim.17
  20.8 23.3 %all_to_all.36 = f32[4,768,128]{2,1,0:T(8,128)S(1)} all-to-all(f32[4,768,128]{2,1,0:T(8,128)S(1)} %broadcast_in_dim.17), channel_id=1, replica_groups={{0,8,16,24},{1,9,17,25},{2,10,18,26},{3,11,19,27},{4,12,20,28},{5,13,21..., dimensions={0} | all-to-all | bytes 3145728 | tf_op jit(solution)/shard_map/all_to_all | solution.py:327
  44.1 2.7 %shard_map.37 = (f32[768,128]{1,0:T(8,128)S(1)}, f32[768,128]{1,0:T(8,128)S(1)}, bf16[384,1024]{1,0:T(8,128)(2,1)S(1)}, bf16[384,1024]{1,0:T(8,128)(2,1)S(1)}, f32[384,384]{1,0:T(8,128)S(1)}) custom-call(f32[3072,128]{1,0:T(8,128)S(1)} %bitcast.9, f32[1024,512]{1,0:T(8,128)} %t_hbm_ref.1), custom_call_target="tpu_custom_call" | custom-call | flops 2415919104 | bytes 1572864 | tf_op jit(solution)/shard_map/pallas_call | solution.py:313
  46.8 5.2 %collective-permute-start = (f32[768,128]{1,0:T(8,128)S(1)}, f32[768,128]{1,0:T(8,128)S(1)}, u32[]{:S(2)}, u32[]{:S(2)}) collective-permute-start(f32[768,128]{1,0:T(8,128)S(1)} %get-tuple-element.19), channel_id=1, source_target_pairs={{0,32},{32,0},{64,96},{96,64},{128,160},{160,128},{192,224},{224,1... | collective-permute-start | bytes 1179656 | tf_op jit(solution)/shard_map/ppermute | solution.py:331
  52.1 1.3 collective-permute-done.b_ref
  53.4 0.1 shard_map.39
  53.4 23.7 %all_to_all.37.s_ref = f32[8,96,128]{2,1,0:T(8,128)S(1)} all-to-all(f32[8,96,128]{2,1,0:T(8,128)S(1)} %bitcast.10), channel_id=1, replica_groups={{0,64,128,192,256,320,384,448},{32,96,160,224,288,352,416,480},{1,65,12..., dimensions={0} | all-to-all | bytes 786432 | tf_op jit(solution)/shard_map/all_to_all | solution.py:347
  77.2 1.9 %collective-permute-start.1 = (f32[48,128]{1,0:T(8,128)S(1)}, f32[48,128]{1,0:T(8,128)S(1)}, u32[]{:S(2)}, u32[]{:S(2)}) collective-permute-start(f32[48,128]{1,0:T(8,128)S(1)} %get-tuple-element.23), channel_id=1, source_target_pairs={{0,1},{1,0},{2,3},{3,2},{4,5},{5,4},{6,7},{7,6},{8,9},{9,8},{10,11... | collective-permute-start | bytes 73736 | tf_op jit(solution)/shard_map/ppermute | solution.py:349
  79.1 2.6 %collective-permute-done.1.got_ref = f32[48,128]{1,0:T(8,128)S(1)} collective-permute-done((f32[48,128]{1,0:T(8,128)S(1)}, f32[48,128]{1,0:T(8,128)S(1)}, u32[]{:S(2)}, u32[]{:S(2)}) %collective-permute-start.1) | collective-permute-done | bytes 24608 | tf_op jit(solution)/shard_map/ppermute | solution.py:349
  81.8 6.3 %collective-permute-start.2 = (f32[96,128]{1,0:T(8,128)S(1)}, f32[96,128]{1,0:T(8,128)S(1)}, u32[]{:S(2)}, u32[]{:S(2)}) collective-permute-start(f32[96,128]{1,0:T(8,128)S(1)} %shard_map.41), channel_id=1, source_target_pairs={{0,4},{1,12},{2,38},{3,46},{4,71},{5,79},{6,97},{7,105},{8,138},{9... | collective-permute-start | bytes 147464 | tf_op jit(solution)/shard_map/ppermute | solution.py:352
  88.1 2.0 %collective-permute-done.2.tc_ref = f32[96,128]{1,0:T(8,128)S(1)} collective-permute-done((f32[96,128]{1,0:T(8,128)S(1)}, f32[96,128]{1,0:T(8,128)S(1)}, u32[]{:S(2)}, u32[]{:S(2)}) %collective-permute-start.2) | collective-permute-done | bytes 49184 | tf_op jit(solution)/shard_map/ppermute | solution.py:352
  90.1 0.7 shard_map.42
  90.8 6.6 %collective-permute-start.3 = (f32[88,128]{1,0:T(8,128)S(1)}, f32[88,128]{1,0:T(8,128)S(1)}, u32[]{:S(2)}, u32[]{:S(2)}) collective-permute-start(f32[88,128]{1,0:T(8,128)S(1)} %get-tuple-element.26.mine_ref), channel_id=1, source_target_pairs={{0,32},{32,0},{64,96},{96,64},{128,160},{160,128},{192,224},{224,1... | collective-permute-start | bytes 135176 | tf_op jit(solution)/shard_map/ppermute | solution.py:331
  97.4 0.9 collective-permute-done.3.other_ref
  98.3 12.7 %all_to_all.38.got_ref = f32[8,40,128]{2,1,0:T(8,128)S(1)} all-to-all(f32[8,40,128]{2,1,0:T(8,128)S(1)} %get-tuple-element.28), channel_id=1, replica_groups={{0,64,128,192,256,320,384,448},{32,96,160,224,288,352,416,480},{1,65,12..., dimensions={0} | all-to-all | bytes 327680 | tf_op jit(solution)/shard_map/all_to_all | solution.py:360
  111.0 13.0 %all_to_all.39.near_ref = f32[8,72,128]{2,1,0:T(8,128)S(1)} all-to-all(f32[8,72,128]{2,1,0:T(8,128)S(1)} %shard_map.44), channel_id=1, replica_groups={{0,1,2,3,4,5,6,7},{8,9,10,11,12,13,14,15},{16,17,18,19,20,21,22,23},{24..., dimensions={0} | all-to-all | bytes 589824 | tf_op jit(solution)/shard_map/all_to_all | solution.py:362
  124.0 10.7 %all_to_all.40 = f32[4,288,128]{2,1,0:T(8,128)S(1)} all-to-all(f32[4,288,128]{2,1,0:T(8,128)S(1)} %shard_map.45), channel_id=1, replica_groups={{0,8,16,24},{1,9,17,25},{2,10,18,26},{3,11,19,27},{4,12,20,28},{5,13,21..., dimensions={0} | all-to-all | bytes 1179648 | tf_op jit(solution)/shard_map/all_to_all | solution.py:364
  134.7 0.9 shard_map.46._
  135.6 6.4 %collective-permute-start.4 = (f32[768,128]{1,0:T(8,128)S(1)}, f32[768,128]{1,0:T(8,128)S(1)}, u32[]{:S(2)}, u32[]{:S(2)}) collective-permute-start(f32[768,128]{1,0:T(8,128)S(1)} %shard_map.47.mine_ref), channel_id=1, source_target_pairs={{0,32},{32,0},{64,96},{96,64},{128,160},{160,128},{192,224},{224,1... | collective-permute-start | bytes 1179656 | tf_op jit(solution)/shard_map/ppermute | solution.py:331
  142.1 3.4 %all-to-all-start.6 = ((f32[8,16,128]{2,1,0:T(8,128)}), f32[8,16,128]{2,1,0:T(8,128)S(1)}, u32[]{:S(2)}, u32[]{:S(2)}) async-start(f32[8,16,128]{2,1,0:T(8,128)} %shard_map.46._), calls=%async_computation.6 | async-start | bytes 131072 | tf_op jit(solution)/shard_map/all_to_all | solution.py:370
  145.5 7.2 %all-to-all-done.6.x_ref = f32[8,16,128]{2,1,0:T(8,128)S(1)} async-done(((f32[8,16,128]{2,1,0:T(8,128)}), f32[8,16,128]{2,1,0:T(8,128)S(1)}, u32[]{:S(2)}, u32[]{:S(2)}) %all-to-all-start.6) | async-done | bytes 65568 | tf_op jit(solution)/shard_map/all_to_all | solution.py:370
  152.7 0.6 shard_map.49
  (12 shorter events, 0.2 us)
Async XLA Ops:
  46.8 6.6 %collective-permute-start = (f32[768,128]{1,0:T(8,128)S(1)}, f32[768,128]{1,0:T(8,128)S(1)}, u32[]{:S(2)}, u32[]{:S(2)}) collective-permute-start(f32[768,128]{1,0:T(8,128)S(1)} %get-tuple-element.19), channel_id=1, source_target_pairs={{0,32},{32,0},{64,96},{96,64},{128,160},{160,128},{192,224},{224,1... | collective-permute-start | bytes 1179656 | tf_op jit(solution)/shard_map/ppermute | solution.py:331
  53.4 36.7 %copy-start = (f32[1024,12]{0,1:T(8,128)S(1)}, f32[1024,12]{0,1:T(8,128)}, u32[]{:S(2)}) copy-start(f32[1024,12]{0,1:T(8,128)} %param.5) | copy-start | bytes 147460
  77.2 4.6 %collective-permute-start.1 = (f32[48,128]{1,0:T(8,128)S(1)}, f32[48,128]{1,0:T(8,128)S(1)}, u32[]{:S(2)}, u32[]{:S(2)}) collective-permute-start(f32[48,128]{1,0:T(8,128)S(1)} %get-tuple-element.23), channel_id=1, source_target_pairs={{0,1},{1,0},{2,3},{3,2},{4,5},{5,4},{6,7},{7,6},{8,9},{9,8},{10,11... | collective-permute-start | bytes 73736 | tf_op jit(solution)/shard_map/ppermute | solution.py:349
  81.8 8.3 %collective-permute-start.2 = (f32[96,128]{1,0:T(8,128)S(1)}, f32[96,128]{1,0:T(8,128)S(1)}, u32[]{:S(2)}, u32[]{:S(2)}) collective-permute-start(f32[96,128]{1,0:T(8,128)S(1)} %shard_map.41), channel_id=1, source_target_pairs={{0,4},{1,12},{2,38},{3,46},{4,71},{5,79},{6,97},{7,105},{8,138},{9... | collective-permute-start | bytes 147464 | tf_op jit(solution)/shard_map/ppermute | solution.py:352
  90.8 7.5 %collective-permute-start.3 = (f32[88,128]{1,0:T(8,128)S(1)}, f32[88,128]{1,0:T(8,128)S(1)}, u32[]{:S(2)}, u32[]{:S(2)}) collective-permute-start(f32[88,128]{1,0:T(8,128)S(1)} %get-tuple-element.26.mine_ref), channel_id=1, source_target_pairs={{0,32},{32,0},{64,96},{96,64},{128,160},{160,128},{192,224},{224,1... | collective-permute-start | bytes 135176 | tf_op jit(solution)/shard_map/ppermute | solution.py:331
  135.6 9.8 %collective-permute-start.4 = (f32[768,128]{1,0:T(8,128)S(1)}, f32[768,128]{1,0:T(8,128)S(1)}, u32[]{:S(2)}, u32[]{:S(2)}) collective-permute-start(f32[768,128]{1,0:T(8,128)S(1)} %shard_map.47.mine_ref), channel_id=1, source_target_pairs={{0,32},{32,0},{64,96},{96,64},{128,160},{160,128},{192,224},{224,1... | collective-permute-start | bytes 1179656 | tf_op jit(solution)/shard_map/ppermute | solution.py:331
  142.1 10.6 %all-to-all-start.6 = ((f32[8,16,128]{2,1,0:T(8,128)}), f32[8,16,128]{2,1,0:T(8,128)S(1)}, u32[]{:S(2)}, u32[]{:S(2)}) async-start(f32[8,16,128]{2,1,0:T(8,128)} %shard_map.46._), calls=%async_computation.6 | async-start | bytes 131072 | tf_op jit(solution)/shard_map/all_to_all | solution.py:370

commit v9 on v8

--- a/solution.py
+++ b/solution.py
@@ -45,8 +45,29 @@
     out_ref[...] = a_ref[...] + b_ref[...]
 
 
+def half_product(core, fh_ref, fl_ref, th_ref, tl_ref, target, acc_ref, cut_ref, ready):
+    col = lax.axis_index("col")
+    x, y = col // Y_SIZE, col % Y_SIZE
+    firsts = [pl.multiple_of((x + 2 * core + half) % X_SIZE * 96, 32) for half in range(2)]
+    for q in range(4):
+        part = pl.ds(256 * q, 256)
+        ready(q, part)
+        fh = jnp.concatenate([fh_ref[pl.ds(first, 96), part] for first in firsts], axis=0)
+        fl = jnp.concatenate([fl_ref[pl.ds(first, 96), part] for first in firsts], axis=0)
+        th, tl = th_ref[part, :], tl_ref[part, :]
+        term = dot_bf16(fh, tl) + dot_bf16(fl, th) + dot_bf16(fh, th)
+        acc_ref[...] = term if q == 0 else acc_ref[...] + term
+    for b in range(4):
+        cut_ref[pl.ds(b, PW // 2, stride=4), :] = acc_ref[:, b * B : (b + 1) * B]
+    for z in range(8):
+        for half in range(2):
+            y_to = (y // 2 * 2 + z + 12 - col // 4) % Y_SIZE
+            first = pl.multiple_of(half * 384 + y_to * 48, 16)
+            target[z * 96 + half * 48 : z * 96 + half * 48 + 48, :] = cut_ref[pl.ds(first, 48), :]
+
+
 def product_kernel(
-    f_ref, t_hbm_ref, send_ref, keep_ref, fh_ref, fl_ref, top_ref, acc_ref, cut_ref, t_ref, sems
+    f_ref, t_hbm_ref, send_ref, fh_ref, fl_ref, top_ref, th_ref, tl_ref, acc_ref, cut_ref, t_ref, sems
 ):
     parts = [pl.ds(256 * q, 256) for q in range(4)]
     copies = [
@@ -64,20 +85,17 @@
             top_ref[:, b * B : (b + 1) * B] = part
             part = jnp.where((row > 0) | (panel < b), part, 0.0)
         fh_ref[:, b * B : (b + 1) * B], fl_ref[:, b * B : (b + 1) * B] = split(part)
-    for q, part in enumerate(parts):
+
+    def ready(q, part):
         copies[q].wait()
-        fh, fl = fh_ref[:, part], fl_ref[:, part]
-        th, tl = split(t_ref[part, :])
-        term = dot_bf16(fh, tl) + dot_bf16(fl, th) + dot_bf16(fh, th)
-        acc_ref[...] = term if q == 0 else acc_ref[...] + term
-    for b in range(4):
-        cut_ref[pl.ds(b, PW, stride=4), :] = acc_ref[:, b * B : (b + 1) * B]
-    for core, target in ((1 - row % 2, send_ref), (row % 2, keep_ref)):
-        for z in range(8):
-            for half in range(2):
-                x_to, y_to = (x + 2 * core + half) % X_SIZE, (y // 2 * 2 + z + 12 - col // 4) % Y_SIZE
-                first = pl.multiple_of((x_to * Y_SIZE + y_to) * 48, 16)
-                target[z * 96 + half * 48 : z * 96 + half * 48 + 48, :] = cut_ref[pl.ds(first, 48), :]
+        th_ref[part, :], tl_ref[part, :] = split(t_ref[part, :])
+
+    half_product(1 - row % 2, fh_ref, fl_ref, th_ref, tl_ref, send_ref, acc_ref, cut_ref, ready)
+
+
+def keep_kernel(fh_ref, fl_ref, th_ref, tl_ref, keep_ref, acc_ref, cut_ref):
+    core = lax.axis_index("row") % 2
+    half_product(core, fh_ref, fl_ref, th_ref, tl_ref, keep_ref, acc_ref, cut_ref, lambda q, part: None)
 
 
 def sum_kernel(s_ref, keep_ref, swap_ref):
@@ -335,10 +353,16 @@
     factor = factor_panels.T.reshape(96, B)
     near = spread(factor, "col", Y_GROUPS).reshape(Y_SIZE * 96, B)
     panels = spread(near, "col", X_GROUPS).reshape(PW * 8, B)
-    send, keep, panel_high, panel_low, ft_corner = call(
-        product_kernel, [f32(768, B), f32(768, B), bf16(PW, 1024), bf16(PW, 1024), f32(PW, PW)], panels,
-        scratch=[vmem(PW, 512), vmem(1536, B), vmem(1024, 512), pltpu.SemaphoreType.DMA((4,))],
-        after=[trail_adj], flops=12 * 1024 * 512 * PW,
+    send, panel_high, panel_low, ft_corner, trail_high, trail_low = call(
+        product_kernel,
+        [f32(768, B), bf16(PW, 1024), bf16(PW, 1024), f32(PW, PW), bf16(1024, 512), bf16(1024, 512)],
+        panels,
+        scratch=[vmem(PW // 2, 512), vmem(768, B), vmem(1024, 512), pltpu.SemaphoreType.DMA((4,))],
+        after=[trail_adj], flops=6 * 1024 * 512 * PW,
+    )
+    keep = call(
+        keep_kernel, f32(768, B), panel_high, panel_low, trail_high, trail_low,
+        scratch=[vmem(PW // 2, 512), vmem(768, B)], flops=6 * 1024 * 512 * PW,
     )
     fac, inv_tp = call(
         inverse_kernel, [f32(15 * B, B), f32(1536, B)], ft_corner, flops=12 * 60 * B**3,

time: 154 us -> 153 us (level)
    pallas_call x13 -> x14, Pallas kernels: 5.15 us -> 5.34 us  [call(): pl.pallas_call(kernel, out_shape=out_shape, in_specs=[spec] * len(args) +...]
  transfers between devices with their start and end apart: 6 -> 6, of which waited for: 5 -> 5; matrix products, arithmetic and copies ran while one was open for 0% -> 0% of each run, Pallas kernels for 0% -> 1%
where the time goes in v9:
time: 153 us
  blocking collectives  103 us (67%)
  starting transfers between devices  29.9 us (20%)
  waiting for transfers between devices  13.2 us (9%)
  Pallas kernels  5.34 us (3%)
    all_to_all x2, blocking collectives, spread(): return lax.all_to_all(copies, axis, 0, 0, axis_index_groups=groups)  43.1 us
    all_to_all x1, blocking collectives, on_device(): pieces = lax.all_to_all(both, 'row', 0, 0, axis_index_groups=Z_GROUPS)  23.7 us
    ppermute x3, starting transfers between devices, between_cores(): return lax.ppermute(value, 'row', [(r, r ^ 1) for r in range(16)])  18.3 us
    all_to_all x1, blocking collectives, on_device(): near = lax.all_to_all(near, 'col', 0, 0, axis_index_groups=Y_GROUPS)  13 us
    all_to_all x1, blocking collectives, on_device(): got = lax.all_to_all(out_u, 'row', 0, 0, axis_index_groups=Z_GROUPS)  12.7 us
    all_to_all x1, blocking collectives, on_device(): lax.all_to_all(wide, 'col', 0, 0, axis_index_groups=X_GROUPS)  10.7 us
    all_to_all x1, waiting for transfers between devices, on_device(): rows_x = lax.all_to_all(solved, 'col', 0, 0, axis_index_groups=Y_GROUPS)  7.24 us
    ppermute x1, starting transfers between devices, on_device(): product = lax.ppermute(product, ('row', 'col'), moves)  6.35 us
  transfers between devices with their start and end apart: 6, of which 5 were waited for; matrix products, arithmetic and copies ran while one was open for 0% of the time, Pallas kernels for 1%

profile of v9, /device:TPU:1, one launch (start us, length us, event | category | flops | bytes accessed | tf_op | source)
XLA Modules:
  0.0 152.7 jit_solution(1607938908925428984)
XLA Ops:
  0.0 0.9 broadcast_in_dim.14
  0.9 19.8 %all_to_all.35 = f32[8,96,128]{2,1,0:T(8,128)S(1)} all-to-all(f32[8,96,128]{2,1,0:T(8,128)S(1)} %broadcast_in_dim.15), channel_id=1, replica_groups={{0,1,2,3,4,5,6,7},{8,9,10,11,12,13,14,15},{16,17,18,19,20,21,22,23},{24..., dimensions={0} | all-to-all | bytes 786432 | tf_op jit(solution)/shard_map/all_to_all | solution.py:345
  20.7 0.1 broadcast_in_dim.17
  20.8 23.3 %all_to_all.36 = f32[4,768,128]{2,1,0:T(8,128)S(1)} all-to-all(f32[4,768,128]{2,1,0:T(8,128)S(1)} %broadcast_in_dim.17), channel_id=1, replica_groups={{0,8,16,24},{1,9,17,25},{2,10,18,26},{3,11,19,27},{4,12,20,28},{5,13,21..., dimensions={0} | all-to-all | bytes 3145728 | tf_op jit(solution)/shard_map/all_to_all | solution.py:345
  44.1 2.1 %shard_map.37 = (f32[768,128]{1,0:T(8,128)S(1)}, bf16[384,1024]{1,0:T(8,128)(2,1)S(1)}, bf16[384,1024]{1,0:T(8,128)(2,1)S(1)}, f32[384,384]{1,0:T(8,128)S(1)}, b...) custom-call(f32[3072,128]{1,0:T(8,128)S(1)} %bitcast.9, f32[1024,512]{1,0:T(8,128)} %t_hbm_ref.1), custom_call_target="tpu_custom_call" | custom-call | flops 1207959552 | bytes 1572864 | tf_op jit(solution)/shard_map/pallas_call | solution.py:331
  46.2 5.2 %collective-permute-start = (f32[768,128]{1,0:T(8,128)S(1)}, f32[768,128]{1,0:T(8,128)S(1)}, u32[]{:S(2)}, u32[]{:S(2)}) collective-permute-start(f32[768,128]{1,0:T(8,128)S(1)} %get-tuple-element.23), channel_id=1, source_target_pairs={{0,32},{32,0},{64,96},{96,64},{128,160},{160,128},{192,224},{224,1... | collective-permute-start | bytes 1179656 | tf_op jit(solution)/shard_map/ppermute | solution.py:349
  51.5 0.8 shard_map.38.a_ref
  52.3 0.5 collective-permute-done.b_ref
  52.8 23.7 %all_to_all.37.s_ref = f32[8,96,128]{2,1,0:T(8,128)S(1)} all-to-all(f32[8,96,128]{2,1,0:T(8,128)S(1)} %bitcast.10), channel_id=1, replica_groups={{0,64,128,192,256,320,384,448},{32,96,160,224,288,352,416,480},{1,65,12..., dimensions={0} | all-to-all | bytes 786432 | tf_op jit(solution)/shard_map/all_to_all | solution.py:371
  76.6 1.9 %collective-permute-start.1 = (f32[48,128]{1,0:T(8,128)S(1)}, f32[48,128]{1,0:T(8,128)S(1)}, u32[]{:S(2)}, u32[]{:S(2)}) collective-permute-start(f32[48,128]{1,0:T(8,128)S(1)} %get-tuple-element.27), channel_id=1, source_target_pairs={{0,1},{1,0},{2,3},{3,2},{4,5},{5,4},{6,7},{7,6},{8,9},{9,8},{10,11... | collective-permute-start | bytes 73736 | tf_op jit(solution)/shard_map/ppermute | solution.py:373
  78.5 2.6 %collective-permute-done.1.got_ref = f32[48,128]{1,0:T(8,128)S(1)} collective-permute-done((f32[48,128]{1,0:T(8,128)S(1)}, f32[48,128]{1,0:T(8,128)S(1)}, u32[]{:S(2)}, u32[]{:S(2)}) %collective-permute-start.1) | collective-permute-done | bytes 24608 | tf_op jit(solution)/shard_map/ppermute | solution.py:373
  81.2 6.4 %collective-permute-start.2 = (f32[96,128]{1,0:T(8,128)S(1)}, f32[96,128]{1,0:T(8,128)S(1)}, u32[]{:S(2)}, u32[]{:S(2)}) collective-permute-start(f32[96,128]{1,0:T(8,128)S(1)} %shard_map.42), channel_id=1, source_target_pairs={{0,4},{1,12},{2,38},{3,46},{4,71},{5,79},{6,97},{7,105},{8,138},{9... | collective-permute-start | bytes 147464 | tf_op jit(solution)/shard_map/ppermute | solution.py:376
  87.5 2.0 %collective-permute-done.2.tc_ref = f32[96,128]{1,0:T(8,128)S(1)} collective-permute-done((f32[96,128]{1,0:T(8,128)S(1)}, f32[96,128]{1,0:T(8,128)S(1)}, u32[]{:S(2)}, u32[]{:S(2)}) %collective-permute-start.2) | collective-permute-done | bytes 49184 | tf_op jit(solution)/shard_map/ppermute | solution.py:376
  89.5 0.7 shard_map.43
  90.2 6.6 %collective-permute-start.3 = (f32[88,128]{1,0:T(8,128)S(1)}, f32[88,128]{1,0:T(8,128)S(1)}, u32[]{:S(2)}, u32[]{:S(2)}) collective-permute-start(f32[88,128]{1,0:T(8,128)S(1)} %get-tuple-element.28.mine_ref), channel_id=1, source_target_pairs={{0,32},{32,0},{64,96},{96,64},{128,160},{160,128},{192,224},{224,1... | collective-permute-start | bytes 135176 | tf_op jit(solution)/shard_map/ppermute | solution.py:349
  96.8 0.9 collective-permute-done.3.other_ref
  97.7 12.7 %all_to_all.38.got_ref = f32[8,40,128]{2,1,0:T(8,128)S(1)} all-to-all(f32[8,40,128]{2,1,0:T(8,128)S(1)} %get-tuple-element.30), channel_id=1, replica_groups={{0,64,128,192,256,320,384,448},{32,96,160,224,288,352,416,480},{1,65,12..., dimensions={0} | all-to-all | bytes 327680 | tf_op jit(solution)/shard_map/all_to_all | solution.py:384
  110.4 13.0 %all_to_all.39.near_ref = f32[8,72,128]{2,1,0:T(8,128)S(1)} all-to-all(f32[8,72,128]{2,1,0:T(8,128)S(1)} %shard_map.45), channel_id=1, replica_groups={{0,1,2,3,4,5,6,7},{8,9,10,11,12,13,14,15},{16,17,18,19,20,21,22,23},{24..., dimensions={0} | all-to-all | bytes 589824 | tf_op jit(solution)/shard_map/all_to_all | solution.py:386
  123.4 10.7 %all_to_all.40 = f32[4,288,128]{2,1,0:T(8,128)S(1)} all-to-all(f32[4,288,128]{2,1,0:T(8,128)S(1)} %shard_map.46), channel_id=1, replica_groups={{0,8,16,24},{1,9,17,25},{2,10,18,26},{3,11,19,27},{4,12,20,28},{5,13,21..., dimensions={0} | all-to-all | bytes 1179648 | tf_op jit(solution)/shard_map/all_to_all | solution.py:388
  134.1 0.9 shard_map.47._
  135.0 6.4 %collective-permute-start.4 = (f32[768,128]{1,0:T(8,128)S(1)}, f32[768,128]{1,0:T(8,128)S(1)}, u32[]{:S(2)}, u32[]{:S(2)}) collective-permute-start(f32[768,128]{1,0:T(8,128)S(1)} %shard_map.48.mine_ref), channel_id=1, source_target_pairs={{0,32},{32,0},{64,96},{96,64},{128,160},{160,128},{192,224},{224,1... | collective-permute-start | bytes 1179656 | tf_op jit(solution)/shard_map/ppermute | solution.py:349
  141.4 3.4 %all-to-all-start.6 = ((f32[8,16,128]{2,1,0:T(8,128)}), f32[8,16,128]{2,1,0:T(8,128)S(1)}, u32[]{:S(2)}, u32[]{:S(2)}) async-start(f32[8,16,128]{2,1,0:T(8,128)} %shard_map.47._), calls=%async_computation.6 | async-start | bytes 131072 | tf_op jit(solution)/shard_map/all_to_all | solution.py:394
  144.9 7.2 %all-to-all-done.6.x_ref = f32[8,16,128]{2,1,0:T(8,128)S(1)} async-done(((f32[8,16,128]{2,1,0:T(8,128)}), f32[8,16,128]{2,1,0:T(8,128)S(1)}, u32[]{:S(2)}, u32[]{:S(2)}) %all-to-all-start.6) | async-done | bytes 65568 | tf_op jit(solution)/shard_map/all_to_all | solution.py:394
  152.1 0.6 shard_map.50
  (13 shorter events, 0.3 us)
Async XLA Ops:
  46.2 6.6 %collective-permute-start = (f32[768,128]{1,0:T(8,128)S(1)}, f32[768,128]{1,0:T(8,128)S(1)}, u32[]{:S(2)}, u32[]{:S(2)}) collective-permute-start(f32[768,128]{1,0:T(8,128)S(1)} %get-tuple-element.23), channel_id=1, source_target_pairs={{0,32},{32,0},{64,96},{96,64},{128,160},{160,128},{192,224},{224,1... | collective-permute-start | bytes 1179656 | tf_op jit(solution)/shard_map/ppermute | solution.py:349
  52.8 36.7 %copy-start = (f32[1024,12]{0,1:T(8,128)S(1)}, f32[1024,12]{0,1:T(8,128)}, u32[]{:S(2)}) copy-start(f32[1024,12]{0,1:T(8,128)} %param.5) | copy-start | bytes 147460
  76.6 4.6 %collective-permute-start.1 = (f32[48,128]{1,0:T(8,128)S(1)}, f32[48,128]{1,0:T(8,128)S(1)}, u32[]{:S(2)}, u32[]{:S(2)}) collective-permute-start(f32[48,128]{1,0:T(8,128)S(1)} %get-tuple-element.27), channel_id=1, source_target_pairs={{0,1},{1,0},{2,3},{3,2},{4,5},{5,4},{6,7},{7,6},{8,9},{9,8},{10,11... | collective-permute-start | bytes 73736 | tf_op jit(solution)/shard_map/ppermute | solution.py:373
  81.2 8.3 %collective-permute-start.2 = (f32[96,128]{1,0:T(8,128)S(1)}, f32[96,128]{1,0:T(8,128)S(1)}, u32[]{:S(2)}, u32[]{:S(2)}) collective-permute-start(f32[96,128]{1,0:T(8,128)S(1)} %shard_map.42), channel_id=1, source_target_pairs={{0,4},{1,12},{2,38},{3,46},{4,71},{5,79},{6,97},{7,105},{8,138},{9... | collective-permute-start | bytes 147464 | tf_op jit(solution)/shard_map/ppermute | solution.py:376
  90.2 7.5 %collective-permute-start.3 = (f32[88,128]{1,0:T(8,128)S(1)}, f32[88,128]{1,0:T(8,128)S(1)}, u32[]{:S(2)}, u32[]{:S(2)}) collective-permute-start(f32[88,128]{1,0:T(8,128)S(1)} %get-tuple-element.28.mine_ref), channel_id=1, source_target_pairs={{0,32},{32,0},{64,96},{96,64},{128,160},{160,128},{192,224},{224,1... | collective-permute-start | bytes 135176 | tf_op jit(solution)/shard_map/ppermute | solution.py:349
  135.0 9.8 %collective-permute-start.4 = (f32[768,128]{1,0:T(8,128)S(1)}, f32[768,128]{1,0:T(8,128)S(1)}, u32[]{:S(2)}, u32[]{:S(2)}) collective-permute-start(f32[768,128]{1,0:T(8,128)S(1)} %shard_map.48.mine_ref), channel_id=1, source_target_pairs={{0,32},{32,0},{64,96},{96,64},{128,160},{160,128},{192,224},{224,1... | collective-permute-start | bytes 1179656 | tf_op jit(solution)/shard_map/ppermute | solution.py:349
  141.4 10.6 %all-to-all-start.6 = ((f32[8,16,128]{2,1,0:T(8,128)}), f32[8,16,128]{2,1,0:T(8,128)S(1)}, u32[]{:S(2)}, u32[]{:S(2)}) async-start(f32[8,16,128]{2,1,0:T(8,128)} %shard_map.47._), calls=%async_computation.6 | async-start | bytes 131072 | tf_op jit(solution)/shard_map/all_to_all | solution.py:394

commit v10 on v9

--- a/solution.py
+++ b/solution.py
@@ -393,7 +393,7 @@
     half = call(half_kernel, f32(768, B), wide, after=[solved], flops=10**10)
     rows_x = lax.all_to_all(solved, "col", 0, 0, axis_index_groups=Y_GROUPS)
     corner = call(
-        corner_kernel, f32(12, PW), half, between_cores(half), fac,
+        corner_kernel, f32(12, PW), half, lax.ppermute(half, "row", [(1, 0)]), fac,
         scratch=[vmem(PW, 512), vmem(PW, PW), vmem(1536, B), vmem(48, B)],
     )
     out = call(output_kernel, f32(12, 1024), rows_x, corner)

time: 153 us -> 154 us (level)
    ppermute x0 -> x1, starting transfers between devices: none -> 6.46 us  [on_device(): lax.ppermute(half, 'row', [(1, 0)])]
    ppermute x3 -> x2, starting transfers between devices: 18.3 us -> 11.8 us  [between_cores(): return lax.ppermute(value, 'row', [(r, r ^ 1) for r in range(16)])]
where the time goes in v10:
time: 154 us; the launch traced here: 153 us
  blocking collectives  103 us (67%)
  starting transfers between devices  29.9 us (19%)
  waiting for transfers between devices  13.9 us (9%)
  Pallas kernels  5.34 us (3%)
    all_to_all x2, blocking collectives, spread(): return lax.all_to_all(copies, axis, 0, 0, axis_index_groups=groups)  43.1 us
    all_to_all x1, blocking collectives, on_device(): pieces = lax.all_to_all(both, 'row', 0, 0, axis_index_groups=Z_GROUPS)  23.7 us
    all_to_all x1, blocking collectives, on_device(): near = lax.all_to_all(near, 'col', 0, 0, axis_index_groups=Y_GROUPS)  13 us
    all_to_all x1, blocking collectives, on_device(): got = lax.all_to_all(out_u, 'row', 0, 0, axis_index_groups=Z_GROUPS)  12.7 us
    ppermute x2, starting transfers between devices, between_cores(): return lax.ppermute(value, 'row', [(r, r ^ 1) for r in range(16)])  11.8 us
    all_to_all x1, blocking collectives, on_device(): lax.all_to_all(wide, 'col', 0, 0, axis_index_groups=X_GROUPS)  10.7 us
    all_to_all x1, waiting for transfers between devices, on_device(): rows_x = lax.all_to_all(solved, 'col', 0, 0, axis_index_groups=Y_GROUPS)  7.91 us
    ppermute x1, starting transfers between devices, on_device(): lax.ppermute(half, 'row', [(1, 0)])  6.46 us
  transfers between devices with their start and end apart: 6, of which 5 were waited for; matrix products, arithmetic and copies ran while one was open for 0% of the time, Pallas kernels for 1%

profile of v10, /device:TPU:1, one launch (start us, length us, event | category | flops | bytes accessed | tf_op | source)
XLA Modules:
  0.0 153.4 jit_solution(8615719554222296376)
XLA Ops:
  0.0 0.9 broadcast_in_dim.14
  0.9 19.8 %all_to_all.35 = f32[8,96,128]{2,1,0:T(8,128)S(1)} all-to-all(f32[8,96,128]{2,1,0:T(8,128)S(1)} %broadcast_in_dim.15), channel_id=1, replica_groups={{0,1,2,3,4,5,6,7},{8,9,10,11,12,13,14,15},{16,17,18,19,20,21,22,23},{24..., dimensions={0} | all-to-all | bytes 786432 | tf_op jit(solution)/shard_map/all_to_all | solution.py:345
  20.7 0.1 broadcast_in_dim.17
  20.8 23.3 %all_to_all.36 = f32[4,768,128]{2,1,0:T(8,128)S(1)} all-to-all(f32[4,768,128]{2,1,0:T(8,128)S(1)} %broadcast_in_dim.17), channel_id=1, replica_groups={{0,8,16,24},{1,9,17,25},{2,10,18,26},{3,11,19,27},{4,12,20,28},{5,13,21..., dimensions={0} | all-to-all | bytes 3145728 | tf_op jit(solution)/shard_map/all_to_all | solution.py:345
  44.1 2.1 %shard_map.37 = (f32[768,128]{1,0:T(8,128)S(1)}, bf16[384,1024]{1,0:T(8,128)(2,1)S(1)}, bf16[384,1024]{1,0:T(8,128)(2,1)S(1)}, f32[384,384]{1,0:T(8,128)S(1)}, b...) custom-call(f32[3072,128]{1,0:T(8,128)S(1)} %bitcast.9, f32[1024,512]{1,0:T(8,128)} %t_hbm_ref.1), custom_call_target="tpu_custom_call" | custom-call | flops 1207959552 | bytes 1572864 | tf_op jit(solution)/shard_map/pallas_call | solution.py:331
  46.2 5.2 %collective-permute-start = (f32[768,128]{1,0:T(8,128)S(1)}, f32[768,128]{1,0:T(8,128)S(1)}, u32[]{:S(2)}, u32[]{:S(2)}) collective-permute-start(f32[768,128]{1,0:T(8,128)S(1)} %get-tuple-element.23), channel_id=1, source_target_pairs={{0,32},{32,0},{64,96},{96,64},{128,160},{160,128},{192,224},{224,1... | collective-permute-start | bytes 1179656 | tf_op jit(solution)/shard_map/ppermute | solution.py:349
  51.5 0.8 shard_map.38.a_ref
  52.3 0.5 collective-permute-done.b_ref
  52.8 23.7 %all_to_all.37.s_ref = f32[8,96,128]{2,1,0:T(8,128)S(1)} all-to-all(f32[8,96,128]{2,1,0:T(8,128)S(1)} %bitcast.10), channel_id=1, replica_groups={{0,64,128,192,256,320,384,448},{32,96,160,224,288,352,416,480},{1,65,12..., dimensions={0} | all-to-all | bytes 786432 | tf_op jit(solution)/shard_map/all_to_all | solution.py:371
  76.6 1.9 %collective-permute-start.1 = (f32[48,128]{1,0:T(8,128)S(1)}, f32[48,128]{1,0:T(8,128)S(1)}, u32[]{:S(2)}, u32[]{:S(2)}) collective-permute-start(f32[48,128]{1,0:T(8,128)S(1)} %get-tuple-element.27), channel_id=1, source_target_pairs={{0,1},{1,0},{2,3},{3,2},{4,5},{5,4},{6,7},{7,6},{8,9},{9,8},{10,11... | collective-permute-start | bytes 73736 | tf_op jit(solution)/shard_map/ppermute | solution.py:373
  78.5 2.6 %collective-permute-done.1.got_ref = f32[48,128]{1,0:T(8,128)S(1)} collective-permute-done((f32[48,128]{1,0:T(8,128)S(1)}, f32[48,128]{1,0:T(8,128)S(1)}, u32[]{:S(2)}, u32[]{:S(2)}) %collective-permute-start.1) | collective-permute-done | bytes 24608 | tf_op jit(solution)/shard_map/ppermute | solution.py:373
  81.2 6.4 %collective-permute-start.2 = (f32[96,128]{1,0:T(8,128)S(1)}, f32[96,128]{1,0:T(8,128)S(1)}, u32[]{:S(2)}, u32[]{:S(2)}) collective-permute-start(f32[96,128]{1,0:T(8,128)S(1)} %shard_map.42), channel_id=1, source_target_pairs={{0,4},{1,12},{2,38},{3,46},{4,71},{5,79},{6,97},{7,105},{8,138},{9... | collective-permute-start | bytes 147464 | tf_op jit(solution)/shard_map/ppermute | solution.py:376
  87.5 2.0 %collective-permute-done.2.tc_ref = f32[96,128]{1,0:T(8,128)S(1)} collective-permute-done((f32[96,128]{1,0:T(8,128)S(1)}, f32[96,128]{1,0:T(8,128)S(1)}, u32[]{:S(2)}, u32[]{:S(2)}) %collective-permute-start.2) | collective-permute-done | bytes 49184 | tf_op jit(solution)/shard_map/ppermute | solution.py:376
  89.5 0.7 shard_map.43
  90.2 6.6 %collective-permute-start.3 = (f32[88,128]{1,0:T(8,128)S(1)}, f32[88,128]{1,0:T(8,128)S(1)}, u32[]{:S(2)}, u32[]{:S(2)}) collective-permute-start(f32[88,128]{1,0:T(8,128)S(1)} %get-tuple-element.28.mine_ref), channel_id=1, source_target_pairs={{0,32},{32,0},{64,96},{96,64},{128,160},{160,128},{192,224},{224,1... | collective-permute-start | bytes 135176 | tf_op jit(solution)/shard_map/ppermute | solution.py:349
  96.8 0.9 collective-permute-done.3.other_ref
  97.7 12.7 %all_to_all.38.got_ref = f32[8,40,128]{2,1,0:T(8,128)S(1)} all-to-all(f32[8,40,128]{2,1,0:T(8,128)S(1)} %get-tuple-element.30), channel_id=1, replica_groups={{0,64,128,192,256,320,384,448},{32,96,160,224,288,352,416,480},{1,65,12..., dimensions={0} | all-to-all | bytes 327680 | tf_op jit(solution)/shard_map/all_to_all | solution.py:384
  110.4 13.0 %all_to_all.39.near_ref = f32[8,72,128]{2,1,0:T(8,128)S(1)} all-to-all(f32[8,72,128]{2,1,0:T(8,128)S(1)} %shard_map.45), channel_id=1, replica_groups={{0,1,2,3,4,5,6,7},{8,9,10,11,12,13,14,15},{16,17,18,19,20,21,22,23},{24..., dimensions={0} | all-to-all | bytes 589824 | tf_op jit(solution)/shard_map/all_to_all | solution.py:386
  123.4 10.7 %all_to_all.40 = f32[4,288,128]{2,1,0:T(8,128)S(1)} all-to-all(f32[4,288,128]{2,1,0:T(8,128)S(1)} %shard_map.46), channel_id=1, replica_groups={{0,8,16,24},{1,9,17,25},{2,10,18,26},{3,11,19,27},{4,12,20,28},{5,13,21..., dimensions={0} | all-to-all | bytes 1179648 | tf_op jit(solution)/shard_map/all_to_all | solution.py:388
  134.1 0.9 shard_map.47._
  135.0 6.5 %collective-permute-start.4 = (f32[768,128]{1,0:T(8,128)S(1)}, f32[768,128]{1,0:T(8,128)S(1)}, u32[]{:S(2)}, u32[]{:S(2)}) collective-permute-start(f32[768,128]{1,0:T(8,128)S(1)} %shard_map.48.mine_ref), channel_id=1, source_target_pairs={{32,0},{33,1},{34,2},{35,3},{36,4},{37,5},{38,6},{39,7},{40,8},{41... | collective-permute-start | bytes 1179656 | tf_op jit(solution)/shard_map/ppermute | solution.py:396
  141.5 3.4 %all-to-all-start.6 = ((f32[8,16,128]{2,1,0:T(8,128)}), f32[8,16,128]{2,1,0:T(8,128)S(1)}, u32[]{:S(2)}, u32[]{:S(2)}) async-start(f32[8,16,128]{2,1,0:T(8,128)} %shard_map.47._), calls=%async_computation.6 | async-start | bytes 131072 | tf_op jit(solution)/shard_map/all_to_all | solution.py:394
  144.9 7.9 %all-to-all-done.6.x_ref = f32[8,16,128]{2,1,0:T(8,128)S(1)} async-done(((f32[8,16,128]{2,1,0:T(8,128)}), f32[8,16,128]{2,1,0:T(8,128)S(1)}, u32[]{:S(2)}, u32[]{:S(2)}) %all-to-all-start.6) | async-done | bytes 65568 | tf_op jit(solution)/shard_map/all_to_all | solution.py:394
  152.8 0.6 shard_map.50
  (13 shorter events, 0.3 us)
Async XLA Ops:
  46.2 6.6 %collective-permute-start = (f32[768,128]{1,0:T(8,128)S(1)}, f32[768,128]{1,0:T(8,128)S(1)}, u32[]{:S(2)}, u32[]{:S(2)}) collective-permute-start(f32[768,128]{1,0:T(8,128)S(1)} %get-tuple-element.23), channel_id=1, source_target_pairs={{0,32},{32,0},{64,96},{96,64},{128,160},{160,128},{192,224},{224,1... | collective-permute-start | bytes 1179656 | tf_op jit(solution)/shard_map/ppermute | solution.py:349
  52.8 36.7 %copy-start = (f32[1024,12]{0,1:T(8,128)S(1)}, f32[1024,12]{0,1:T(8,128)}, u32[]{:S(2)}) copy-start(f32[1024,12]{0,1:T(8,128)} %param.5) | copy-start | bytes 147460
  76.6 4.6 %collective-permute-start.1 = (f32[48,128]{1,0:T(8,128)S(1)}, f32[48,128]{1,0:T(8,128)S(1)}, u32[]{:S(2)}, u32[]{:S(2)}) collective-permute-start(f32[48,128]{1,0:T(8,128)S(1)} %get-tuple-element.27), channel_id=1, source_target_pairs={{0,1},{1,0},{2,3},{3,2},{4,5},{5,4},{6,7},{7,6},{8,9},{9,8},{10,11... | collective-permute-start | bytes 73736 | tf_op jit(solution)/shard_map/ppermute | solution.py:373
  81.2 8.3 %collective-permute-start.2 = (f32[96,128]{1,0:T(8,128)S(1)}, f32[96,128]{1,0:T(8,128)S(1)}, u32[]{:S(2)}, u32[]{:S(2)}) collective-permute-start(f32[96,128]{1,0:T(8,128)S(1)} %shard_map.42), channel_id=1, source_target_pairs={{0,4},{1,12},{2,38},{3,46},{4,71},{5,79},{6,97},{7,105},{8,138},{9... | collective-permute-start | bytes 147464 | tf_op jit(solution)/shard_map/ppermute | solution.py:376
  90.2 7.5 %collective-permute-start.3 = (f32[88,128]{1,0:T(8,128)S(1)}, f32[88,128]{1,0:T(8,128)S(1)}, u32[]{:S(2)}, u32[]{:S(2)}) collective-permute-start(f32[88,128]{1,0:T(8,128)S(1)} %get-tuple-element.28.mine_ref), channel_id=1, source_target_pairs={{0,32},{32,0},{64,96},{96,64},{128,160},{160,128},{192,224},{224,1... | collective-permute-start | bytes 135176 | tf_op jit(solution)/shard_map/ppermute | solution.py:349
  135.0 9.8 %collective-permute-start.4 = (f32[768,128]{1,0:T(8,128)S(1)}, f32[768,128]{1,0:T(8,128)S(1)}, u32[]{:S(2)}, u32[]{:S(2)}) collective-permute-start(f32[768,128]{1,0:T(8,128)S(1)} %shard_map.48.mine_ref), channel_id=1, source_target_pairs={{32,0},{33,1},{34,2},{35,3},{36,4},{37,5},{38,6},{39,7},{40,8},{41... | collective-permute-start | bytes 1179656 | tf_op jit(solution)/shard_map/ppermute | solution.py:396
  141.5 11.3 %all-to-all-start.6 = ((f32[8,16,128]{2,1,0:T(8,128)}), f32[8,16,128]{2,1,0:T(8,128)S(1)}, u32[]{:S(2)}, u32[]{:S(2)}) async-start(f32[8,16,128]{2,1,0:T(8,128)} %shard_map.47._), calls=%async_computation.6 | async-start | bytes 131072 | tf_op jit(solution)/shard_map/all_to_all | solution.py:394
